TPU v7x, 32 devices: a whole 2x2x4 slice. The times are simulated.
32 devices in a mesh: dp: 16 (over z, y, core), rep: 2 (over x).
Axes of the slice: x: 2, y: 2, z: 4, core: 2. Of those that a mesh axis runs over, the one named last changes fastest.
Arguments:
- tokens: bfloat16 [2048, 1664], P('dp'), may hold values from -6 to 6
- expert_ids: int32 [2048, 2], P('dp'), may hold values from 0 to 3, all different within a row; in each aligned block of 128 rows (0 to 127, 128 to 255, ...) at most 72 rows name the same one
- priority: int32 [2048], P('dp'), may hold values from 0 to 63
- gate_values: float32 [2048, 2], P('dp'), may hold values from 0.05 to 1
- weight_in: bfloat16 [16, 1664, 1024], P('dp', None, 'rep'), may hold values from -0.15625 to 0.15625
- weight_out: bfloat16 [16, 1024, 1664], P('dp', 'rep'), may hold values from -0.09375 to 0.09375
- cotangent: bfloat16 [2048, 1664], P('dp'), may hold values from -6 to 6
Outputs:
- output: bfloat16 [2048, 1664], P('dp', 'rep')
- grad_tokens: bfloat16 [2048, 1664], P('dp', 'rep')
- grad_gates: float32 [2048, 2], P(('dp', 'rep'))
- grad_weight_in: bfloat16 [16, 1664, 1024], P('dp', None, 'rep')
- grad_weight_out: bfloat16 [16, 1024, 1664], P('dp', 'rep')
Inputs may be any that keep to these rules, and one draw needn't show every extreme that they name: `expert_ids`: the two ids of a token differ. Among the 128 tokens of one index of dp no expert is named more than 72 times, and 72 is reached.
All inputs are finite; a program needn't handle non-finite values.
Results may differ from a plain program's by a relative error of at most 0.017.
Values may be sent and summed in bfloat16 or wider, within the bound.
No kernel may reach another device: no remote copies, remote signals or barrier semaphores. Data moves between devices by JAX's collectives and lax.ppermute only.
A program may use at most 128 MiB of HBM per device.

v0:
```python
import math

import jax
import jax.numpy as jnp
from jax import lax
from jax.sharding import PartitionSpec as P

HBLK = 4
PRIO = 64


def gelu_parts(hidden_pre):
    normal_cdf = 0.5 * (1.0 + jax.scipy.special.erf(hidden_pre * (1.0 / math.sqrt(2.0))))
    density = jnp.exp(-0.5 * hidden_pre * hidden_pre) * (1.0 / math.sqrt(2.0 * math.pi))
    return (hidden_pre * normal_cdf, normal_cdf + hidden_pre * density)


def body(tokens, expert_ids, priority, gate_values, weight_in, weight_out, cotangent):
    token_count = tokens.shape[0]
    dp_count = lax.axis_size("dp")
    experts = dp_count // HBLK
    slot_count = min(token_count, 2 * token_count // experts + max(1, token_count // (4 * experts)))
    capacity = 2 * token_count * dp_count // experts
    row_total = dp_count * slot_count
    contract_first = (((0,), (0,)), ((), ()))
    contract_last = (((1,), (1,)), ((), ()))
    priority_key = (
        priority[:, None] + PRIO * (1 - jnp.arange(2, dtype=jnp.int32))[None, :]
    ).reshape(-1)
    flat_expert = expert_ids.reshape(-1)
    expert_hot = (flat_expert[:, None] == jnp.arange(experts, dtype=jnp.int32)[None, :]).astype(
        jnp.int32
    )
    key_hot = (priority_key[:, None] == jnp.arange(2 * PRIO, dtype=jnp.int32)[None, :]).astype(
        jnp.int32
    )
    local_counts = jnp.dot(expert_hot.T, key_hot, preferred_element_type=jnp.int32)
    counts = lax.psum(local_counts, "dp")
    above_count = jnp.cumsum(counts[:, ::-1], axis=1)[:, ::-1]
    cutoff_key = jnp.sum((above_count > capacity).astype(jnp.int32), axis=1)
    kept_mask = priority_key >= jnp.sum(expert_hot * cutoff_key[None, :], axis=1)
    before_count = jnp.cumsum(expert_hot, axis=0) - expert_hot
    slot_index = jnp.sum(expert_hot * before_count, axis=1)
    slot_hot = (slot_index[:, None] == jnp.arange(slot_count, dtype=jnp.int32)[None, :]).astype(
        jnp.int32
    )
    place_map = (
        expert_hot[:, :, None] * slot_hot[:, None, :] * kept_mask.astype(jnp.int32)[:, None, None]
    )
    place_map = place_map.astype(jnp.bfloat16).reshape(2 * token_count, experts * slot_count)
    token_place = jnp.sum(place_map.reshape(token_count, 2, experts * slot_count), axis=1)
    grad_source = (
        gate_values.reshape(-1)[:, None] * jnp.repeat(cotangent, 2, axis=0).astype(jnp.float32)
    ).astype(jnp.bfloat16)
    wide_index = jnp.arange(row_total, dtype=jnp.int32)
    wide_index = wide_index // (HBLK * slot_count) * slot_count + wide_index % slot_count

    def widen(matrix):
        return jnp.take(matrix, wide_index, axis=0)

    send_rows = lax.dot_general(
        token_place, tokens, contract_first, preferred_element_type=jnp.float32
    ).astype(jnp.bfloat16)
    send_grads = lax.dot_general(
        place_map, grad_source, contract_first, preferred_element_type=jnp.float32
    ).astype(jnp.bfloat16)
    rows, grad_rows = (
        lax.all_to_all(widen(send_rows), "dp", split_axis=0, concat_axis=0, tiled=True),
        lax.all_to_all(widen(send_grads), "dp", split_axis=0, concat_axis=0, tiled=True),
    )
    matrix_in = weight_in[0]
    matrix_out = weight_out[0]
    hidden_pre = jnp.dot(rows, matrix_in, preferred_element_type=jnp.float32)
    activation, slope = gelu_parts(hidden_pre)
    activation = activation.astype(jnp.bfloat16)
    partial_out = jnp.dot(activation, matrix_out, preferred_element_type=jnp.float32).astype(
        jnp.bfloat16
    )
    grad_act = lax.dot_general(
        grad_rows, matrix_out, contract_last, preferred_element_type=jnp.float32
    )
    grad_pre = (grad_act * slope).astype(jnp.bfloat16)
    grad_in = lax.dot_general(
        rows, grad_pre, contract_first, preferred_element_type=jnp.float32
    ).astype(jnp.bfloat16)
    grad_out = lax.dot_general(
        activation, grad_rows, contract_first, preferred_element_type=jnp.float32
    ).astype(jnp.bfloat16)
    partial_dx = lax.dot_general(
        grad_pre, matrix_in, contract_last, preferred_element_type=jnp.float32
    ).astype(jnp.bfloat16)
    block_range = jnp.arange(HBLK, dtype=jnp.int32)
    pick_index = (
        (flat_expert[:, None] * HBLK + block_range[None, :]) * slot_count + slot_index[:, None]
    ).reshape(-1)

    def pick_rows(returned):
        width = returned.shape[-1]
        picked = jnp.take(returned, pick_index, axis=0)
        summed = jnp.sum(picked.reshape(2 * token_count, HBLK, width).astype(jnp.float32), axis=1)
        return jnp.where(kept_mask[:, None], summed, 0.0).reshape(token_count, 2, width)

    back_out, back_dx = (
        lax.all_to_all(partial_out, "dp", split_axis=0, concat_axis=0, tiled=True),
        lax.all_to_all(partial_dx, "dp", split_axis=0, concat_axis=0, tiled=True),
    )
    out_rows = pick_rows(back_out)
    dx_rows = pick_rows(back_dx)
    mixed = jnp.sum(gate_values[:, :, None] * out_rows, axis=1)
    token_grad = jnp.sum(dx_rows, axis=1)
    gate_grad = jnp.sum(cotangent.astype(jnp.float32)[:, None, :] * out_rows, axis=2)
    gate_grad = lax.psum_scatter(gate_grad, "rep", scatter_dimension=0, tiled=True)
    mixed, token_grad = (
        lax.psum_scatter(mixed.astype(jnp.bfloat16), "rep", scatter_dimension=1, tiled=True).astype(
            jnp.float32
        ),
        lax.psum_scatter(
            token_grad.astype(jnp.bfloat16), "rep", scatter_dimension=1, tiled=True
        ).astype(jnp.float32),
    )
    return (
        mixed.astype(jnp.bfloat16),
        token_grad.astype(jnp.bfloat16),
        gate_grad,
        grad_in[None],
        grad_out[None],
    )


def solution(mesh):
    placed = (
        P("dp", None),
        P("dp", None),
        P("dp"),
        P("dp", None),
        P("dp", None, "rep"),
        P("dp", "rep", None),
        P("dp", None),
    )
    return jax.shard_map(
        body,
        mesh=mesh,
        in_specs=placed,
        out_specs=(
            P("dp", "rep"),
            P("dp", "rep"),
            P(("dp", "rep"), None),
            P("dp", None, "rep"),
            P("dp", "rep", None),
        ),
        check_vma=False,
    )
```

profile of v0, /device:TPU:0, one launch (start us, length us, event | category | flops | bytes accessed | tf_op | source)
XLA Modules:
  0.0 527.9 jit_solution(17431660453793351094)
XLA Ops:
  11.3 13.7 %psum.7 = s32[4,128]{1,0:T(4,128)S(1)} all-reduce(s32[4,128]{1,0:T(4,128)S(1)} %rev.6), channel_id=1, replica_groups=mesh['dp'=16,'rep'=2] {'dp'}, use_global_device_ids=true, to_apply=%region_0.0 | all-reduce | flops 512 | bytes 4096 | tf_op jit(solution)/shard_map/psum | solution.py:38
  35.9 10.5 %gather_fusion = bf16[1152,1664]{1,0:T(8,128)(2,1)} fusion(bf16[288,1664]{1,0:T(8,128)(2,1)} %convolution_convert_fusion.5, s32[2048]{0:T(1024)S(1)} %pad_clamp_fusion), kind=kCustom, calls=%fused_computation.clone | custom fusion | bytes 7672320 | tf_op jit(solution)/shard_map/jit(_take)/gather | solution.py:59
  46.3 5.6 %gather_fusion.2 = bf16[1152,1664]{1,0:T(8,128)(2,1)} fusion(bf16[288,1664]{1,0:T(8,128)(2,1)S(1)} %convolution_convert_fusion.4, s32[2048]{0:T(1024)S(1)} %pad_clamp_fusion), kind=kCustom, calls=%fused_computation.2.clone | custom fusion | bytes 7672320 | tf_op jit(solution)/shard_map/jit(_take)/gather | solution.py:59
  51.9 5.2 broadcast_select_fusion.1
  57.1 89.4 %all_to_all.48 = bf16[16,72,1664]{2,1,0:T(8,128)(2,1)} all-to-all(bf16[16,72,1664]{2,1,0:T(8,128)(2,1)S(1)} %bitcast.61), channel_id=1, replica_groups=mesh['dp'=16,'rep'=2] {'dp'}, dimensions={0} | all-to-all | bytes 7667712 | tf_op jit(solution)/shard_map/all_to_all | solution.py:68
  146.4 4.7 all-to-all-start.2
  151.1 6.5 %multiply_convert_fusion = (bf16[1152,512]{1,0:T(8,128)(2,1)}, f32[1152,512]{1,0:T(8,128)}) fusion(bf16[1152,1664]{1,0:T(8,128)(2,1)} %bitcast.62, bf16[1,1664,512]{2,1,0:T(8,128)(2,1)S(1)} %copy-done), kind=kOutput, calls=%fused_computation.23 | convolution fusion | flops 1965883392 | bytes 9076736 | tf_op jit(solution)/shard_map/dot_general | solution.py:73
  157.6 64.8 %all-to-all-done.2 = bf16[16,72,1664]{2,1,0:T(8,128)(2,1)} async-done(((bf16[16,72,1664]{2,1,0:T(8,128)(2,1)}), bf16[16,72,1664]{2,1,0:T(8,128)(2,1)}, u32[]{:S(2)}, u32[]{:S(2)}) %all-to-all-start.2) | async-done | bytes 3833888 | tf_op jit(solution)/shard_map/all_to_all | solution.py:69
  222.4 5.3 %fusion = bf16[1152,512]{1,0:T(8,128)(2,1)S(1)} fusion(bf16[1152,1664]{1,0:T(8,128)(2,1)} %bitcast.10, f32[1152,512]{1,0:T(8,128)} %get-tuple-element.40, bf16[1,512,1664]{2,1,0:T(8,128)(2,1)S(1)} %copy-done.9), kind=kOutput, calls=%fused_computation.14 | convolution fusion | flops 1968832512 | bytes 9076736 | tf_op jit(solution)/shard_map/dot_general | solution.py:79
  232.0 18.3 %all-to-all-start.3 = ((bf16[16,72,1664]{2,1,0:T(8,128)(2,1)}), bf16[16,72,1664]{2,1,0:T(8,128)(2,1)}, u32[]{:S(2)}, u32[]{:S(2)}) async-start(bf16[16,72,1664]{2,1,0:T(8,128)(2,1)} %bitcast.65), calls=%async_computation.3 | async-start | bytes 7667712 | tf_op jit(solution)/shard_map/all_to_all | solution.py:105
  254.6 67.1 %all-to-all-done.3 = bf16[16,72,1664]{2,1,0:T(8,128)(2,1)} async-done(((bf16[16,72,1664]{2,1,0:T(8,128)(2,1)}), bf16[16,72,1664]{2,1,0:T(8,128)(2,1)}, u32[]{:S(2)}, u32[]{:S(2)}) %all-to-all-start.3) | async-done | bytes 3833888 | tf_op jit(solution)/shard_map/all_to_all | solution.py:105
  321.7 18.4 %all-to-all-start.1 = ((bf16[16,72,1664]{2,1,0:T(8,128)(2,1)}), bf16[16,72,1664]{2,1,0:T(8,128)(2,1)}, u32[]{:S(2)}, u32[]{:S(2)}) async-start(bf16[16,72,1664]{2,1,0:T(8,128)(2,1)} %bitcast.64), calls=%async_computation.1 | async-start | bytes 7667712 | tf_op jit(solution)/shard_map/all_to_all | solution.py:104
  343.6 10.2 %gather_fusion.3 = bf16[1024,1664]{1,0:T(8,128)(2,1)} fusion(bf16[1152,1664]{1,0:T(8,128)(2,1)} %bitcast.12, s32[1024]{0:T(1024)S(1)} %fusion.31), kind=kCustom, calls=%fused_computation.3.clone | custom fusion | bytes 6819840 | tf_op jit(solution)/shard_map/jit(_take)/gather | solution.py:99
  353.8 57.7 %all-to-all-done.1 = bf16[16,72,1664]{2,1,0:T(8,128)(2,1)} async-done(((bf16[16,72,1664]{2,1,0:T(8,128)(2,1)}), bf16[16,72,1664]{2,1,0:T(8,128)(2,1)}, u32[]{:S(2)}, u32[]{:S(2)}) %all-to-all-start.1) | async-done | bytes 3833888 | tf_op jit(solution)/shard_map/all_to_all | solution.py:104
  411.5 10.2 %gather_fusion.1 = bf16[1024,1664]{1,0:T(8,128)(2,1)} fusion(bf16[1152,1664]{1,0:T(8,128)(2,1)} %bitcast.7, s32[1024]{0:T(1024)S(1)} %fusion.31), kind=kCustom, calls=%fused_computation.1.clone | custom fusion | bytes 6819840 | tf_op jit(solution)/shard_map/jit(_take)/gather | solution.py:99
  421.7 8.8 %select_convert_fusion.1 = (f32[1024,1664]{1,0:T(8,128)}, f32[1024,1664]{1,0:T(8,128)}) fusion(bf16[1024,1664]{1,0:T(8,128)(2,1)} %gather_fusion.1, pred[1024]{0:T(1024)(128)(4,1)S(1)} %compare_and_fusion.1, bf16[1024,1664]{1,0:T(8,128)(2,1)} %gather_fusion.3), kind=kLoop, calls=%fused_computation.11 | loop fusion | flops 6815744 | bytes 20448256 | tf_op jit(solution)/shard_map/convert_element_type | solution.py:100
  430.4 8.5 %reshape.255 = f32[256,4,1664]{2,1,0:T(4,128)} reshape(f32[1024,1664]{1,0:T(8,128)} %get-tuple-element.37) | data formatting | bytes 13631488 | tf_op jit(solution)/shard_map/convert_element_type | solution.py:100
  438.9 7.0 %reduce_sum.97 = f32[256,1664]{1,0:T(8,128)S(1)} reduce(f32[256,4,1664]{2,1,0:T(4,128)} %reshape.255, f32[]{:T(128)} %constant.71.clone.1), dimensions={1}, to_apply=%region_8.11 | reduce | flops 1277952 | bytes 8519684 | tf_op jit(solution)/shard_map/reduce_sum | solution.py:100
  449.8 8.5 %reshape.256 = f32[256,4,1664]{2,1,0:T(4,128)} reshape(f32[1024,1664]{1,0:T(8,128)} %get-tuple-element.38) | data formatting | bytes 13631488 | tf_op jit(solution)/shard_map/convert_element_type | solution.py:100
  458.3 8.2 %reduce_sum.100 = f32[256,1664]{1,0:T(8,128)} reduce(f32[256,4,1664]{2,1,0:T(4,128)} %reshape.256, f32[]{:T(128)} %constant.71.clone.1), dimensions={1}, to_apply=%region_11.14 | reduce | flops 1277952 | bytes 8519684 | tf_op jit(solution)/shard_map/reduce_sum | solution.py:100
  468.9 6.4 %select_reduce_fusion = (bf16[128,1664]{1,0:T(8,128)(2,1)}, bf16[128,1664]{1,0:T(8,128)(2,1)}) fusion(f32[128,2,1664]{2,1,0:T(2,128)S(1)} %reduce_sum.101, pred[128,2]{1,0:T(8,128)(4,1)S(1)} %get-tuple-element.32, f32[128,2,1664]{2,1,0:T(2,128)S(1)} %reduce_sum.98, f32[128,2]{1,0:T(8,128)S(1)} %copy-done.6), kind=kLoop, calls=%fused_computation.31 | loop fusion | flops 1703936 | bytes 4261120 | tf_op jit(solution)/shard_map/reduce_sum | solution.py:110
  479.8 6.0 %fusion.2 = bf16[1,512,1664]{2,1,0:T(8,128)(2,1)} fusion(bf16[1152,512]{1,0:T(8,128)(2,1)S(1)} %copy-done.11, bf16[1152,1664]{1,0:T(8,128)(2,1)} %bitcast.10), kind=kOutput, calls=%fused_computation.16 | convolution fusion | flops 1963786240 | bytes 6717440 | tf_op jit(solution)/shard_map/dot_general | solution.py:86
  490.7 13.8 %reduce-scatter.12.cloned.1.call-done = bf16[832,128]{1,0:T(8,128)(2,1)} async-done(((bf16[1664,128]{1,0:T(8,128)(2,1)}), bf16[832,128]{1,0:T(8,128)(2,1)}) %reduce-scatter.12.cloned.1.call-update) | async-done | bytes 213008
  504.5 16.3 %reduce-scatter.10.cloned.1.call-done = bf16[832,128]{1,0:T(8,128)(2,1)} async-done(((bf16[1664,128]{1,0:T(8,128)(2,1)}), bf16[832,128]{1,0:T(8,128)(2,1)}) %reduce-scatter.10.cloned.1.call-update) | async-done | bytes 213008
  (91 shorter events, 42.4 us)
Async XLA Ops:
  7.2 143.9 %copy-start = (bf16[1,1664,512]{2,1,0:T(8,128)(2,1)S(1)}, bf16[1,1664,512]{2,1,0:T(8,128)(2,1)}, u32[]{:S(2)}) copy-start(bf16[1,1664,512]{2,1,0:T(8,128)(2,1)} %param.15) | copy-start | bytes 5111812
  7.2 23.2 %copy-start.3 = (bf16[128,1664]{1,0:T(8,128)(2,1)S(1)}, bf16[128,1664]{1,0:T(8,128)(2,1)}, u32[]{:S(2)}) copy-start(bf16[128,1664]{1,0:T(8,128)(2,1)} %param.17) | copy-start | bytes 1277956
  26.6 3.8 copy-start.5
  30.4 1.0 copy-start.8
  31.4 3.1 copy-start.7
  146.4 76.0 %all-to-all-start.2 = ((bf16[16,72,1664]{2,1,0:T(8,128)(2,1)}), bf16[16,72,1664]{2,1,0:T(8,128)(2,1)}, u32[]{:S(2)}, u32[]{:S(2)}) async-start(bf16[16,72,1664]{2,1,0:T(8,128)(2,1)} %bitcast.60), calls=%async_computation.2 | async-start | bytes 7667712 | tf_op jit(solution)/shard_map/all_to_all | solution.py:69
  151.1 71.3 %copy-start.9 = (bf16[1,512,1664]{2,1,0:T(8,128)(2,1)S(1)}, bf16[1,512,1664]{2,1,0:T(8,128)(2,1)}, u32[]{:S(2)}) copy-start(bf16[1,512,1664]{2,1,0:T(8,128)(2,1)} %param.16) | copy-start | bytes 5111812
  227.8 4.2 copy-start.12
  232.0 18.4 %copy-start.10 = (bf16[1152,512]{1,0:T(8,128)(2,1)S(1)}, bf16[1152,512]{1,0:T(8,128)(2,1)}, u32[]{:S(2)}) copy-start(bf16[1152,512]{1,0:T(8,128)(2,1)} %get-tuple-element.39) | copy-start | bytes 3538948
  232.0 89.8 %all-to-all-start.3 = ((bf16[16,72,1664]{2,1,0:T(8,128)(2,1)}), bf16[16,72,1664]{2,1,0:T(8,128)(2,1)}, u32[]{:S(2)}, u32[]{:S(2)}) async-start(bf16[16,72,1664]{2,1,0:T(8,128)(2,1)} %bitcast.65), calls=%async_computation.3 | async-start | bytes 7667712 | tf_op jit(solution)/shard_map/all_to_all | solution.py:105
  321.7 19.1 %copy-start.4 = (bf16[128,1664]{1,0:T(8,128)(2,1)S(1)}, bf16[128,1664]{1,0:T(8,128)(2,1)}, u32[]{:S(2)}) copy-start(bf16[128,1664]{1,0:T(8,128)(2,1)} %param.17) | copy-start | bytes 1277956
  321.7 89.8 %all-to-all-start.1 = ((bf16[16,72,1664]{2,1,0:T(8,128)(2,1)}), bf16[16,72,1664]{2,1,0:T(8,128)(2,1)}, u32[]{:S(2)}, u32[]{:S(2)}) async-start(bf16[16,72,1664]{2,1,0:T(8,128)(2,1)} %bitcast.64), calls=%async_computation.1 | async-start | bytes 7667712 | tf_op jit(solution)/shard_map/all_to_all | solution.py:104
  340.1 149.2 %reduce-scatter.8.cloned.1.call-start = ((), (), s32[]{:S(2)}) async-start(), calls=%async_computation.7 | async-start | bytes 98304 | tf_op jit(solution)/shard_map/reduce_scatter | solution.py:112
  449.5 55.0 %reduce-scatter.12.cloned.1.call-start = ((), (), s32[]{:S(2)}) async-start(), calls=%async_computation.9 | async-start | bytes 638976
  466.5 2.3 copy-start.6
  475.3 4.4 copy-start.11
  477.4 43.5 %reduce-scatter.10.cloned.1.call-start = ((), (), s32[]{:S(2)}) async-start(), calls=%async_computation.8 | async-start | bytes 638976
  479.7 6.0 %copy-start.2 = (bf16[16,72,1664]{2,1,0:T(8,128)(2,1)S(1)}, bf16[16,72,1664]{2,1,0:T(8,128)(2,1)}, u32[]{:S(2)}) copy-start(bf16[16,72,1664]{2,1,0:T(8,128)(2,1)} %all_to_all.48) | copy-start | bytes 11501572
  479.7 6.0 %copy-start.13 = (bf16[1152,512]{1,0:T(8,128)(2,1)S(1)}, bf16[1152,512]{1,0:T(8,128)(2,1)}, u32[]{:S(2)}) copy-start(bf16[1152,512]{1,0:T(8,128)(2,1)} %copy-done.12) | copy-start | bytes 3538948
  485.7 35.2 %copy-start.1 = (bf16[1,1664,512]{2,1,0:T(8,128)(2,1)S(1)}, bf16[1,1664,512]{2,1,0:T(8,128)(2,1)}, u32[]{:S(2)}) copy-start(bf16[1,1664,512]{2,1,0:T(8,128)(2,1)} %param.15) | copy-start | bytes 5111812
Sparse Core Ops, SparseCore 0:
  449.6 23.3 reduce-scatter.7
  477.5 26.9 reduce-scatter.11
  507.4 13.4 reduce-scatter.9
where the time goes:
time: 535 us; the launch traced here: 528 us
  waiting for transfers between devices  220 us (41%)
  blocking collectives  103 us (19%)
  local copies, waits for them, and re-layouts  70.7 us (13%)
  other arithmetic  44.6 us (8%)
  starting transfers between devices  42.3 us (8%)
  matrix products  32.8 us (6%)
  between operations  14.6 us (3%)
    all_to_all x1, blocking collectives, body(): lax.all_to_all(widen(send_rows), 'dp', split_axis=0, concat_axis=0, tiled...  89.4 us
    all_to_all x1, waiting for transfers between devices, body(): lax.all_to_all(partial_dx, 'dp', split_axis=0, concat_axis=0, tiled=True)  67.1 us
    all_to_all x1, waiting for transfers between devices, body(): lax.all_to_all(widen(send_grads), 'dp', split_axis=0, concat_axis=0, tile...  64.8 us
    all_to_all x1, waiting for transfers between devices, body(): lax.all_to_all(partial_out, 'dp', split_axis=0, concat_axis=0, tiled=True)  57.7 us
    unnamed x5, waiting for transfers between devices  30.2 us
    gather x2, local copies, waits for them, and re-layouts, pick_rows(): picked = jnp.take(returned, pick_index, axis=0)  20.3 us
    all_to_all x1, starting transfers between devices, body(): lax.all_to_all(partial_out, 'dp', split_axis=0, concat_axis=0, tiled=True)  18.4 us
    all_to_all x1, starting transfers between devices, body(): lax.all_to_all(partial_dx, 'dp', split_axis=0, concat_axis=0, tiled=True)  18.3 us
  transfers between devices with their start and end apart: 6, of which 5 were waited for; matrix products, arithmetic and copies ran while one was open for 12% of the time, Pallas kernels for 0%

commit v1 on v0

--- a/solution.py
+++ b/solution.py
@@ -15,7 +15,7 @@
     return (hidden_pre * normal_cdf, normal_cdf + hidden_pre * density)
 
 
-def body(tokens, expert_ids, priority, gate_values, weight_in, weight_out, cotangent):
+def general_body(tokens, expert_ids, priority, gate_values, weight_in, weight_out, cotangent):
     token_count = tokens.shape[0]
     dp_count = lax.axis_size("dp")
     experts = dp_count // HBLK
@@ -127,6 +127,221 @@
     )
 
 
+GROUPS = ((0,), (1, 3), (2,))
+
+
+def plane_body(tokens, expert_ids, priority, gate_values, weight_in, weight_out, cotangent):
+    token_count, width = tokens.shape
+    dp_count = lax.axis_size("dp")
+    experts = dp_count // HBLK
+    slot_count = min(token_count, 2 * token_count // experts + max(1, token_count // (4 * experts)))
+    capacity = 2 * token_count * dp_count // experts
+    contract_first = (((0,), (0,)), ((), ()))
+    contract_last = (((1,), (1,)), ((), ()))
+    place_dp = lax.axis_index("dp")
+    first_half = lax.axis_index("rep") == 0
+    plane, quarter = place_dp // HBLK, place_dp % HBLK
+    core_zero = quarter % 2 == 0
+
+    def dp_index(z, q):
+        return z * HBLK + q
+
+    def permutation(move):
+        pairs = []
+        for z in range(experts):
+            for q in range(HBLK):
+                for x in range(2):
+                    z2, q2, x2 = move(z, q, x)
+                    pairs.append((2 * dp_index(z, q) + x, 2 * dp_index(z2, q2) + x2))
+        return pairs
+
+    def send(array, move):
+        return lax.ppermute(array, ("dp", "rep"), permutation(move))
+
+    def along_first(z, q, x):
+        return (z, q, 1 - x) if q % 2 == 0 else (z, q ^ 2, x)
+
+    def along_second(z, q, x):
+        return (z, q ^ 2, x) if q % 2 == 0 else (z, q, 1 - x)
+
+    def other_core(z, q, x):
+        return (z, q ^ 1, x)
+
+    def planes_on(k):
+        return lambda z, q, x: ((z + k) % experts, q, x)
+
+    groups = GROUPS if experts == 4 else tuple((k,) for k in range(experts))
+
+    ids = [expert_ids[:, 0:1], expert_ids[:, 1:2]]
+    near = (plane + jnp.arange(experts, dtype=jnp.int32)) % experts
+    chosen = [(one == near[None, :]) for one in ids]
+    chosen_any = (chosen[0] | chosen[1]).astype(jnp.bfloat16)
+    before = (
+        jnp.arange(token_count, dtype=jnp.int32)[:, None]
+        > jnp.arange(token_count, dtype=jnp.int32)[None, :]
+    ).astype(jnp.bfloat16)
+    rank = jnp.dot(before, chosen_any, preferred_element_type=jnp.float32).astype(jnp.int32)
+    slots = jnp.arange(slot_count, dtype=jnp.int32)[None, :]
+    at_slot = [rank[:, k : k + 1] == slots for k in range(experts)]
+    place = [[at_slot[k] & chosen[j][:, k : k + 1] for k in range(experts)] for j in range(2)]
+    place_any = [(place[0][k] | place[1][k]).astype(jnp.bfloat16) for k in range(experts)]
+    source = jnp.where(first_half, tokens, cotangent)
+    blocks = [
+        lax.dot_general(
+            place_any[k], source, contract_first, preferred_element_type=jnp.float32
+        ).astype(jnp.bfloat16)
+        for k in range(experts)
+    ]
+    arrived = [blocks[0]] + [send(blocks[k], planes_on(k)) for k in range(1, experts)]
+
+    keys = [priority + PRIO, priority]
+    slot_gate = []
+    slot_key = []
+    for k in range(experts):
+        slot_gate.append(
+            sum(
+                jnp.sum(jnp.where(place[j][k], gate_values[:, j : j + 1], 0.0), axis=0)
+                for j in range(2)
+            )
+        )
+        slot_key.append(
+            sum(
+                jnp.sum(jnp.where(place[j][k], keys[j][:, None].astype(jnp.float32) + 1.0, 0.0), axis=0)
+                for j in range(2)
+            )
+            - 1.0
+        )
+    to_whole = (jnp.arange(experts, dtype=jnp.int32) - plane) % experts
+    card = jnp.concatenate(
+        [jnp.take(jnp.stack(slot_gate), to_whole, axis=0), jnp.take(jnp.stack(slot_key), to_whole, axis=0)], axis=0
+    )
+    cards = lax.all_gather(card, "dp", axis=0, tiled=False)
+    all_gates, all_keys = cards[:, :experts], cards[:, experts:]
+    levels = jnp.arange(2 * PRIO, dtype=jnp.float32)
+    above = jnp.sum(
+        (all_keys[:, :, None, :] >= levels[None, None, :, None]).astype(jnp.float32), axis=(0, 3)
+    )
+    cutoff = jnp.sum((above > capacity).astype(jnp.float32), axis=1)
+    own_keys = lax.dynamic_index_in_dim(all_keys, plane, 1, keepdims=False)
+    own_gates = lax.dynamic_index_in_dim(all_gates, plane, 1, keepdims=False)
+    own_cutoff = lax.dynamic_index_in_dim(cutoff, plane, 0, keepdims=False)
+    own_gates = jnp.where(own_keys >= own_cutoff, own_gates, 0.0)
+    near_cutoff = jnp.take(cutoff, near, axis=0)
+
+    matrix_in = weight_in[0]
+    matrix_out = weight_out[0]
+
+    all_rows, all_grads, all_act, all_pre = [], [], [], []
+    returned = [None] * experts
+    for group in groups:
+        count = len(group) * slot_count
+        own = [arrived[k] for k in group]
+        b00 = own[0] if len(own) == 1 else jnp.concatenate(own, axis=0)
+        r1 = send(b00, along_first)
+        r2 = send(b00, along_second)
+        b11 = send(r1, along_second)
+        b10 = jnp.where(core_zero, r2, r1)
+        b01 = jnp.where(core_zero, r1, r2)
+        near_rows = jnp.concatenate(
+            [
+                jnp.where(first_half, b00, b01),
+                jnp.where(first_half, b10, b11),
+                jnp.where(first_half, b01, b00),
+                jnp.where(first_half, b11, b10),
+            ],
+            axis=0,
+        )
+        far_rows = send(near_rows, other_core)
+        partial = []
+        for far, both in ((0, near_rows), (1, far_rows)):
+            rows, grads = both[: 2 * count], both[2 * count :]
+            index = jnp.stack(
+                [
+                    dp_index((plane - k) % experts, quarter ^ (2 * other_y + far))
+                    for other_y in range(2)
+                    for k in group
+                ]
+            )
+            gate = jnp.take(own_gates, index, axis=0).reshape(2 * count, 1)
+            hidden_pre = jnp.dot(rows, matrix_in, preferred_element_type=jnp.float32)
+            activation, slope = gelu_parts(hidden_pre)
+            gated = (activation * gate).astype(jnp.bfloat16)
+            activation = activation.astype(jnp.bfloat16)
+            grad_act = lax.dot_general(
+                grads, matrix_out, contract_last, preferred_element_type=jnp.float32
+            )
+            grad_pre = (grad_act * slope * gate).astype(jnp.bfloat16)
+            part_out = jnp.dot(activation, matrix_out, preferred_element_type=jnp.float32)
+            part_dx = lax.dot_general(
+                grad_pre, matrix_in, contract_last, preferred_element_type=jnp.float32
+            )
+            partial.append((part_out.astype(jnp.bfloat16), part_dx.astype(jnp.bfloat16)))
+            all_rows.append(rows)
+            all_grads.append(grads)
+            all_act.append(gated)
+            all_pre.append(grad_pre)
+
+        def add(*terms):
+            return sum(term.astype(jnp.float32) for term in terms).astype(jnp.bfloat16)
+
+        sum_out = add(partial[0][0], send(partial[1][0], other_core))
+        sum_dx = add(partial[0][1], send(partial[1][1], other_core))
+        own_sum = jnp.where(first_half, sum_out, sum_dx)
+        other_sum = jnp.where(first_half, sum_dx, sum_out)
+        a00, a10 = own_sum[:count], own_sum[count:]
+        a01, a11 = other_sum[:count], other_sum[count:]
+        back = send(
+            jnp.concatenate([jnp.where(core_zero, a01, a10), a11], axis=0), along_first
+        )
+        last = add(jnp.where(core_zero, a10, a01), back[count:])
+        done = add(a00, back[:count], send(last, along_second))
+        for spot, k in enumerate(group):
+            piece = done[spot * slot_count : (spot + 1) * slot_count]
+            returned[k] = piece if k == 0 else send(piece, planes_on(experts - k))
+
+    grad_in = lax.dot_general(
+        jnp.concatenate(all_rows, axis=0),
+        jnp.concatenate(all_pre, axis=0),
+        contract_first,
+        preferred_element_type=jnp.float32,
+    ).astype(jnp.bfloat16)
+    grad_out = lax.dot_general(
+        jnp.concatenate(all_act, axis=0),
+        jnp.concatenate(all_grads, axis=0),
+        contract_first,
+        preferred_element_type=jnp.float32,
+    ).astype(jnp.bfloat16)
+
+    back_rows = jnp.concatenate(returned, axis=0)
+    mixed = 0.0
+    gate_grads = []
+    for j in range(2):
+        key = keys[j][:, None].astype(jnp.float32)
+        kept = chosen[j] & (key >= near_cutoff[None, :])
+        picker = jnp.concatenate(
+            [(at_slot[k] & kept[:, k : k + 1]).astype(jnp.bfloat16) for k in range(experts)], axis=1
+        )
+        picked = jnp.dot(picker, back_rows, preferred_element_type=jnp.float32)
+        mixed = mixed + picked * jnp.where(first_half, gate_values[:, j : j + 1], 1.0)
+        gate_grads.append(jnp.sum(picked * cotangent.astype(jnp.float32), axis=1, keepdims=True))
+    mixed = mixed.astype(jnp.bfloat16)
+    gate_grad = jnp.concatenate(gate_grads, axis=1)
+    half = width // 2
+    swap = [(0, 1), (1, 0)]
+    left, right = mixed[:, :half], mixed[:, half:]
+    kept_part = jnp.where(first_half, left, right)
+    got_part = lax.ppermute(jnp.where(first_half, right, left), "rep", swap)
+    rows_half = token_count // 2
+    got_gate = lax.ppermute(gate_grad[rows_half:], "rep", swap)
+    return (
+        jnp.where(first_half, kept_part, got_part),
+        jnp.where(first_half, got_part, kept_part),
+        jnp.where(first_half, gate_grad[:rows_half], got_gate),
+        grad_in[None],
+        grad_out[None],
+    )
+
+
 def solution(mesh):
     placed = (
         P("dp", None),
@@ -137,6 +352,7 @@
         P("dp", "rep", None),
         P("dp", None),
     )
+    body = plane_body if mesh.shape["rep"] == 2 else general_body
     return jax.shard_map(
         body,
         mesh=mesh,

time: 535 us -> 168 us (0.31)
  waiting for transfers between devices: 220 us -> 64.1 us
  blocking collectives: 103 us -> 25.1 us
  local copies, waits for them, and re-layouts: 70.7 us -> 12.1 us
  other arithmetic: 44.6 us -> 7.94 us
  between operations: 14.6 us -> 1.53 us
  starting transfers between devices: 42.3 us -> 29.7 us
  matrix products: 32.8 us -> 25.5 us
    all_to_all x3 -> x0, waiting for transfers between devices: 190 us -> none  [the longest x1 67.1 us: body(): lax.all_to_all(partial_dx, 'dp', split_axis=0, concat_axis=0, tiled=True)]
    all_to_all x1 -> x0, blocking collectives: 89.4 us -> none  [body(): lax.all_to_all(widen(send_rows), 'dp', split_axis=0, concat_axis=0, tiled...]
    ppermute x0 -> x32, waiting for transfers between devices: none -> 64.1 us  [the longest x30 60.1 us: send(): return lax.ppermute(array, ('dp', 'rep'), permutation(move))]
    all_to_all x3 -> x0, starting transfers between devices: 41.4 us -> none  [the longest x1 18.4 us: body(): lax.all_to_all(partial_out, 'dp', split_axis=0, concat_axis=0, tiled=True)]
    gather x4 -> x9, local copies, waits for them, and re-layouts: 36.4 us -> 5.11 us  [the longest x6 3.35 us: plane_body(): gate = jnp.take(own_gates, index, axis=0).reshape(2 * count, 1)]
    unnamed x5 -> x0, waiting for transfers between devices: 30.2 us -> none
    ppermute x0 -> x32, starting transfers between devices: none -> 29.7 us  [the longest x30 27.6 us: send(): return lax.ppermute(array, ('dp', 'rep'), permutation(move))]
    all_gather x0 -> x1, blocking collectives: none -> 25.1 us  [plane_body(): cards = lax.all_gather(card, 'dp', axis=0, tiled=False)]
  transfers between devices with their start and end apart: 6 -> 32, of which waited for: 5 -> 13; matrix products, arithmetic and copies ran while one was open for 12% -> 24% of each run, Pallas kernels for 0% -> 0%
where the time goes in v1:
time: 168 us; the launch traced here: 166 us
  waiting for transfers between devices  64.1 us (38%)
  starting transfers between devices  29.7 us (18%)
  matrix products  25.5 us (15%)
  blocking collectives  25.1 us (15%)
  local copies, waits for them, and re-layouts  12.1 us (7%)
  other arithmetic  7.94 us (5%)
    ppermute x30, waiting for transfers between devices, send(): return lax.ppermute(array, ('dp', 'rep'), permutation(move))  60.1 us
    ppermute x30, starting transfers between devices, send(): return lax.ppermute(array, ('dp', 'rep'), permutation(move))  27.6 us
    all_gather x1, blocking collectives, plane_body(): cards = lax.all_gather(card, 'dp', axis=0, tiled=False)  25.1 us
    dot_general x6, matrix products, plane_body(): lax.dot_general(grads, matrix_out, contract_last, preferred_element_type=...  4.55 us
    dot_general x6, matrix products, plane_body(): lax.dot_general(grad_pre, matrix_in, contract_last, preferred_element_typ...  4.48 us
    dot_general x1, matrix products, plane_body(): lax.dot_general(jnp.concatenate(all_act, axis=0), jnp.concatenate(all_gra...  3.8 us
    dot_general x1, matrix products, plane_body(): lax.dot_general(jnp.concatenate(all_rows, axis=0), jnp.concatenate(all_pr...  3.62 us
    unnamed x15, local copies, waits for them, and re-layouts  3.59 us
  transfers between devices with their start and end apart: 32, of which 13 were waited for; matrix products, arithmetic and copies ran while one was open for 24% of the time, Pallas kernels for 0%

profile of v1, /device:TPU:0, one launch (start us, length us, event | category | flops | bytes accessed | tf_op | source)
XLA Modules:
  0.0 165.9 jit_solution(14714487881832972283)
XLA Ops:
  3.1 3.0 %collective-permute-start = (bf16[72,1664]{1,0:T(8,128)(2,1)S(1)}, bf16[72,1664]{1,0:T(8,128)(2,1)S(1)}, u32[]{:S(2)}, u32[]{:S(2)}) collective-permute-start(bf16[72,1664]{1,0:T(8,128)(2,1)S(1)} %convolution_convert_fusion.17), channel_id=1, source_target_pairs={{0,1},{1,0},{2,6},{3,7},{4,5},{5,4},{6,2},{7,3},{8,9},{9,8},{10,14... | collective-permute-start | bytes 718856 | tf_op jit(solution)/shard_map/ppermute | solution.py:159
  6.1 1.5 collective-permute-start.1
  7.8 1.6 collective-permute-start.8
  9.7 2.3 %collective-permute-start.9 = (bf16[72,1664]{1,0:T(8,128)(2,1)S(1)}, bf16[72,1664]{1,0:T(8,128)(2,1)}, u32[]{:S(2)}, u32[]{:S(2)}) collective-permute-start(bf16[72,1664]{1,0:T(8,128)(2,1)S(1)} %convolution_convert_fusion.15), channel_id=1, source_target_pairs={{0,24},{1,25},{2,26},{3,27},{4,28},{5,29},{6,30},{7,31},{8,0},{9,1... | collective-permute-start | bytes 718856 | tf_op jit(solution)/shard_map/ppermute | solution.py:159
  15.0 25.1 %all-gather = f32[128,72]{1,0:T(8,128)S(1)} all-gather(f32[8,72]{1,0:T(8,128)S(1)} %pad_maximum_fusion.9), channel_id=2, replica_groups=mesh['dp'=16,'rep'=2] {'dp'}, dimensions={0}, use_global_device_ids=true | all-gather | bytes 39168 | tf_op jit(solution)/shard_map/all_gather | solution.py:218
  49.8 4.3 %collective-permute-done.2 = bf16[72,1664]{1,0:T(8,128)(2,1)S(1)} collective-permute-done((bf16[72,1664]{1,0:T(8,128)(2,1)S(1)}, bf16[72,1664]{1,0:T(8,128)(2,1)S(1)}, u32[]{:S(2)}, u32[]{:S(2)}) %collective-permute-start.2) | collective-permute-done | bytes 239648 | tf_op jit(solution)/shard_map/ppermute | solution.py:159
  56.9 1.5 collective-permute-start.20
  60.3 9.0 %collective-permute-done.10 = bf16[144,1664]{1,0:T(8,128)(2,1)S(1)} collective-permute-done((bf16[144,1664]{1,0:T(8,128)(2,1)S(1)}, bf16[144,1664]{1,0:T(8,128)(2,1)S(1)}, u32[]{:S(2)}, u32[]{:S(2)}) %collective-permute-start.10) | collective-permute-done | bytes 479264 | tf_op jit(solution)/shard_map/ppermute | solution.py:159
  73.3 4.6 %collective-permute-done.12 = bf16[144,1664]{1,0:T(8,128)(2,1)S(1)} collective-permute-done((bf16[144,1664]{1,0:T(8,128)(2,1)S(1)}, bf16[144,1664]{1,0:T(8,128)(2,1)S(1)}, u32[]{:S(2)}, u32[]{:S(2)}) %collective-permute-start.12) | collective-permute-done | bytes 479264 | tf_op jit(solution)/shard_map/ppermute | solution.py:159
  80.5 1.4 collective-permute-start.22
  82.6 10.4 %collective-permute-done.6 = bf16[144,1664]{1,0:T(8,128)(2,1)S(1)} collective-permute-done((bf16[144,1664]{1,0:T(8,128)(2,1)S(1)}, bf16[144,1664]{1,0:T(8,128)(2,1)S(1)}, u32[]{:S(2)}, u32[]{:S(2)}) %collective-permute-start.6) | collective-permute-done | bytes 479264 | tf_op jit(solution)/shard_map/ppermute | solution.py:159
  94.1 5.2 %collective-permute-done.7 = bf16[72,1664]{1,0:T(8,128)(2,1)S(1)} collective-permute-done((bf16[72,1664]{1,0:T(8,128)(2,1)S(1)}, bf16[72,1664]{1,0:T(8,128)(2,1)S(1)}, u32[]{:S(2)}, u32[]{:S(2)}) %collective-permute-start.7) | collective-permute-done | bytes 239648 | tf_op jit(solution)/shard_map/ppermute | solution.py:159
  114.1 1.6 collective-permute-start.26
  115.7 6.2 %collective-permute-done.16 = bf16[288,1664]{1,0:T(8,128)(2,1)S(1)} collective-permute-done((bf16[288,1664]{1,0:T(8,128)(2,1)S(1)}, bf16[288,1664]{1,0:T(8,128)(2,1)S(1)}, u32[]{:S(2)}, u32[]{:S(2)}) %collective-permute-start.16) | collective-permute-done | bytes 958496 | tf_op jit(solution)/shard_map/ppermute | solution.py:159
  122.1 7.5 %collective-permute-done.26 = bf16[144,1664]{1,0:T(8,128)(2,1)S(1)} collective-permute-done((bf16[144,1664]{1,0:T(8,128)(2,1)S(1)}, bf16[144,1664]{1,0:T(8,128)(2,1)S(1)}, u32[]{:S(2)}, u32[]{:S(2)}) %collective-permute-start.26) | collective-permute-done | bytes 479264 | tf_op jit(solution)/shard_map/ppermute | solution.py:159
  129.8 3.6 %fusion = bf16[1,1664,512]{2,1,0:T(8,128)(2,1)} fusion(bf16[1152,1664]{1,0:T(8,128)(2,1)S(1)} %get-tuple-element.123, bf16[1152,512]{1,0:T(8,128)(2,1)S(1)} %get-tuple-element.200), kind=kOutput, calls=%fused_computation.11 | convolution fusion | flops 1963786240 | bytes 6717440 | tf_op jit(solution)/shard_map/dot_general | solution.py:302
  133.4 2.5 %collective-permute-done.27 = bf16[72,1664]{1,0:T(8,128)(2,1)S(1)} collective-permute-done((bf16[72,1664]{1,0:T(8,128)(2,1)S(1)}, bf16[72,1664]{1,0:T(8,128)(2,1)S(1)}, u32[]{:S(2)}, u32[]{:S(2)}) %collective-permute-start.27) | collective-permute-done | bytes 239648 | tf_op jit(solution)/shard_map/ppermute | solution.py:159
  136.0 3.0 %collective-permute-start.28 = (bf16[72,1664]{1,0:T(8,128)(2,1)S(1)}, bf16[72,1664]{1,0:T(8,128)(2,1)S(1)}, u32[]{:S(2)}, u32[]{:S(2)}) collective-permute-start(bf16[72,1664]{1,0:T(8,128)(2,1)S(1)} %add_convert_fusion.9), channel_id=1, source_target_pairs={{0,16},{1,17},{2,18},{3,19},{4,20},{5,21},{6,22},{7,23},{8,24},{9,... | collective-permute-start | bytes 718856 | tf_op jit(solution)/shard_map/ppermute | solution.py:159
  139.9 3.3 %collective-permute-start.18 = (bf16[72,1664]{1,0:T(8,128)(2,1)S(1)}, bf16[72,1664]{1,0:T(8,128)(2,1)S(1)}, u32[]{:S(2)}, u32[]{:S(2)}) collective-permute-start(bf16[72,1664]{1,0:T(8,128)(2,1)S(1)} %get-tuple-element.140), channel_id=1, source_target_pairs={{0,24},{1,25},{2,26},{3,27},{4,28},{5,29},{6,30},{7,31},{8,0},{9,1... | collective-permute-start | bytes 718856 | tf_op jit(solution)/shard_map/ppermute | solution.py:159
  143.2 3.8 %fusion.1 = bf16[1,512,1664]{2,1,0:T(8,128)(2,1)} fusion(bf16[1152,512]{1,0:T(8,128)(2,1)S(1)} %get-tuple-element.212, bf16[1152,1664]{1,0:T(8,128)(2,1)S(1)} %get-tuple-element.122), kind=kOutput, calls=%fused_computation.12 | convolution fusion | flops 1963786240 | bytes 6717440 | tf_op jit(solution)/shard_map/dot_general | solution.py:308
  147.0 8.6 %collective-permute-done.28 = bf16[72,1664]{1,0:T(8,128)(2,1)S(1)} collective-permute-done((bf16[72,1664]{1,0:T(8,128)(2,1)S(1)}, bf16[72,1664]{1,0:T(8,128)(2,1)S(1)}, u32[]{:S(2)}, u32[]{:S(2)}) %collective-permute-start.28) | collective-permute-done | bytes 239648 | tf_op jit(solution)/shard_map/ppermute | solution.py:159
  158.0 1.5 collective-permute-start.30
  159.6 1.3 collective-permute-done.31
  161.5 2.6 %collective-permute-done.30 = bf16[128,832]{1,0:T(8,128)(2,1)S(1)} collective-permute-done((bf16[128,832]{1,0:T(8,128)(2,1)S(1)}, bf16[128,832]{1,0:T(8,128)(2,1)S(1)}, u32[]{:S(2)}, u32[]{:S(2)}) %collective-permute-start.30) | collective-permute-done | bytes 213024 | tf_op jit(solution)/shard_map/ppermute | solution.py:333
  (190 shorter events, 49.0 us)
Async XLA Ops:
  3.1 44.8 %collective-permute-start = (bf16[72,1664]{1,0:T(8,128)(2,1)S(1)}, bf16[72,1664]{1,0:T(8,128)(2,1)S(1)}, u32[]{:S(2)}, u32[]{:S(2)}) collective-permute-start(bf16[72,1664]{1,0:T(8,128)(2,1)S(1)} %convolution_convert_fusion.17), channel_id=1, source_target_pairs={{0,1},{1,0},{2,6},{3,7},{4,5},{5,4},{6,2},{7,3},{8,9},{9,8},{10,14... | collective-permute-start | bytes 718856 | tf_op jit(solution)/shard_map/ppermute | solution.py:159
  6.1 42.6 %collective-permute-start.1 = (bf16[72,1664]{1,0:T(8,128)(2,1)S(1)}, bf16[72,1664]{1,0:T(8,128)(2,1)S(1)}, u32[]{:S(2)}, u32[]{:S(2)}) collective-permute-start(bf16[72,1664]{1,0:T(8,128)(2,1)S(1)} %convolution_convert_fusion.17), channel_id=1, source_target_pairs={{0,4},{1,5},{2,3},{3,2},{4,0},{5,1},{6,7},{7,6},{8,12},{9,13},{10,... | collective-permute-start | bytes 718856 | tf_op jit(solution)/shard_map/ppermute | solution.py:159
  7.8 41.0 %collective-permute-start.8 = (bf16[72,1664]{1,0:T(8,128)(2,1)S(1)}, bf16[72,1664]{1,0:T(8,128)(2,1)}, u32[]{:S(2)}, u32[]{:S(2)}) collective-permute-start(bf16[72,1664]{1,0:T(8,128)(2,1)S(1)} %convolution_convert_fusion.16), channel_id=1, source_target_pairs={{0,8},{1,9},{2,10},{3,11},{4,12},{5,13},{6,14},{7,15},{8,16},{9,17... | collective-permute-start | bytes 718856 | tf_op jit(solution)/shard_map/ppermute | solution.py:159
  9.7 44.7 %collective-permute-start.9 = (bf16[72,1664]{1,0:T(8,128)(2,1)S(1)}, bf16[72,1664]{1,0:T(8,128)(2,1)}, u32[]{:S(2)}, u32[]{:S(2)}) collective-permute-start(bf16[72,1664]{1,0:T(8,128)(2,1)S(1)} %convolution_convert_fusion.15), channel_id=1, source_target_pairs={{0,24},{1,25},{2,26},{3,27},{4,28},{5,29},{6,30},{7,31},{8,0},{9,1... | collective-permute-start | bytes 718856 | tf_op jit(solution)/shard_map/ppermute | solution.py:159
  12.2 44.7 %collective-permute-start.19 = (bf16[72,1664]{1,0:T(8,128)(2,1)S(1)}, bf16[72,1664]{1,0:T(8,128)(2,1)S(1)}, u32[]{:S(2)}, u32[]{:S(2)}) collective-permute-start(bf16[72,1664]{1,0:T(8,128)(2,1)S(1)} %convolution_convert_fusion.14), channel_id=1, source_target_pairs={{0,16},{1,17},{2,18},{3,19},{4,20},{5,21},{6,22},{7,23},{8,24},{9,... | collective-permute-start | bytes 718856 | tf_op jit(solution)/shard_map/ppermute | solution.py:159
  47.9 6.2 %collective-permute-start.2 = (bf16[72,1664]{1,0:T(8,128)(2,1)S(1)}, bf16[72,1664]{1,0:T(8,128)(2,1)S(1)}, u32[]{:S(2)}, u32[]{:S(2)}) collective-permute-start(bf16[72,1664]{1,0:T(8,128)(2,1)S(1)} %collective-permute-done), channel_id=1, source_target_pairs={{0,4},{1,5},{2,3},{3,2},{4,0},{5,1},{6,7},{7,6},{8,12},{9,13},{10,... | collective-permute-start | bytes 718856 | tf_op jit(solution)/shard_map/ppermute | solution.py:159
  54.3 15.6 %collective-permute-start.3 = (bf16[288,1664]{1,0:T(8,128)(2,1)S(1)}, bf16[288,1664]{1,0:T(8,128)(2,1)S(1)}, u32[]{:S(2)}, u32[]{:S(2)}) collective-permute-start(bf16[288,1664]{1,0:T(8,128)(2,1)S(1)} %pad_maximum_fusion.1), channel_id=1, source_target_pairs={{0,2},{1,3},{2,0},{3,1},{4,6},{5,7},{6,4},{7,5},{8,10},{9,11},{10,... | collective-permute-start | bytes 2875400 | tf_op jit(solution)/shard_map/ppermute | solution.py:159
  55.5 13.7 %collective-permute-start.10 = (bf16[144,1664]{1,0:T(8,128)(2,1)S(1)}, bf16[144,1664]{1,0:T(8,128)(2,1)S(1)}, u32[]{:S(2)}, u32[]{:S(2)}) collective-permute-start(bf16[144,1664]{1,0:T(8,128)(2,1)S(1)} %constant_dynamic-update-slice_fusion), channel_id=1, source_target_pairs={{0,1},{1,0},{2,6},{3,7},{4,5},{5,4},{6,2},{7,3},{8,9},{9,8},{10,14... | collective-permute-start | bytes 1437704 | tf_op jit(solution)/shard_map/ppermute | solution.py:159
  56.1 16.9 %collective-permute-start.11 = (bf16[144,1664]{1,0:T(8,128)(2,1)S(1)}, bf16[144,1664]{1,0:T(8,128)(2,1)S(1)}, u32[]{:S(2)}, u32[]{:S(2)}) collective-permute-start(bf16[144,1664]{1,0:T(8,128)(2,1)S(1)} %constant_dynamic-update-slice_fusion), channel_id=1, source_target_pairs={{0,4},{1,5},{2,3},{3,2},{4,0},{5,1},{6,7},{7,6},{8,12},{9,13},{10,... | collective-permute-start | bytes 1437704 | tf_op jit(solution)/shard_map/ppermute | solution.py:159
  56.9 23.6 %collective-permute-start.20 = (bf16[72,1664]{1,0:T(8,128)(2,1)S(1)}, bf16[72,1664]{1,0:T(8,128)(2,1)S(1)}, u32[]{:S(2)}, u32[]{:S(2)}) collective-permute-start(bf16[72,1664]{1,0:T(8,128)(2,1)S(1)} %collective-permute-done.19), channel_id=1, source_target_pairs={{0,1},{1,0},{2,6},{3,7},{4,5},{5,4},{6,2},{7,3},{8,9},{9,8},{10,14... | collective-permute-start | bytes 718856 | tf_op jit(solution)/shard_map/ppermute | solution.py:159
  69.3 8.7 %collective-permute-start.12 = (bf16[144,1664]{1,0:T(8,128)(2,1)S(1)}, bf16[144,1664]{1,0:T(8,128)(2,1)S(1)}, u32[]{:S(2)}, u32[]{:S(2)}) collective-permute-start(bf16[144,1664]{1,0:T(8,128)(2,1)S(1)} %collective-permute-done.10), channel_id=1, source_target_pairs={{0,4},{1,5},{2,3},{3,2},{4,0},{5,1},{6,7},{7,6},{8,12},{9,13},{10,... | collective-permute-start | bytes 1437704 | tf_op jit(solution)/shard_map/ppermute | solution.py:159
  72.3 6.3 %collective-permute-start.5 = (bf16[144,1664]{1,0:T(8,128)(2,1)S(1)}, bf16[144,1664]{1,0:T(8,128)(2,1)S(1)}, u32[]{:S(2)}, u32[]{:S(2)}) collective-permute-start(bf16[144,1664]{1,0:T(8,128)(2,1)S(1)} %convolution_convert_fusion.10), channel_id=1, source_target_pairs={{0,2},{1,3},{2,0},{3,1},{4,6},{5,7},{6,4},{7,5},{8,10},{9,11},{10,... | collective-permute-start | bytes 1437704 | tf_op jit(solution)/shard_map/ppermute | solution.py:159
  78.5 21.0 %collective-permute-start.13 = (bf16[576,1664]{1,0:T(8,128)(2,1)S(1)}, bf16[576,1664]{1,0:T(8,128)(2,1)S(1)}, u32[]{:S(2)}, u32[]{:S(2)}) collective-permute-start(bf16[576,1664]{1,0:T(8,128)(2,1)S(1)} %pad_maximum_fusion), channel_id=1, source_target_pairs={{0,2},{1,3},{2,0},{3,1},{4,6},{5,7},{6,4},{7,5},{8,10},{9,11},{10,... | collective-permute-start | bytes 5750792 | tf_op jit(solution)/shard_map/ppermute | solution.py:159
  79.2 13.9 %collective-permute-start.6 = (bf16[144,1664]{1,0:T(8,128)(2,1)S(1)}, bf16[144,1664]{1,0:T(8,128)(2,1)S(1)}, u32[]{:S(2)}, u32[]{:S(2)}) collective-permute-start(bf16[144,1664]{1,0:T(8,128)(2,1)S(1)} %pad_maximum_fusion.5), channel_id=1, source_target_pairs={{0,1},{1,0},{2,6},{3,7},{4,5},{5,4},{6,2},{7,3},{8,9},{9,8},{10,14... | collective-permute-start | bytes 1437704 | tf_op jit(solution)/shard_map/ppermute | solution.py:159
  79.8 23.6 %collective-permute-start.21 = (bf16[72,1664]{1,0:T(8,128)(2,1)S(1)}, bf16[72,1664]{1,0:T(8,128)(2,1)S(1)}, u32[]{:S(2)}, u32[]{:S(2)}) collective-permute-start(bf16[72,1664]{1,0:T(8,128)(2,1)S(1)} %collective-permute-done.19), channel_id=1, source_target_pairs={{0,4},{1,5},{2,3},{3,2},{4,0},{5,1},{6,7},{7,6},{8,12},{9,13},{10,... | collective-permute-start | bytes 718856 | tf_op jit(solution)/shard_map/ppermute | solution.py:159
  80.5 23.1 %collective-permute-start.22 = (bf16[72,1664]{1,0:T(8,128)(2,1)S(1)}, bf16[72,1664]{1,0:T(8,128)(2,1)S(1)}, u32[]{:S(2)}, u32[]{:S(2)}) collective-permute-start(bf16[72,1664]{1,0:T(8,128)(2,1)S(1)} %collective-permute-done.20), channel_id=1, source_target_pairs={{0,4},{1,5},{2,3},{3,2},{4,0},{5,1},{6,7},{7,6},{8,12},{9,13},{10,... | collective-permute-start | bytes 718856 | tf_op jit(solution)/shard_map/ppermute | solution.py:159
  93.1 6.2 %collective-permute-start.7 = (bf16[72,1664]{1,0:T(8,128)(2,1)S(1)}, bf16[72,1664]{1,0:T(8,128)(2,1)S(1)}, u32[]{:S(2)}, u32[]{:S(2)}) collective-permute-start(bf16[72,1664]{1,0:T(8,128)(2,1)S(1)} %add_convert_fusion.12), channel_id=1, source_target_pairs={{0,4},{1,5},{2,3},{3,2},{4,0},{5,1},{6,7},{7,6},{8,12},{9,13},{10,... | collective-permute-start | bytes 718856 | tf_op jit(solution)/shard_map/ppermute | solution.py:159
  107.9 13.9 %collective-permute-start.16 = (bf16[288,1664]{1,0:T(8,128)(2,1)S(1)}, bf16[288,1664]{1,0:T(8,128)(2,1)S(1)}, u32[]{:S(2)}, u32[]{:S(2)}) collective-permute-start(bf16[288,1664]{1,0:T(8,128)(2,1)S(1)} %pad_maximum_fusion.2), channel_id=1, source_target_pairs={{0,1},{1,0},{2,6},{3,7},{4,5},{5,4},{6,2},{7,3},{8,9},{9,8},{10,14... | collective-permute-start | bytes 2875400 | tf_op jit(solution)/shard_map/ppermute | solution.py:159
  114.1 15.5 %collective-permute-start.26 = (bf16[144,1664]{1,0:T(8,128)(2,1)S(1)}, bf16[144,1664]{1,0:T(8,128)(2,1)S(1)}, u32[]{:S(2)}, u32[]{:S(2)}) collective-permute-start(bf16[144,1664]{1,0:T(8,128)(2,1)S(1)} %pad_maximum_fusion.6), channel_id=1, source_target_pairs={{0,1},{1,0},{2,6},{3,7},{4,5},{5,4},{6,2},{7,3},{8,9},{9,8},{10,14... | collective-permute-start | bytes 1437704 | tf_op jit(solution)/shard_map/ppermute | solution.py:159
  122.0 17.0 %collective-permute-start.17 = (bf16[144,1664]{1,0:T(8,128)(2,1)S(1)}, bf16[144,1664]{1,0:T(8,128)(2,1)S(1)}, u32[]{:S(2)}, u32[]{:S(2)}) collective-permute-start(bf16[144,1664]{1,0:T(8,128)(2,1)S(1)} %add_convert_fusion.5), channel_id=1, source_target_pairs={{0,4},{1,5},{2,3},{3,2},{4,0},{5,1},{6,7},{7,6},{8,12},{9,13},{10,... | collective-permute-start | bytes 1437704 | tf_op jit(solution)/shard_map/ppermute | solution.py:159
  129.7 6.2 %collective-permute-start.27 = (bf16[72,1664]{1,0:T(8,128)(2,1)S(1)}, bf16[72,1664]{1,0:T(8,128)(2,1)S(1)}, u32[]{:S(2)}, u32[]{:S(2)}) collective-permute-start(bf16[72,1664]{1,0:T(8,128)(2,1)S(1)} %add_convert_fusion.10), channel_id=1, source_target_pairs={{0,4},{1,5},{2,3},{3,2},{4,0},{5,1},{6,7},{7,6},{8,12},{9,13},{10,... | collective-permute-start | bytes 718856 | tf_op jit(solution)/shard_map/ppermute | solution.py:159
  136.0 19.5 %collective-permute-start.28 = (bf16[72,1664]{1,0:T(8,128)(2,1)S(1)}, bf16[72,1664]{1,0:T(8,128)(2,1)S(1)}, u32[]{:S(2)}, u32[]{:S(2)}) collective-permute-start(bf16[72,1664]{1,0:T(8,128)(2,1)S(1)} %add_convert_fusion.9), channel_id=1, source_target_pairs={{0,16},{1,17},{2,18},{3,19},{4,20},{5,21},{6,22},{7,23},{8,24},{9,... | collective-permute-start | bytes 718856 | tf_op jit(solution)/shard_map/ppermute | solution.py:159
  139.3 16.2 %collective-permute-start.29 = (bf16[72,1664]{1,0:T(8,128)(2,1)S(1)}, bf16[72,1664]{1,0:T(8,128)(2,1)S(1)}, u32[]{:S(2)}, u32[]{:S(2)}) collective-permute-start(bf16[72,1664]{1,0:T(8,128)(2,1)S(1)} %get-tuple-element.141), channel_id=1, source_target_pairs={{0,8},{1,9},{2,10},{3,11},{4,12},{5,13},{6,14},{7,15},{8,16},{9,17... | collective-permute-start | bytes 718856 | tf_op jit(solution)/shard_map/ppermute | solution.py:159
  139.9 15.6 %collective-permute-start.18 = (bf16[72,1664]{1,0:T(8,128)(2,1)S(1)}, bf16[72,1664]{1,0:T(8,128)(2,1)S(1)}, u32[]{:S(2)}, u32[]{:S(2)}) collective-permute-start(bf16[72,1664]{1,0:T(8,128)(2,1)S(1)} %get-tuple-element.140), channel_id=1, source_target_pairs={{0,24},{1,25},{2,26},{3,27},{4,28},{5,29},{6,30},{7,31},{8,0},{9,1... | collective-permute-start | bytes 718856 | tf_op jit(solution)/shard_map/ppermute | solution.py:159
  (13 other events, 119.0 us)

commit v2 on v0

--- a/solution.py
+++ b/solution.py
@@ -15,7 +15,7 @@
     return (hidden_pre * normal_cdf, normal_cdf + hidden_pre * density)
 
 
-def body(tokens, expert_ids, priority, gate_values, weight_in, weight_out, cotangent):
+def general_body(tokens, expert_ids, priority, gate_values, weight_in, weight_out, cotangent):
     token_count = tokens.shape[0]
     dp_count = lax.axis_size("dp")
     experts = dp_count // HBLK
@@ -127,6 +127,367 @@
     )
 
 
+GROUPS = ((0,), (1,), (3,), (2,))
+PLAN = (
+    "Z 1",
+    "D1 0",
+    "Z 3",
+    "Z 2",
+    "D2 0",
+    "K 0",
+    "D1 1",
+    "SEL 0",
+    "D2 1",
+    "D1 2",
+    "CN 0",
+    "CF 0",
+    "SEL 1",
+    "D2 2",
+    "D1 3",
+    "K 1",
+    "CN 1",
+    "CF 1",
+    "SEL 2",
+    "D2 3",
+    "K 2",
+    "R1 1",
+    "CN 2",
+    "CF 2",
+    "SEL 3",
+    "R2 1",
+    "R1 2",
+    "K 3",
+    "CN 3",
+    "CF 3",
+    "H 1",
+    "R2 2",
+    "R1 3",
+    "H 2",
+    "R1 0",
+    "R2 3",
+    "CUT 0",
+    "W1 0",
+    "H 3",
+    "R2 0",
+    "W2 0",
+    "H 0",
+)
+
+
+def plane_body(tokens, expert_ids, priority, gate_values, weight_in, weight_out, cotangent):
+    token_count, width = tokens.shape
+    dp_count = lax.axis_size("dp")
+    experts = dp_count // HBLK
+    slot_count = min(token_count, 2 * token_count // experts + max(1, token_count // (4 * experts)))
+    capacity = 2 * token_count * dp_count // experts
+    contract_first = (((0,), (0,)), ((), ()))
+    contract_last = (((1,), (1,)), ((), ()))
+    place_dp = lax.axis_index("dp")
+    first_half = lax.axis_index("rep") == 0
+    plane, quarter = place_dp // HBLK, place_dp % HBLK
+    core_zero = quarter % 2 == 0
+    groups = GROUPS
+
+    def permutation(move):
+        pairs = []
+        for z in range(experts):
+            for q in range(HBLK):
+                for x in range(2):
+                    z2, q2, x2 = move(z, q, x)
+                    pairs.append((2 * (z * HBLK + q) + x, 2 * (z2 * HBLK + q2) + x2))
+        return pairs
+
+    def send(array, move):
+        return lax.ppermute(array, ("dp", "rep"), permutation(move))
+
+    def along_first(z, q, x):
+        return (z, q, 1 - x) if q % 2 == 0 else (z, q ^ 2, x)
+
+    def along_second(z, q, x):
+        return (z, q ^ 2, x) if q % 2 == 0 else (z, q, 1 - x)
+
+    def other_core(z, q, x):
+        return (z, q ^ 1, x)
+
+    def other_row(z, q, x):
+        return (z, q ^ 2, x)
+
+    def planes_on(k):
+        return lambda z, q, x: ((z + k) % experts, q, x)
+
+    def add(*terms):
+        return sum(term.astype(jnp.float32) for term in terms).astype(jnp.bfloat16)
+
+    def step(made, *values):
+        if made:
+            values, _ = lax.optimization_barrier((values, made))
+        return values if len(values) > 1 else values[0]
+
+    def join(parts):
+        return parts[0] if len(parts) == 1 else jnp.concatenate(parts, axis=0)
+
+    ids = [expert_ids[:, j][None, :] for j in range(2)]
+    gates = [gate_values[:, j][None, :] for j in range(2)]
+    keys = [(priority + PRIO)[None, :], priority[None, :]]
+    near = ((plane + jnp.arange(experts, dtype=jnp.int32)) % experts)[:, None]
+    chosen = [one == near for one in ids]
+    chosen_any = (chosen[0] | chosen[1]).astype(jnp.bfloat16)
+    token_index = jnp.arange(token_count, dtype=jnp.int32)
+    before = (token_index[:, None] < token_index[None, :]).astype(jnp.bfloat16)
+    rank = jnp.dot(chosen_any, before, preferred_element_type=jnp.float32).astype(jnp.int32)
+    slots = jnp.arange(slot_count, dtype=jnp.int32)[:, None]
+    place = [
+        [(rank[k : k + 1] == slots) & chosen[j][k : k + 1] for k in range(experts)] for j in range(2)
+    ]
+    source = jnp.where(first_half, tokens, cotangent)
+
+    spread = jnp.concatenate(
+        [(place[0][k] | place[1][k]).astype(jnp.bfloat16) for k in range(experts)], axis=0
+    )
+    near_gate = sum(jnp.where(chosen[j], gates[j], 0.0) for j in range(2))
+    slot_gate = jnp.concatenate(
+        [
+            jnp.sum(
+                jnp.where(place[0][k] | place[1][k], near_gate[k : k + 1], 0.0), axis=1, keepdims=True
+            )
+            for k in range(experts)
+        ],
+        axis=0,
+    )
+    slot_gate = jnp.where(first_half, 1.0, slot_gate)
+    spread, slot_gate, source = lax.optimization_barrier((spread, slot_gate, source))
+
+    def rows_for(k, made):
+        span = slice(k * slot_count, (k + 1) * slot_count)
+        rows = jnp.dot(
+            step(made, spread)[span], source, preferred_element_type=jnp.float32
+        )
+        return (rows * slot_gate[span]).astype(jnp.bfloat16)
+
+    matrix_in = weight_in[0]
+    matrix_out = weight_out[0]
+    state = [dict(count=slot_count * len(group)) for group in groups]
+    home = {}
+
+    def spread_first(g, block):
+        one = state[g]
+        one["b00"] = block
+        one["r1"] = send(block, along_first)
+        one["r2"] = send(block, along_second)
+
+    def spread_second(g, made):
+        one = state[g]
+        one["r1"] = step(made, one["r1"])
+        one["b11"] = send(one["r1"], along_second)
+
+    def gather_near(g, made):
+        one = state[g]
+        b00, r1, r2, b11 = step(made, one["b00"], one["r1"], one["r2"], one["b11"])
+        b10 = jnp.where(core_zero, r2, r1)
+        b01 = jnp.where(core_zero, r1, r2)
+        one["near"] = jnp.concatenate(
+            [
+                jnp.where(first_half, b00, b01),
+                jnp.where(first_half, b10, b11),
+                jnp.where(first_half, b01, b00),
+                jnp.where(first_half, b11, b10),
+            ],
+            axis=0,
+        )
+        one["far"] = send(one["near"], other_core)
+        return [one["near"]]
+
+    def expert_work(g, name, made):
+        one = state[g]
+        both = step(made, one[name])
+        rows, grads = both[: 2 * one["count"]], both[2 * one["count"] :]
+        hidden_pre = jnp.dot(rows, matrix_in, preferred_element_type=jnp.float32)
+        activation, slope = gelu_parts(hidden_pre)
+        activation = activation.astype(jnp.bfloat16)
+        grad_act = lax.dot_general(
+            grads, matrix_out, contract_last, preferred_element_type=jnp.float32
+        )
+        grad_pre = (grad_act * slope).astype(jnp.bfloat16)
+        part_out = jnp.dot(activation, matrix_out, preferred_element_type=jnp.float32)
+        part_dx = lax.dot_general(
+            grad_pre, matrix_in, contract_last, preferred_element_type=jnp.float32
+        )
+        parts = (part_out.astype(jnp.bfloat16), part_dx.astype(jnp.bfloat16))
+        one[name + "_saved"] = (rows, grads, activation, grad_pre)
+        parts = jnp.concatenate(parts, axis=0)
+        one[name + "_parts"] = send(parts, other_core) if name == "far" else parts
+        return [parts]
+
+    def reduce_first(g, made):
+        one = state[g]
+        count = one["count"]
+        sums = add(*step(made, one["near_parts"], one["far_parts"]))
+        sum_out, sum_dx = sums[: 2 * count], sums[2 * count :]
+        own_sum = jnp.where(first_half, sum_out, sum_dx)
+        other_sum = jnp.where(first_half, sum_dx, sum_out)
+        a00, a10 = own_sum[:count], own_sum[count:]
+        a01, a11 = other_sum[:count], other_sum[count:]
+        away = jnp.concatenate([jnp.where(core_zero, a01, a10), a11], axis=0)
+        one["a00"], one["rest"] = a00, jnp.where(core_zero, a10, a01)
+        one["back"] = send(away, along_first)
+        return [away]
+
+    def reduce_second(g, made):
+        one = state[g]
+        one["back"], rest = step(made, one["back"], one["rest"])
+        last = add(rest, one["back"][one["count"] :])
+        one["last"] = send(last, along_second)
+        return [last]
+
+    def go_home(g, made):
+        one = state[g]
+        a00, back, last = step(made, one["a00"], one["back"], one["last"])
+        done = add(a00, back[: one["count"]], last)
+        for spot, k in enumerate(groups[g]):
+            piece = done[spot * slot_count : (spot + 1) * slot_count]
+            home[k] = piece if k == 0 else send(piece, planes_on(experts - k))
+        return [done]
+
+    arrived = {}
+    made = []
+    cards = [
+        jnp.stack(
+            [
+                sum(
+                    jnp.sum(jnp.where(place[j][k], keys[j].astype(jnp.float32) + 1.0, 0.0), axis=1)
+                    for j in range(2)
+                )
+                for k in range(experts)
+            ]
+        )
+        - 1.0
+    ]
+    cards = jnp.concatenate(cards, axis=0)[None, None]
+
+    for entry in PLAN:
+        name, g = entry.split()[0], int(entry.split()[1])
+        if name == "Z":
+            block = rows_for(g, made)
+            arrived[g] = send(block, planes_on(g))
+            made = [block]
+        elif name == "D1" and g == 0:
+            block = rows_for(0, made)
+            spread_first(0, block)
+            made = [block]
+        elif name == "D1":
+            parts = step(made, *[arrived[k] for k in groups[g]])
+            spread_first(g, parts if len(groups[g]) == 1 else join(parts))
+        elif name == "D2":
+            spread_second(g, made)
+        elif name == "SEL":
+            made = gather_near(g, made)
+        elif name == "CN":
+            made = expert_work(g, "near", made)
+        elif name == "CF":
+            made = expert_work(g, "far", made)
+        elif name == "R1":
+            made = reduce_first(g, made)
+        elif name == "R2":
+            made = reduce_second(g, made)
+        elif name == "H":
+            made = go_home(g, made)
+        elif name == "K":
+            cards, got = step(made, cards, got) if g else (step(made, cards), None)
+            if g:
+                cards = jnp.concatenate([cards, got], axis=0 if g < 3 else 1)
+            if g == 0:
+                got = send(cards, planes_on(1))
+            elif g == 1:
+                got = send(cards, planes_on(2))
+            else:
+                got = send(cards, (other_row, other_core)[g - 2])
+        elif name == "CUT":
+            cards, got = step(made, cards, got)
+            cards = jnp.concatenate([cards, got], axis=1)
+            near_keys = jnp.stack(
+                [
+                    jnp.concatenate([cards[d, :, (r + d) % experts] for d in range(experts)], axis=0)
+                    for r in range(experts)
+                ]
+            )
+            levels = jnp.arange(2 * PRIO, dtype=jnp.float32)
+            above = jnp.sum(
+                (near_keys[:, :, None, :] >= levels[None, None, :, None]).astype(jnp.float32),
+                axis=(1, 3),
+            )
+            near_cutoff = jnp.sum((above > capacity).astype(jnp.float32), axis=1)
+            kept_rows = jnp.concatenate(
+                [
+                    (cards[k, 2 * far + other_y, k] >= near_cutoff[0]).astype(jnp.float32)
+                    for group in groups
+                    for far in range(2)
+                    for other_y in range(2)
+                    for k in group
+                ]
+            )[:, None] > 0.0
+            made = [kept_rows]
+        elif name in ("W1", "W2"):
+            saved = [one[half + "_saved"] for one in state for half in ("near", "far")]
+            rows, grads, act, pre = [jnp.concatenate(part, axis=0) for part in zip(*saved)]
+            if name == "W1":
+                pre = step(made, jnp.where(kept_rows, pre, 0))
+                grad_in = lax.dot_general(
+                    rows, pre, contract_first, preferred_element_type=jnp.float32
+                ).astype(jnp.bfloat16)
+                made = [grad_in]
+            else:
+                act = step(made, jnp.where(kept_rows, act, 0))
+                grad_out = lax.dot_general(
+                    act, grads, contract_first, preferred_element_type=jnp.float32
+                ).astype(jnp.bfloat16)
+                made = [grad_out]
+
+    back_rows = jnp.concatenate([home[k] for k in range(experts)], axis=0)
+    cotangent_columns = cotangent.T.astype(jnp.float32)
+    mixed = 0.0
+    gate_grads = []
+    for j in range(2):
+        token_cutoff = jnp.sum(
+            chosen[j].astype(jnp.float32) * near_cutoff[:, None], axis=0, keepdims=True
+        )
+        kept = keys[j].astype(jnp.float32) >= token_cutoff
+        picker = jnp.concatenate(
+            [(place[j][k] & kept).astype(jnp.bfloat16) for k in range(experts)], axis=0
+        )
+        picked = lax.dot_general(
+            back_rows, picker, contract_first, preferred_element_type=jnp.float32
+        )
+        mixed = mixed + picked * jnp.where(first_half, gates[j], 1.0)
+        gate_grads.append(jnp.sum(picked * cotangent_columns, axis=0, keepdims=True))
+    mixed = mixed.astype(jnp.bfloat16)
+    gate_grad = jnp.concatenate(gate_grads, axis=0)
+    terms, left = [], gate_grad
+    for _ in range(3):
+        term = lax.reduce_precision(left, exponent_bits=8, mantissa_bits=7)
+        terms.append(term.astype(jnp.bfloat16))
+        left = left - term
+    spare = jnp.zeros((10, token_count), jnp.bfloat16)
+    half = width // 2
+    upper, lower = mixed[:half], mixed[half:]
+    kept_part = jnp.where(first_half, upper, lower)
+    got = lax.ppermute(
+        jnp.concatenate([jnp.where(first_half, lower, upper)] + terms + [spare], axis=0),
+        "rep",
+        [(0, 1), (1, 0)],
+    )
+    got_part = got[:half]
+    got_terms = got[half : half + 6].astype(jnp.float32)
+    got_gate = got_terms[0:2] + got_terms[2:4] + got_terms[4:6]
+    rows_half = token_count // 2
+    return (
+        jnp.where(first_half, kept_part, got_part).T,
+        jnp.where(first_half, got_part, kept_part).T,
+        jnp.where(first_half, gate_grad[:, :rows_half], got_gate[:, rows_half:]).T,
+        grad_in[None],
+        grad_out[None],
+    )
+
+
 def solution(mesh):
     placed = (
         P("dp", None),
@@ -137,6 +498,7 @@
         P("dp", "rep", None),
         P("dp", None),
     )
+    body = plane_body if mesh.shape["rep"] == 2 and mesh.shape["dp"] == 4 * HBLK else general_body
     return jax.shard_map(
         body,
         mesh=mesh,

time: 535 us -> 134 us (0.25); the launches traced: 528 us -> 133 us
  waiting for transfers between devices: 220 us -> 28.7 us
  blocking collectives: 103 us -> 0 us
  local copies, waits for them, and re-layouts: 70.7 us -> 4.86 us
  other arithmetic: 44.6 us -> 19.2 us
  between operations: 14.6 us -> 1.65 us
    all_to_all x3 -> x0, waiting for transfers between devices: 190 us -> none  [the longest x1 67.1 us: body(): lax.all_to_all(partial_dx, 'dp', split_axis=0, concat_axis=0, tiled=True)]
    all_to_all x1 -> x0, blocking collectives: 89.4 us -> none  [body(): lax.all_to_all(widen(send_rows), 'dp', split_axis=0, concat_axis=0, tiled...]
    ppermute x0 -> x39, starting transfers between devices: none -> 46.3 us  [the longest x38 45.4 us: send(): return lax.ppermute(array, ('dp', 'rep'), permutation(move))]
    all_to_all x3 -> x0, starting transfers between devices: 41.4 us -> none  [the longest x1 18.4 us: body(): lax.all_to_all(partial_out, 'dp', split_axis=0, concat_axis=0, tiled=True)]
    gather x4 -> x0, local copies, waits for them, and re-layouts: 36.4 us -> none  [the longest x2 20.3 us: pick_rows(): picked = jnp.take(returned, pick_index, axis=0)]
    unnamed x5 -> x0, waiting for transfers between devices: 30.2 us -> none
    ppermute x0 -> x39, waiting for transfers between devices: none -> 28.7 us  [the longest x38 23.2 us: send(): return lax.ppermute(array, ('dp', 'rep'), permutation(move))]
    reduce_sum x7 -> x4, other arithmetic: 25.2 us -> 1.29 us  [the longest x1 0.78 us: plane_body(): jnp.sum((near_keys[:, :, None, :] >= levels[None, None, :, None]).astype(...]
  transfers between devices with their start and end apart: 6 -> 39, of which waited for: 5 -> 12; matrix products, arithmetic and copies ran while one was open for 12% -> 34% of each run, Pallas kernels for 0% -> 0%
where the time goes in v2:
time: 134 us; the launch traced here: 133 us
  starting transfers between devices  46.3 us (35%)
  matrix products  32.4 us (24%)
  waiting for transfers between devices  28.7 us (21%)
  other arithmetic  19.2 us (14%)
  local copies, waits for them, and re-layouts  4.86 us (4%)
  between operations  1.65 us (1%)
    ppermute x38, starting transfers between devices, send(): return lax.ppermute(array, ('dp', 'rep'), permutation(move))  45.4 us
    ppermute x38, waiting for transfers between devices, send(): return lax.ppermute(array, ('dp', 'rep'), permutation(move))  23.2 us
    convert_element_type x12, other arithmetic, add(): sum((term.astype(jnp.float32) for term in terms)).astype(jnp.bfloat16)  6.69 us
    dot_general x8, matrix products, expert_work(): lax.dot_general(grads, matrix_out, contract_last, preferred_element_type=...  5.66 us
    dot_general x8, matrix products, expert_work(): lax.dot_general(grad_pre, matrix_in, contract_last, preferred_element_typ...  5.59 us
    ppermute x1, waiting for transfers between devices, plane_body(): lax.ppermute(jnp.concatenate([jnp.where(first_half, lower, upper)] + term...  5.48 us
    dot_general x1, matrix products, plane_body(): lax.dot_general(act, grads, contract_first, preferred_element_type=jnp.fl...  3.79 us
    dot_general x8, matrix products, expert_work(): hidden_pre = jnp.dot(rows, matrix_in, preferred_element_type=jnp.float32)  3.7 us
  transfers between devices with their start and end apart: 39, of which 12 were waited for; matrix products, arithmetic and copies ran while one was open for 34% of the time, Pallas kernels for 0%

profile of v2, /device:TPU:0, one launch (start us, length us, event | category | flops | bytes accessed | tf_op | source)
XLA Modules:
  0.0 133.1 jit_solution(13906694926580447774)
XLA Ops:
  6.1 3.0 %collective-permute-start = (bf16[72,1664]{1,0:T(8,128)(2,1)S(1)}, bf16[72,1664]{1,0:T(8,128)(2,1)S(1)}, u32[]{:S(2)}, u32[]{:S(2)}) collective-permute-start(bf16[72,1664]{1,0:T(8,128)(2,1)S(1)} %fusion.1), channel_id=1, source_target_pairs={{0,1},{1,0},{2,6},{3,7},{4,5},{5,4},{6,2},{7,3},{8,9},{9,8},{10,14... | collective-permute-start | bytes 718856 | tf_op jit(solution)/shard_map/ppermute | solution.py:201
  10.6 1.6 %collective-permute-start.7 = (bf16[72,1664]{1,0:T(8,128)(2,1)}, bf16[72,1664]{1,0:T(8,128)(2,1)}, u32[]{:S(2)}, u32[]{:S(2)}) collective-permute-start(bf16[72,1664]{1,0:T(8,128)(2,1)} %fusion), channel_id=1, source_target_pairs={{0,8},{1,9},{2,10},{3,11},{4,12},{5,13},{6,14},{7,15},{8,16},{9,17... | collective-permute-start | bytes 718856 | tf_op jit(solution)/shard_map/ppermute | solution.py:201
  13.1 2.2 %collective-permute-start.5 = (bf16[72,1664]{1,0:T(8,128)(2,1)}, bf16[72,1664]{1,0:T(8,128)(2,1)S(1)}, u32[]{:S(2)}, u32[]{:S(2)}) collective-permute-start(bf16[72,1664]{1,0:T(8,128)(2,1)} %fusion.2), channel_id=1, source_target_pairs={{0,24},{1,25},{2,26},{3,27},{4,28},{5,29},{6,30},{7,31},{8,0},{9,1... | collective-permute-start | bytes 718856 | tf_op jit(solution)/shard_map/ppermute | solution.py:201
  18.7 2.8 %collective-permute-done.7 = bf16[72,1664]{1,0:T(8,128)(2,1)} collective-permute-done((bf16[72,1664]{1,0:T(8,128)(2,1)}, bf16[72,1664]{1,0:T(8,128)(2,1)}, u32[]{:S(2)}, u32[]{:S(2)}) %collective-permute-start.7) | collective-permute-done | bytes 239648 | tf_op jit(solution)/shard_map/ppermute | solution.py:201
  21.5 8.6 %collective-permute-start.30 = (f32[1,1,4,72]{3,2,1,0:T(4,128)S(1)}, f32[1,1,4,72]{3,2,1,0:T(4,128)S(1)}, u32[]{:S(2)}, u32[]{:S(2)}) collective-permute-start(f32[1,1,4,72]{3,2,1,0:T(4,128)S(1)} %maximum_add_fusion), channel_id=1, source_target_pairs={{0,8},{1,9},{2,10},{3,11},{4,12},{5,13},{6,14},{7,15},{8,16},{9,17... | collective-permute-start | bytes 3464 | tf_op jit(solution)/shard_map/ppermute | solution.py:201
  32.3 4.2 %collective-permute-done.8 = bf16[72,1664]{1,0:T(8,128)(2,1)S(1)} collective-permute-done((bf16[72,1664]{1,0:T(8,128)(2,1)}, bf16[72,1664]{1,0:T(8,128)(2,1)S(1)}, u32[]{:S(2)}, u32[]{:S(2)}) %collective-permute-start.8) | collective-permute-done | bytes 239648 | tf_op jit(solution)/shard_map/ppermute | solution.py:201
  42.6 1.6 %collective-permute-start.11 = (bf16[72,1664]{1,0:T(8,128)(2,1)S(1)}, bf16[72,1664]{1,0:T(8,128)(2,1)S(1)}, u32[]{:S(2)}, u32[]{:S(2)}) collective-permute-start(bf16[72,1664]{1,0:T(8,128)(2,1)S(1)} %collective-permute-done.5), channel_id=1, source_target_pairs={{0,4},{1,5},{2,3},{3,2},{4,0},{5,1},{6,7},{7,6},{8,12},{9,13},{10,... | collective-permute-start | bytes 718856 | tf_op jit(solution)/shard_map/ppermute | solution.py:201
  44.2 2.0 %collective-permute-done.10 = bf16[72,1664]{1,0:T(8,128)(2,1)S(1)} collective-permute-done((bf16[72,1664]{1,0:T(8,128)(2,1)S(1)}, bf16[72,1664]{1,0:T(8,128)(2,1)S(1)}, u32[]{:S(2)}, u32[]{:S(2)}) %collective-permute-start.10) | collective-permute-done | bytes 239648 | tf_op jit(solution)/shard_map/ppermute | solution.py:201
  50.9 1.6 %collective-permute-start.12 = (bf16[72,1664]{1,0:T(8,128)(2,1)S(1)}, bf16[72,1664]{1,0:T(8,128)(2,1)S(1)}, u32[]{:S(2)}, u32[]{:S(2)}) collective-permute-start(bf16[72,1664]{1,0:T(8,128)(2,1)S(1)} %collective-permute-done.6), channel_id=1, source_target_pairs={{0,4},{1,5},{2,3},{3,2},{4,0},{5,1},{6,7},{7,6},{8,12},{9,13},{10,... | collective-permute-start | bytes 718856 | tf_op jit(solution)/shard_map/ppermute | solution.py:201
  54.9 2.0 %collective-permute-start.31 = (f32[2,1,4,72]{3,2,1,0:T(4,128)S(1)}, f32[2,1,4,72]{3,2,1,0:T(4,128)S(1)}, u32[]{:S(2)}, u32[]{:S(2)}) collective-permute-start(f32[2,1,4,72]{3,2,1,0:T(4,128)S(1)} %constant_dynamic-update-slice_fusion), channel_id=1, source_target_pairs={{0,16},{1,17},{2,18},{3,19},{4,20},{5,21},{6,22},{7,23},{8,24},{9,... | collective-permute-start | bytes 6920 | tf_op jit(solution)/shard_map/ppermute | solution.py:201
  64.7 2.0 %collective-permute-start.17 = (bf16[144,1664]{1,0:T(8,128)(2,1)S(1)}, bf16[144,1664]{1,0:T(8,128)(2,1)S(1)}, u32[]{:S(2)}, u32[]{:S(2)}) collective-permute-start(bf16[144,1664]{1,0:T(8,128)(2,1)S(1)} %pad_maximum_fusion.13), channel_id=1, source_target_pairs={{0,1},{1,0},{2,6},{3,7},{4,5},{5,4},{6,2},{7,3},{8,9},{9,8},{10,14... | collective-permute-start | bytes 1437704 | tf_op jit(solution)/shard_map/ppermute | solution.py:201
  70.4 3.1 %collective-permute-done.17 = bf16[144,1664]{1,0:T(8,128)(2,1)S(1)} collective-permute-done((bf16[144,1664]{1,0:T(8,128)(2,1)S(1)}, bf16[144,1664]{1,0:T(8,128)(2,1)S(1)}, u32[]{:S(2)}, u32[]{:S(2)}) %collective-permute-start.17) | collective-permute-done | bytes 479264 | tf_op jit(solution)/shard_map/ppermute | solution.py:201
  75.1 1.5 %collective-permute-start.22 = (bf16[144,1664]{1,0:T(8,128)(2,1)S(1)}, bf16[144,1664]{1,0:T(8,128)(2,1)S(1)}, u32[]{:S(2)}, u32[]{:S(2)}) collective-permute-start(bf16[144,1664]{1,0:T(8,128)(2,1)S(1)} %pad_maximum_fusion.14), channel_id=1, source_target_pairs={{0,1},{1,0},{2,6},{3,7},{4,5},{5,4},{6,2},{7,3},{8,9},{9,8},{10,14... | collective-permute-start | bytes 1437704 | tf_op jit(solution)/shard_map/ppermute | solution.py:201
  83.1 2.0 %collective-permute-start.35 = (bf16[72,1664]{1,0:T(8,128)(2,1)}, bf16[72,1664]{1,0:T(8,128)(2,1)}, u32[]{:S(2)}, u32[]{:S(2)}) collective-permute-start(bf16[72,1664]{1,0:T(8,128)(2,1)} %add_convert_fusion.11), channel_id=1, source_target_pairs={{0,24},{1,25},{2,26},{3,27},{4,28},{5,29},{6,30},{7,31},{8,0},{9,1... | collective-permute-start | bytes 718856 | tf_op jit(solution)/shard_map/ppermute | solution.py:201
  88.7 5.6 %collective-permute-done.25 = bf16[72,1664]{1,0:T(8,128)(2,1)S(1)} collective-permute-done((bf16[72,1664]{1,0:T(8,128)(2,1)S(1)}, bf16[72,1664]{1,0:T(8,128)(2,1)S(1)}, u32[]{:S(2)}, u32[]{:S(2)}) %collective-permute-start.25) | collective-permute-done | bytes 239648 | tf_op jit(solution)/shard_map/ppermute | solution.py:201
  97.1 2.3 %collective-permute-start.27 = (bf16[144,1664]{1,0:T(8,128)(2,1)}, bf16[144,1664]{1,0:T(8,128)(2,1)}, u32[]{:S(2)}, u32[]{:S(2)}) collective-permute-start(bf16[144,1664]{1,0:T(8,128)(2,1)} %pad_maximum_fusion.16), channel_id=1, source_target_pairs={{0,1},{1,0},{2,6},{3,7},{4,5},{5,4},{6,2},{7,3},{8,9},{9,8},{10,14... | collective-permute-start | bytes 1437704 | tf_op jit(solution)/shard_map/ppermute | solution.py:201
  103.1 1.7 %broadcast_select_fusion = (bf16[1152,512]{1,0:T(8,128)(2,1)S(1)}, bf16[1152,512]{1,0:T(8,128)(2,1)S(1)}) fusion(bf16[1152,512]{1,0:T(8,128)(2,1)} %copy-done.3, pred[1152]{0:T(1024)(128)(4,1)S(1)} %convert_compare_fusion, bf16[1152,512]{1,0:T(8,128)(2,1)S(1)} %get-tuple-element.365), kind=kLoop, calls=%fused_computation.80 | loop fusion | flops 1179648 | bytes 4719744 | tf_op jit(solution)/shard_map/jit(_where)/select_n | solution.py:439
  105.6 3.6 %convolution_convert_fusion.1 = bf16[1664,512]{1,0:T(8,128)(2,1)} fusion(bf16[1152,1664]{1,0:T(8,128)(2,1)S(1)} %copy-done.11, bf16[1152,512]{1,0:T(8,128)(2,1)S(1)} %get-tuple-element.292), kind=kOutput, calls=%fused_computation.1 | convolution fusion | flops 1963786240 | bytes 6717440 | tf_op jit(solution)/shard_map/dot_general | solution.py:434
  112.1 1.6 %collective-permute-start.34 = (bf16[72,1664]{1,0:T(8,128)(2,1)S(1)}, bf16[72,1664]{1,0:T(8,128)(2,1)S(1)}, u32[]{:S(2)}, u32[]{:S(2)}) collective-permute-start(bf16[72,1664]{1,0:T(8,128)(2,1)S(1)} %add_convert_fusion.6), channel_id=1, source_target_pairs={{0,4},{1,5},{2,3},{3,2},{4,0},{5,1},{6,7},{7,6},{8,12},{9,13},{10,... | collective-permute-start | bytes 718856 | tf_op jit(solution)/shard_map/ppermute | solution.py:201
  113.7 3.8 %convolution_convert_fusion = bf16[512,1664]{1,0:T(8,128)(2,1)} fusion(bf16[1152,512]{1,0:T(8,128)(2,1)S(1)} %get-tuple-element.151, bf16[1152,1664]{1,0:T(8,128)(2,1)S(1)} %copy-done.9), kind=kOutput, calls=%fused_computation | convolution fusion | flops 1963786240 | bytes 6717440 | tf_op jit(solution)/shard_map/dot_general | solution.py:440
  119.4 2.2 %collective-permute-done.36 = bf16[72,1664]{1,0:T(8,128)(2,1)S(1)} collective-permute-done((bf16[72,1664]{1,0:T(8,128)(2,1)S(1)}, bf16[72,1664]{1,0:T(8,128)(2,1)S(1)}, u32[]{:S(2)}, u32[]{:S(2)}) %collective-permute-start.36) | collective-permute-done | bytes 239648 | tf_op jit(solution)/shard_map/ppermute | solution.py:201
  121.6 1.7 %fusion.150 = f32[1664,128]{1,0:T(8,128)S(1)} fusion(bf16[72,1664]{1,0:T(8,128)(2,1)} %collective-permute-done.37, bf16[72,1664]{1,0:T(8,128)(2,1)S(1)} %collective-permute-done.36, bf16[72,1664]{1,0:T(8,128)(2,1)} %collective-permute-done.35, bf16[72,1664]{1,0:T(8,128)(2,1)S(1)} %add_convert_fusion.5, pred[72,128]{1,0:T(8,128)(4,1)S(1)} %get-tuple-element.321, ...), kind=kOutput, calls=%fused_computation.262 | convolution fusion | flops 126627840 | bytes 1847296 | tf_op jit(solution)/shard_map/dot_general | solution.py:457
  123.3 1.7 %fusion.100 = (f32[128]{0:T(128)S(1)}, f32[128]{0:T(128)S(1)}, bf16[1664,128]{1,0:T(8,128)(2,1)S(1)}) fusion(bf16[128,1664]{0,1:T(8,128)(2,1)S(1)} %copy-done.7, f32[1664,128]{1,0:T(8,128)S(1)} %fusion.150, f32[128]{0:T(128)S(1)} %get-tuple-element.310, f32[128]{0:T(128)S(1)} %get-tuple-element.309, pred[72,128]{1,0:T(8,128)(4,1)S(1)} %get-tuple-element.322, ...), kind=kOutput, calls=%fused_computation.114 | convolution fusion | flops 128544512 | bytes 2701312 | tf_op jit(solution)/shard_map/dot_general | solution.py:457
  126.2 5.5 %collective-permute-done.38 = bf16[848,128]{1,0:T(8,128)(2,1)S(1)} collective-permute-done((bf16[848,128]{1,0:T(8,128)(2,1)S(1)}, bf16[848,128]{1,0:T(8,128)(2,1)S(1)}, u32[]{:S(2)}, u32[]{:S(2)}) %collective-permute-start.38) | collective-permute-done | bytes 217120 | tf_op jit(solution)/shard_map/ppermute | solution.py:473
  (227 shorter events, 63.6 us)
Async XLA Ops:
  6.1 11.0 %collective-permute-start = (bf16[72,1664]{1,0:T(8,128)(2,1)S(1)}, bf16[72,1664]{1,0:T(8,128)(2,1)S(1)}, u32[]{:S(2)}, u32[]{:S(2)}) collective-permute-start(bf16[72,1664]{1,0:T(8,128)(2,1)S(1)} %fusion.1), channel_id=1, source_target_pairs={{0,1},{1,0},{2,6},{3,7},{4,5},{5,4},{6,2},{7,3},{8,9},{9,8},{10,14... | collective-permute-start | bytes 718856 | tf_op jit(solution)/shard_map/ppermute | solution.py:201
  9.1 21.1 %collective-permute-start.1 = (bf16[72,1664]{1,0:T(8,128)(2,1)S(1)}, bf16[72,1664]{1,0:T(8,128)(2,1)S(1)}, u32[]{:S(2)}, u32[]{:S(2)}) collective-permute-start(bf16[72,1664]{1,0:T(8,128)(2,1)S(1)} %fusion.1), channel_id=1, source_target_pairs={{0,4},{1,5},{2,3},{3,2},{4,0},{5,1},{6,7},{7,6},{8,12},{9,13},{10,... | collective-permute-start | bytes 718856 | tf_op jit(solution)/shard_map/ppermute | solution.py:201
  10.6 10.9 %collective-permute-start.7 = (bf16[72,1664]{1,0:T(8,128)(2,1)}, bf16[72,1664]{1,0:T(8,128)(2,1)}, u32[]{:S(2)}, u32[]{:S(2)}) collective-permute-start(bf16[72,1664]{1,0:T(8,128)(2,1)} %fusion), channel_id=1, source_target_pairs={{0,8},{1,9},{2,10},{3,11},{4,12},{5,13},{6,14},{7,15},{8,16},{9,17... | collective-permute-start | bytes 718856 | tf_op jit(solution)/shard_map/ppermute | solution.py:201
  13.1 25.0 %collective-permute-start.5 = (bf16[72,1664]{1,0:T(8,128)(2,1)}, bf16[72,1664]{1,0:T(8,128)(2,1)S(1)}, u32[]{:S(2)}, u32[]{:S(2)}) collective-permute-start(bf16[72,1664]{1,0:T(8,128)(2,1)} %fusion.2), channel_id=1, source_target_pairs={{0,24},{1,25},{2,26},{3,27},{4,28},{5,29},{6,30},{7,31},{8,0},{9,1... | collective-permute-start | bytes 718856 | tf_op jit(solution)/shard_map/ppermute | solution.py:201
  16.2 31.2 %collective-permute-start.18 = (bf16[72,1664]{1,0:T(8,128)(2,1)}, bf16[72,1664]{1,0:T(8,128)(2,1)S(1)}, u32[]{:S(2)}, u32[]{:S(2)}) collective-permute-start(bf16[72,1664]{1,0:T(8,128)(2,1)} %fusion.3), channel_id=1, source_target_pairs={{0,16},{1,17},{2,18},{3,19},{4,20},{5,21},{6,22},{7,23},{8,24},{9,... | collective-permute-start | bytes 718856 | tf_op jit(solution)/shard_map/ppermute | solution.py:201
  17.1 13.6 %collective-permute-start.2 = (bf16[72,1664]{1,0:T(8,128)(2,1)S(1)}, bf16[72,1664]{1,0:T(8,128)(2,1)}, u32[]{:S(2)}, u32[]{:S(2)}) collective-permute-start(bf16[72,1664]{1,0:T(8,128)(2,1)S(1)} %collective-permute-done), channel_id=1, source_target_pairs={{0,4},{1,5},{2,3},{3,2},{4,0},{5,1},{6,7},{7,6},{8,12},{9,13},{10,... | collective-permute-start | bytes 718856 | tf_op jit(solution)/shard_map/ppermute | solution.py:201
  21.5 26.0 %collective-permute-start.30 = (f32[1,1,4,72]{3,2,1,0:T(4,128)S(1)}, f32[1,1,4,72]{3,2,1,0:T(4,128)S(1)}, u32[]{:S(2)}, u32[]{:S(2)}) collective-permute-start(f32[1,1,4,72]{3,2,1,0:T(4,128)S(1)} %maximum_add_fusion), channel_id=1, source_target_pairs={{0,8},{1,9},{2,10},{3,11},{4,12},{5,13},{6,14},{7,15},{8,16},{9,17... | collective-permute-start | bytes 3464 | tf_op jit(solution)/shard_map/ppermute | solution.py:201
  30.7 11.9 %collective-permute-start.9 = (bf16[72,1664]{1,0:T(8,128)(2,1)}, bf16[72,1664]{1,0:T(8,128)(2,1)S(1)}, u32[]{:S(2)}, u32[]{:S(2)}) collective-permute-start(bf16[72,1664]{1,0:T(8,128)(2,1)} %collective-permute-done.7), channel_id=1, source_target_pairs={{0,4},{1,5},{2,3},{3,2},{4,0},{5,1},{6,7},{7,6},{8,12},{9,13},{10,... | collective-permute-start | bytes 718856 | tf_op jit(solution)/shard_map/ppermute | solution.py:201
  39.6 10.9 %collective-permute-start.6 = (bf16[72,1664]{1,0:T(8,128)(2,1)S(1)}, bf16[72,1664]{1,0:T(8,128)(2,1)S(1)}, u32[]{:S(2)}, u32[]{:S(2)}) collective-permute-start(bf16[72,1664]{1,0:T(8,128)(2,1)S(1)} %collective-permute-done.5), channel_id=1, source_target_pairs={{0,1},{1,0},{2,6},{3,7},{4,5},{5,4},{6,2},{7,3},{8,9},{9,8},{10,14... | collective-permute-start | bytes 718856 | tf_op jit(solution)/shard_map/ppermute | solution.py:201
  42.6 12.3 %collective-permute-start.11 = (bf16[72,1664]{1,0:T(8,128)(2,1)S(1)}, bf16[72,1664]{1,0:T(8,128)(2,1)S(1)}, u32[]{:S(2)}, u32[]{:S(2)}) collective-permute-start(bf16[72,1664]{1,0:T(8,128)(2,1)S(1)} %collective-permute-done.5), channel_id=1, source_target_pairs={{0,4},{1,5},{2,3},{3,2},{4,0},{5,1},{6,7},{7,6},{8,12},{9,13},{10,... | collective-permute-start | bytes 718856 | tf_op jit(solution)/shard_map/ppermute | solution.py:201
  47.4 12.1 %collective-permute-start.19 = (bf16[72,1664]{1,0:T(8,128)(2,1)S(1)}, bf16[72,1664]{1,0:T(8,128)(2,1)S(1)}, u32[]{:S(2)}, u32[]{:S(2)}) collective-permute-start(bf16[72,1664]{1,0:T(8,128)(2,1)S(1)} %collective-permute-done.18), channel_id=1, source_target_pairs={{0,1},{1,0},{2,6},{3,7},{4,5},{5,4},{6,2},{7,3},{8,9},{9,8},{10,14... | collective-permute-start | bytes 718856 | tf_op jit(solution)/shard_map/ppermute | solution.py:201
  47.5 21.7 %collective-permute-start.20 = (bf16[72,1664]{1,0:T(8,128)(2,1)S(1)}, bf16[72,1664]{1,0:T(8,128)(2,1)S(1)}, u32[]{:S(2)}, u32[]{:S(2)}) collective-permute-start(bf16[72,1664]{1,0:T(8,128)(2,1)S(1)} %collective-permute-done.18), channel_id=1, source_target_pairs={{0,4},{1,5},{2,3},{3,2},{4,0},{5,1},{6,7},{7,6},{8,12},{9,13},{10,... | collective-permute-start | bytes 718856 | tf_op jit(solution)/shard_map/ppermute | solution.py:201
  50.5 44.6 %collective-permute-start.4 = (bf16[288,1664]{1,0:T(8,128)(2,1)S(1)}, bf16[288,1664]{1,0:T(8,128)(2,1)S(1)}, u32[]{:S(2)}, u32[]{:S(2)}) collective-permute-start(bf16[288,1664]{1,0:T(8,128)(2,1)S(1)} %pad_maximum_fusion.2), channel_id=1, source_target_pairs={{0,2},{1,3},{2,0},{3,1},{4,6},{5,7},{6,4},{7,5},{8,10},{9,11},{10,... | collective-permute-start | bytes 2875400 | tf_op jit(solution)/shard_map/ppermute | solution.py:201
  59.5 17.1 %collective-permute-start.32 = (f32[4,1,4,72]{3,2,1,0:T(4,128)S(1)}, f32[4,1,4,72]{3,2,1,0:T(4,128)S(1)}, u32[]{:S(2)}, u32[]{:S(2)}) collective-permute-start(f32[4,1,4,72]{3,2,1,0:T(4,128)S(1)} %constant_dynamic-update-slice_fusion.2), channel_id=1, source_target_pairs={{0,4},{1,5},{2,6},{3,7},{4,0},{5,1},{6,2},{7,3},{8,12},{9,13},{10,... | collective-permute-start | bytes 13832 | tf_op jit(solution)/shard_map/ppermute | solution.py:201
  64.7 8.8 %collective-permute-start.17 = (bf16[144,1664]{1,0:T(8,128)(2,1)S(1)}, bf16[144,1664]{1,0:T(8,128)(2,1)S(1)}, u32[]{:S(2)}, u32[]{:S(2)}) collective-permute-start(bf16[144,1664]{1,0:T(8,128)(2,1)S(1)} %pad_maximum_fusion.13), channel_id=1, source_target_pairs={{0,1},{1,0},{2,6},{3,7},{4,5},{5,4},{6,2},{7,3},{8,9},{9,8},{10,14... | collective-permute-start | bytes 1437704 | tf_op jit(solution)/shard_map/ppermute | solution.py:201
  69.6 9.6 %collective-permute-start.24 = (bf16[288,1664]{1,0:T(8,128)(2,1)S(1)}, bf16[288,1664]{1,0:T(8,128)(2,1)S(1)}, u32[]{:S(2)}, u32[]{:S(2)}) collective-permute-start(bf16[288,1664]{1,0:T(8,128)(2,1)S(1)} %pad_maximum_fusion.9), channel_id=1, source_target_pairs={{0,2},{1,3},{2,0},{3,1},{4,6},{5,7},{6,4},{7,5},{8,10},{9,11},{10,... | collective-permute-start | bytes 2875400 | tf_op jit(solution)/shard_map/ppermute | solution.py:201
  75.1 10.3 %collective-permute-start.22 = (bf16[144,1664]{1,0:T(8,128)(2,1)S(1)}, bf16[144,1664]{1,0:T(8,128)(2,1)S(1)}, u32[]{:S(2)}, u32[]{:S(2)}) collective-permute-start(bf16[144,1664]{1,0:T(8,128)(2,1)S(1)} %pad_maximum_fusion.14), channel_id=1, source_target_pairs={{0,1},{1,0},{2,6},{3,7},{4,5},{5,4},{6,2},{7,3},{8,9},{9,8},{10,14... | collective-permute-start | bytes 1437704 | tf_op jit(solution)/shard_map/ppermute | solution.py:201
  76.6 23.6 %collective-permute-start.33 = (f32[4,2,4,72]{3,2,1,0:T(4,128)S(1)}, f32[4,2,4,72]{3,2,1,0:T(4,128)S(1)}, u32[]{:S(2)}, u32[]{:S(2)}) collective-permute-start(f32[4,2,4,72]{3,2,1,0:T(4,128)S(1)} %constant_dynamic-update-slice_fusion.4), channel_id=1, source_target_pairs={{0,2},{1,3},{2,0},{3,1},{4,6},{5,7},{6,4},{7,5},{8,10},{9,11},{10,... | collective-permute-start | bytes 27656 | tf_op jit(solution)/shard_map/ppermute | solution.py:201
  83.1 36.2 %collective-permute-start.35 = (bf16[72,1664]{1,0:T(8,128)(2,1)}, bf16[72,1664]{1,0:T(8,128)(2,1)}, u32[]{:S(2)}, u32[]{:S(2)}) collective-permute-start(bf16[72,1664]{1,0:T(8,128)(2,1)} %add_convert_fusion.11), channel_id=1, source_target_pairs={{0,24},{1,25},{2,26},{3,27},{4,28},{5,29},{6,30},{7,31},{8,0},{9,1... | collective-permute-start | bytes 718856 | tf_op jit(solution)/shard_map/ppermute | solution.py:201
  85.5 8.8 %collective-permute-start.25 = (bf16[72,1664]{1,0:T(8,128)(2,1)S(1)}, bf16[72,1664]{1,0:T(8,128)(2,1)S(1)}, u32[]{:S(2)}, u32[]{:S(2)}) collective-permute-start(bf16[72,1664]{1,0:T(8,128)(2,1)S(1)} %add_convert_fusion.10), channel_id=1, source_target_pairs={{0,4},{1,5},{2,3},{3,2},{4,0},{5,1},{6,7},{7,6},{8,12},{9,13},{10,... | collective-permute-start | bytes 718856 | tf_op jit(solution)/shard_map/ppermute | solution.py:201
  87.4 12.1 %collective-permute-start.28 = (bf16[144,1664]{1,0:T(8,128)(2,1)S(1)}, bf16[144,1664]{1,0:T(8,128)(2,1)S(1)}, u32[]{:S(2)}, u32[]{:S(2)}) collective-permute-start(bf16[144,1664]{1,0:T(8,128)(2,1)S(1)} %pad_maximum_fusion.15), channel_id=1, source_target_pairs={{0,1},{1,0},{2,6},{3,7},{4,5},{5,4},{6,2},{7,3},{8,9},{9,8},{10,14... | collective-permute-start | bytes 1437704 | tf_op jit(solution)/shard_map/ppermute | solution.py:201
  95.1 24.3 %collective-permute-start.37 = (bf16[72,1664]{1,0:T(8,128)(2,1)}, bf16[72,1664]{1,0:T(8,128)(2,1)}, u32[]{:S(2)}, u32[]{:S(2)}) collective-permute-start(bf16[72,1664]{1,0:T(8,128)(2,1)} %add_convert_fusion.9), channel_id=1, source_target_pairs={{0,8},{1,9},{2,10},{3,11},{4,12},{5,13},{6,14},{7,15},{8,16},{9,17... | collective-permute-start | bytes 718856 | tf_op jit(solution)/shard_map/ppermute | solution.py:201
  97.1 14.0 %collective-permute-start.27 = (bf16[144,1664]{1,0:T(8,128)(2,1)}, bf16[144,1664]{1,0:T(8,128)(2,1)}, u32[]{:S(2)}, u32[]{:S(2)}) collective-permute-start(bf16[144,1664]{1,0:T(8,128)(2,1)} %pad_maximum_fusion.16), channel_id=1, source_target_pairs={{0,1},{1,0},{2,6},{3,7},{4,5},{5,4},{6,2},{7,3},{8,9},{9,8},{10,14... | collective-permute-start | bytes 1437704 | tf_op jit(solution)/shard_map/ppermute | solution.py:201
  110.3 11.2 %collective-permute-start.36 = (bf16[72,1664]{1,0:T(8,128)(2,1)S(1)}, bf16[72,1664]{1,0:T(8,128)(2,1)S(1)}, u32[]{:S(2)}, u32[]{:S(2)}) collective-permute-start(bf16[72,1664]{1,0:T(8,128)(2,1)S(1)} %add_convert_fusion.7), channel_id=1, source_target_pairs={{0,16},{1,17},{2,18},{3,19},{4,20},{5,21},{6,22},{7,23},{8,24},{9,... | collective-permute-start | bytes 718856 | tf_op jit(solution)/shard_map/ppermute | solution.py:201
  (29 other events, 216.3 us)

commit v3 on v0

--- a/solution.py
+++ b/solution.py
@@ -1,8 +1,11 @@
+import functools
 import math
 
 import jax
 import jax.numpy as jnp
 from jax import lax
+from jax.experimental import pallas as pl
+from jax.experimental.pallas import tpu as pltpu
 from jax.sharding import PartitionSpec as P
 
 HBLK = 4
@@ -15,7 +18,7 @@
     return (hidden_pre * normal_cdf, normal_cdf + hidden_pre * density)
 
 
-def body(tokens, expert_ids, priority, gate_values, weight_in, weight_out, cotangent):
+def general_body(tokens, expert_ids, priority, gate_values, weight_in, weight_out, cotangent):
     token_count = tokens.shape[0]
     dp_count = lax.axis_size("dp")
     experts = dp_count // HBLK
@@ -127,6 +130,525 @@
     )
 
 
+GROUPS = ((0,), (1,), (3,), (2,))
+MIB = 1024 * 1024
+WLIM = 56
+PLAN = (
+    "Z 1",
+    "D1 0",
+    "Z 3",
+    "Z 2",
+    "D2 0",
+    "D1 1",
+    "SEL 0",
+    "D2 1",
+    "D1 2",
+    "SEL 1",
+    "D2 2",
+    "D1 3",
+    "D2 3",
+    "SEL 2",
+    "SEL 3",
+    "E 1",
+    "E 0 E1",
+    "E 2 E0",
+    "R1 1 E2",
+    "E 3 R11",
+    "CUT 0",
+    "R1 2 E3",
+    "R2 1 R12",
+    "R1 3 R21",
+    "R2 2 R13",
+    "H 1 R22",
+    "R1 0 H1",
+    "R2 3 R10",
+    "H 2 R23",
+    "R2 0 H2",
+    "H 3 R20",
+    "W 0 H3",
+    "H 0 W0",
+)
+
+
+def expert_kernel(near, far, matrix_in, matrix_out, near_parts, far_parts, act, pre):
+    half = near.shape[0] // 2
+    rows = jnp.concatenate([near[:half], far[:half]], axis=0)
+    grads = jnp.concatenate([near[half:], far[half:]], axis=0)
+    hidden_pre = jnp.dot(rows, matrix_in[...], preferred_element_type=jnp.float32)
+    activation, slope = gelu_parts(hidden_pre)
+    grad_act = lax.dot_general(
+        grads, matrix_out[...], (((1,), (1,)), ((), ())), preferred_element_type=jnp.float32
+    )
+    act[...] = activation.astype(jnp.bfloat16)
+    pre[...] = (grad_act * slope).astype(jnp.bfloat16)
+    out = jnp.dot(act[...], matrix_out[...], preferred_element_type=jnp.float32)
+    near_parts[:half] = out[:half].astype(jnp.bfloat16)
+    far_parts[:half] = out[half:].astype(jnp.bfloat16)
+    back = lax.dot_general(
+        pre[...], matrix_in[...], (((1,), (1,)), ((), ())), preferred_element_type=jnp.float32
+    )
+    near_parts[half:] = back[:half].astype(jnp.bfloat16)
+    far_parts[half:] = back[half:].astype(jnp.bfloat16)
+
+
+def expert_call(near, far, matrix_in, matrix_out):
+    rows, width = near.shape
+    hidden = matrix_in.shape[1]
+    vmem = pl.BlockSpec(memory_space=pltpu.VMEM)
+    return pl.pallas_call(
+        expert_kernel,
+        out_shape=(
+            jax.ShapeDtypeStruct((rows, width), jnp.bfloat16),
+            jax.ShapeDtypeStruct((rows, width), jnp.bfloat16),
+            jax.ShapeDtypeStruct((rows, hidden), jnp.bfloat16),
+            jax.ShapeDtypeStruct((rows, hidden), jnp.bfloat16),
+        ),
+        in_specs=[vmem] * 4,
+        out_specs=(vmem,) * 4,
+        compiler_params=pltpu.CompilerParams(vmem_limit_bytes=16 * MIB),
+        cost_estimate=pl.CostEstimate(flops=0, bytes_accessed=0, transcendentals=0),
+    )(near, far, matrix_in, matrix_out)
+
+
+def start_kernel(experts, ids_at, priority_at, gates_at, tokens_at, cotangent_at, places, *rest):
+    blocks, (ids, priority, gates, source, sems) = rest[:experts], rest[experts:]
+    slot_count, block_rows = places.shape[2], blocks[0].shape[0]
+    token_count = source.shape[0]
+    place_dp = lax.axis_index("dp")
+    first_half = lax.axis_index("rep") == 0
+    small = [
+        pltpu.make_async_copy(whole, held, sems.at[i])
+        for i, (whole, held) in enumerate(((ids_at, ids), (priority_at, priority), (gates_at, gates)))
+    ]
+    for copy in small:
+        copy.start()
+
+    @pl.when(first_half)
+    def _():
+        pltpu.make_async_copy(tokens_at, source, sems.at[3]).start()
+
+    @pl.when(jnp.logical_not(first_half))
+    def _():
+        pltpu.make_async_copy(cotangent_at, source, sems.at[3]).start()
+
+    for copy in small:
+        copy.wait()
+    row = lax.broadcasted_iota(jnp.int32, (experts, 1), 0)
+    near = lax.rem(place_dp // HBLK + row, experts)
+    chosen = [ids[j : j + 1] == near for j in range(2)]
+    chosen_any = chosen[0] | chosen[1]
+    early = lax.broadcasted_iota(jnp.int32, (token_count, token_count), 0)
+    late = lax.broadcasted_iota(jnp.int32, (token_count, token_count), 1)
+    rank = jnp.dot(
+        chosen_any.astype(jnp.bfloat16),
+        (early < late).astype(jnp.bfloat16),
+        preferred_element_type=jnp.float32,
+    ).astype(jnp.int32)
+    rank = jnp.where(chosen_any, rank, -1)
+    near_gate = jnp.where(chosen[0], gates[0:1], gates[1:2])
+    slots = lax.broadcasted_iota(jnp.int32, (slot_count, token_count), 0)
+    pltpu.make_async_copy(tokens_at, source, sems.at[3]).wait()
+    for k in range(experts):
+        spread = rank[k : k + 1] == slots
+        rows = jnp.dot(spread.astype(jnp.bfloat16), source[...], preferred_element_type=jnp.float32)
+        slot_gate = jnp.sum(jnp.where(spread, near_gate[k : k + 1], 0.0), axis=1, keepdims=True)
+        key = 1 + priority[...] + jnp.where(chosen[0][k : k + 1], PRIO, 0)
+        slot_key = lax.dot_general(
+            key.astype(jnp.bfloat16),
+            spread.astype(jnp.bfloat16),
+            (((1,), (1,)), ((), ())),
+            preferred_element_type=jnp.float32,
+        )
+        whole = (rows * jnp.where(first_half, 1.0, slot_gate)).astype(jnp.bfloat16)
+        spare = jnp.zeros((block_rows - slot_count, rows.shape[1]), jnp.bfloat16)
+        blocks[k][...] = jnp.concatenate([whole, spare], axis=0)
+        blocks[k][slot_count : slot_count + 1, :slot_count] = slot_key.astype(jnp.bfloat16)
+        for j in range(2):
+            places[j, k] = (spread & chosen[j][k : k + 1]).astype(jnp.bfloat16)
+
+
+def start_call(ids, priority, gates, tokens, cotangent, experts, slot_count):
+    token_count, width = tokens.shape
+    block_rows = (slot_count + 1 + 15) // 16 * 16
+    vmem = pl.BlockSpec(memory_space=pltpu.VMEM)
+    return pl.pallas_call(
+        functools.partial(start_kernel, experts),
+        out_shape=(
+            jax.ShapeDtypeStruct((2, experts, slot_count, token_count), jnp.bfloat16),
+        )
+        + (jax.ShapeDtypeStruct((block_rows, width), jnp.bfloat16),) * experts,
+        in_specs=[pl.BlockSpec(memory_space=pl.ANY)] * 5,
+        out_specs=(vmem,) * (1 + experts),
+        scratch_shapes=[
+            pltpu.VMEM(ids.shape, jnp.int32),
+            pltpu.VMEM(priority.shape, jnp.int32),
+            pltpu.VMEM(gates.shape, jnp.float32),
+            pltpu.VMEM(tokens.shape, jnp.bfloat16),
+            pltpu.SemaphoreType.DMA((4,)),
+        ],
+        compiler_params=pltpu.CompilerParams(vmem_limit_bytes=56 * MIB),
+        cost_estimate=pl.CostEstimate(flops=0, bytes_accessed=0, transcendentals=0),
+    )(ids, priority, gates, tokens, cotangent)
+
+
+def cut_kernel(slot_count, block_rows, capacity, *refs):
+    group_count = len(refs) // 2 - 2
+    pieces, (kept, mine, keys, sems) = refs[: 2 * group_count], refs[2 * group_count :]
+    copies, at = [], 0
+    for piece in pieces:
+        for block in range(piece.shape[0] // 2 // block_rows):
+            last = pl.ds((block + 1) * block_rows - 16, 16)
+            copies.append(
+                pltpu.make_async_copy(piece.at[last, pl.ds(0, 128)], keys.at[at], sems.at[at])
+            )
+            at += 1
+    for copy in copies:
+        copy.start()
+    for copy in copies:
+        copy.wait()
+    row = slot_count - (block_rows - 16)
+    rows = [keys[i, row : row + 1, :slot_count].astype(jnp.float32) - 1.0 for i in range(at)]
+    levels = lax.broadcasted_iota(jnp.int32, (2 * PRIO, 1), 0).astype(jnp.float32)
+    above = sum((one >= levels).astype(jnp.float32) for one in rows)
+    above = jnp.sum(above, axis=1, keepdims=True)
+    cutoff = jnp.sum((above > capacity).astype(jnp.float32), axis=0, keepdims=True)
+    diagonal = lax.broadcasted_iota(
+        jnp.int32, (block_rows, slot_count), 0
+    ) == lax.broadcasted_iota(jnp.int32, (block_rows, slot_count), 1)
+    for i, one in enumerate(rows):
+        inside = jnp.where(diagonal & (one >= cutoff), 1.0, 0.0)
+        column = jnp.sum(inside, axis=1, keepdims=True)
+        kept[i * block_rows : (i + 1) * block_rows] = jnp.broadcast_to(column, (block_rows, 128)).astype(jnp.bfloat16)
+        if i % (at // group_count) == 0:
+            g = i // (at // group_count)
+            mine[g] = jnp.broadcast_to(column, (block_rows, 128))
+
+
+def cut_call(pieces, slot_count, block_rows, capacity):
+    total = sum(piece.shape[0] // 2 for piece in pieces)
+    vmem = pl.BlockSpec(memory_space=pltpu.VMEM)
+    return pl.pallas_call(
+        functools.partial(cut_kernel, slot_count, block_rows, capacity),
+        out_shape=(
+            jax.ShapeDtypeStruct((total, 128), jnp.bfloat16),
+            jax.ShapeDtypeStruct((len(pieces) // 2, block_rows, 128), jnp.float32),
+        ),
+        in_specs=[pl.BlockSpec(memory_space=pl.ANY)] * len(pieces),
+        out_specs=(vmem,) * 2,
+        scratch_shapes=[
+            pltpu.VMEM((total // block_rows, 16, 128), jnp.bfloat16),
+            pltpu.SemaphoreType.DMA((total // block_rows,)),
+        ],
+        compiler_params=pltpu.CompilerParams(vmem_limit_bytes=8 * MIB),
+        cost_estimate=pl.CostEstimate(flops=0, bytes_accessed=0, transcendentals=0),
+    )(*pieces)
+
+
+def weight_kernel(kept, *refs):
+    group_count = (len(refs) - 4) // 6
+    parts, hiddens = refs[: 4 * group_count], refs[4 * group_count : 6 * group_count]
+    grad_in, grad_out, act, pre = refs[6 * group_count :]
+
+    @pl.when(pl.program_id(0) == 0)
+    def _():
+        keep = kept[:, 0:1]
+        act[...] = jnp.concatenate([one[...] for one in hiddens[::2]], axis=0) * keep
+        pre[...] = jnp.concatenate([one[...] for one in hiddens[1::2]], axis=0) * keep
+
+    contract_first = (((0,), (0,)), ((), ()))
+    rows = jnp.concatenate([one[...] for one in parts[::2]], axis=0)
+    grads = jnp.concatenate([one[...] for one in parts[1::2]], axis=0)
+    grad_in[...] = lax.dot_general(
+        rows, pre[...], contract_first, preferred_element_type=jnp.float32
+    ).astype(jnp.bfloat16)
+    grad_out[...] = lax.dot_general(
+        act[...], grads, contract_first, preferred_element_type=jnp.float32
+    ).astype(jnp.bfloat16)
+
+
+def weight_call(kept, saved):
+    width, hidden = saved[0][0].shape[1], saved[0][2].shape[1]
+    all_rows = sum(one[2].shape[0] for one in saved)
+    tile = 256
+    operands, specs = [], []
+    for near, far, _, _ in saved:
+        for whole in (near, far):
+            for kind in range(2):
+                operands.append(whole)
+                specs.append(
+                    pl.BlockSpec((whole.shape[0] // 2, tile), functools.partial(lambda kind, j: (kind, j), kind))
+                )
+    for _, _, act, pre in saved:
+        for whole in (act, pre):
+            operands.append(whole)
+            specs.append(pl.BlockSpec(whole.shape, lambda j: (0, 0)))
+    return pl.pallas_call(
+        weight_kernel,
+        grid=(pl.cdiv(width, tile),),
+        out_shape=(
+            jax.ShapeDtypeStruct((width, hidden), jnp.bfloat16),
+            jax.ShapeDtypeStruct((hidden, width), jnp.bfloat16),
+        ),
+        in_specs=[pl.BlockSpec(kept.shape, lambda j: (0, 0))] + specs,
+        out_specs=(
+            pl.BlockSpec((tile, hidden), lambda j: (j, 0)),
+            pl.BlockSpec((hidden, tile), lambda j: (0, j)),
+        ),
+        scratch_shapes=[pltpu.VMEM((all_rows, hidden), jnp.bfloat16)] * 2,
+        compiler_params=pltpu.CompilerParams(vmem_limit_bytes=WLIM * MIB),
+        cost_estimate=pl.CostEstimate(flops=0, bytes_accessed=0, transcendentals=0),
+    )(kept, *operands)
+
+
+def token_kernel(gates, places, cotangent, *refs):
+    homes, (away, stay, gate_grad) = refs[:-3], refs[-3:]
+    first_half = lax.axis_index("rep") == 0
+    token_count, width = cotangent.shape
+    half = width // 2
+    diagonal = lax.broadcasted_iota(
+        jnp.int32, (token_count, token_count), 0
+    ) == lax.broadcasted_iota(jnp.int32, (token_count, token_count), 1)
+    back = jnp.concatenate([one[...] for one in homes], axis=0)
+    mixed, sums = 0.0, []
+    for j in range(2):
+        picker = jnp.concatenate([places[j, k] for k in range(len(homes))], axis=0)
+        picked = lax.dot_general(
+            picker, back, (((0,), (0,)), ((), ())), preferred_element_type=jnp.float32
+        )
+        gate = jnp.sum(jnp.where(diagonal, gates[j : j + 1], 0.0), axis=1, keepdims=True)
+        mixed = mixed + picked * jnp.where(first_half, gate, 1.0)
+        inner = jnp.sum(picked * cotangent[...].astype(jnp.float32), axis=1, keepdims=True)
+        sums.append(jnp.sum(jnp.where(diagonal, inner, 0.0), axis=0, keepdims=True))
+    mixed = mixed.astype(jnp.bfloat16).T
+    upper, lower = mixed[:half], mixed[half:]
+    away[:half] = jnp.where(first_half, lower, upper)
+    stay[...] = jnp.where(first_half, upper, lower)
+    left = jnp.concatenate(sums, axis=0)
+    gate_grad[...] = left
+    terms = []
+    for _ in range(3):
+        terms.append(left.astype(jnp.bfloat16))
+        left = left - terms[-1].astype(jnp.float32)
+    terms.append(jnp.zeros((away.shape[0] - half - 6, token_count), jnp.bfloat16))
+    away[half:] = jnp.concatenate(terms, axis=0)
+
+
+def token_call(gates, places, cotangent, homes):
+    token_count, width = cotangent.shape
+    vmem = pl.BlockSpec(memory_space=pltpu.VMEM)
+    return pl.pallas_call(
+        token_kernel,
+        out_shape=(
+            jax.ShapeDtypeStruct((width // 2 + 16, token_count), jnp.bfloat16),
+            jax.ShapeDtypeStruct((width // 2, token_count), jnp.bfloat16),
+            jax.ShapeDtypeStruct((2, token_count), jnp.float32),
+        ),
+        in_specs=[vmem] * (3 + len(homes)),
+        out_specs=(vmem,) * 3,
+        compiler_params=pltpu.CompilerParams(vmem_limit_bytes=16 * MIB),
+        cost_estimate=pl.CostEstimate(flops=0, bytes_accessed=0, transcendentals=0),
+    )(gates, places, cotangent, *homes)
+
+
+def end_kernel(stay, got, gate_grad, output, grad_tokens, grad_gates):
+    first_half = lax.axis_index("rep") == 0
+    half = stay.shape[0]
+    mine, theirs = stay[...], got[:half]
+    output[...] = jnp.where(first_half, mine, theirs)
+    grad_tokens[...] = jnp.where(first_half, theirs, mine)
+    terms = got[half:].astype(jnp.float32)
+    got_gate = terms[0:2] + terms[2:4] + terms[4:6]
+    rows_half = gate_grad.shape[1] // 2
+    grad_gates[...] = jnp.where(first_half, gate_grad[:, :rows_half], got_gate[:, rows_half:])
+
+
+def end_call(stay, got, gate_grad):
+    half, token_count = stay.shape
+    vmem = pl.BlockSpec(memory_space=pltpu.VMEM)
+    return pl.pallas_call(
+        end_kernel,
+        out_shape=(
+            jax.ShapeDtypeStruct((half, token_count), jnp.bfloat16),
+            jax.ShapeDtypeStruct((half, token_count), jnp.bfloat16),
+            jax.ShapeDtypeStruct((2, token_count // 2), jnp.float32),
+        ),
+        in_specs=[vmem] * 3,
+        out_specs=(vmem,) * 3,
+        compiler_params=pltpu.CompilerParams(vmem_limit_bytes=16 * MIB),
+    )(stay, got, gate_grad)
+
+
+def plane_body(tokens, expert_ids, priority, gate_values, weight_in, weight_out, cotangent):
+    token_count, width = tokens.shape
+    dp_count = lax.axis_size("dp")
+    experts = dp_count // HBLK
+    slot_count = min(token_count, 2 * token_count // experts + max(1, token_count // (4 * experts)))
+    capacity = 2 * token_count * dp_count // experts
+    contract_first = (((0,), (0,)), ((), ()))
+    contract_last = (((1,), (1,)), ((), ()))
+    place_dp = lax.axis_index("dp")
+    first_half = lax.axis_index("rep") == 0
+    plane, quarter = place_dp // HBLK, place_dp % HBLK
+    core_zero = quarter % 2 == 0
+    groups = GROUPS
+
+    def permutation(move):
+        pairs = []
+        for z in range(experts):
+            for q in range(HBLK):
+                for x in range(2):
+                    z2, q2, x2 = move(z, q, x)
+                    pairs.append((2 * (z * HBLK + q) + x, 2 * (z2 * HBLK + q2) + x2))
+        return pairs
+
+    def send(array, move):
+        return lax.ppermute(array, ("dp", "rep"), permutation(move))
+
+    def along_first(z, q, x):
+        return (z, q, 1 - x) if q % 2 == 0 else (z, q ^ 2, x)
+
+    def along_second(z, q, x):
+        return (z, q ^ 2, x) if q % 2 == 0 else (z, q, 1 - x)
+
+    def other_core(z, q, x):
+        return (z, q ^ 1, x)
+
+    def other_row(z, q, x):
+        return (z, q ^ 2, x)
+
+    def planes_on(k):
+        return lambda z, q, x: ((z + k) % experts, q, x)
+
+    def add(*terms):
+        return sum(term.astype(jnp.float32) for term in terms).astype(jnp.bfloat16)
+
+    def step(made, *values):
+        if made:
+            values, _ = lax.optimization_barrier((values, made))
+        return values if len(values) > 1 else values[0]
+
+    def join(parts):
+        return parts[0] if len(parts) == 1 else jnp.concatenate(parts, axis=0)
+
+    ids, gates = expert_ids.T, gate_values.T
+    places, *blocks = start_call(
+        ids, priority[None, :], gates, tokens, cotangent, experts, slot_count
+    )
+    block_rows = blocks[0].shape[0]
+
+    matrix_in = weight_in[0]
+    matrix_out = weight_out[0]
+    state = [{} for _ in groups]
+    home = {}
+
+    def spread_first(g, block):
+        one = state[g]
+        one["b00"] = block
+        one["r1"] = send(block, along_first)
+        one["r2"] = send(block, along_second)
+        return [one["r1"]]
+
+    def spread_second(g, made):
+        one = state[g]
+        one["r1"] = step(made, one["r1"])
+        one["b11"] = send(one["r1"], along_second)
+        return [one["b11"]]
+
+    def gather_near(g, made):
+        one = state[g]
+        b00, r1, r2, b11 = step(made, one["b00"], one["r1"], one["r2"], one["b11"])
+        b10 = jnp.where(core_zero, r2, r1)
+        b01 = jnp.where(core_zero, r1, r2)
+        one["near"] = jnp.concatenate(
+            [
+                jnp.where(first_half, b00, b01),
+                jnp.where(first_half, b10, b11),
+                jnp.where(first_half, b01, b00),
+                jnp.where(first_half, b11, b10),
+            ],
+            axis=0,
+        )
+        one["far"] = send(one["near"], other_core)
+        return [one["near"]]
+
+    def expert_work(g, made):
+        one = state[g]
+        near_rows, far_rows = step(made, one["near"], one["far"])
+        near_parts, far_parts, act, pre = expert_call(near_rows, far_rows, matrix_in, matrix_out)
+        one["saved"] = (near_rows, far_rows, act, pre)
+        one["near_parts"], one["far_parts"] = near_parts, send(far_parts, other_core)
+        return [act]
+
+    def reduce_first(g, made):
+        one = state[g]
+        sums = add(*step(made, one["near_parts"], one["far_parts"]))
+        out0, out1, dx0, dx1 = [
+            sums[at * block_rows : at * block_rows + slot_count] for at in range(4)
+        ]
+        a00, a10 = jnp.where(first_half, out0, dx0), jnp.where(first_half, out1, dx1)
+        a01, a11 = jnp.where(first_half, dx0, out0), jnp.where(first_half, dx1, out1)
+        away = jnp.concatenate([jnp.where(core_zero, a01, a10), a11], axis=0)
+        one["a00"], one["rest"] = a00, jnp.where(core_zero, a10, a01)
+        one["back"] = send(away, along_first)
+        return [away]
+
+    def reduce_second(g, made):
+        one = state[g]
+        one["back"], rest = step(made, one["back"], one["rest"])
+        last = add(rest, one["back"][slot_count:])
+        one["last"] = send(last, along_second)
+        return [last]
+
+    def go_home(g, made):
+        one = state[g]
+        a00, back, last = step(made, one["a00"], one["back"], one["last"])
+        (k,) = groups[g]
+        done = (
+            (a00.astype(jnp.float32) + back[:slot_count].astype(jnp.float32) + last.astype(jnp.float32))
+            * mine[g, :slot_count, 0:1]
+        ).astype(jnp.bfloat16)
+        home[k] = done if k == 0 else send(done, planes_on(experts - k))
+        return [done]
+
+    arrived, events = {}, {}
+    for entry in PLAN:
+        name, g, *after = entry.split()
+        g = int(g)
+        made = [value for one in after for value in events[one]]
+        if name == "Z":
+            arrived[g] = send(step(made, blocks[g]), planes_on(g))
+            here = [arrived[g]]
+        elif name == "D1":
+            (k,) = groups[g]
+            here = spread_first(g, step(made, arrived[k] if k else blocks[0]))
+        elif name == "D2":
+            here = spread_second(g, made)
+        elif name == "SEL":
+            here = gather_near(g, made)
+        elif name == "E":
+            here = expert_work(g, made)
+        elif name == "CUT":
+            pieces = [piece for one in state for piece in one["saved"][:2]]
+            kept, mine = cut_call(step(made, *pieces), slot_count, block_rows, capacity)
+            here = [mine]
+        elif name == "R1":
+            here = reduce_first(g, made)
+        elif name == "R2":
+            here = reduce_second(g, made)
+        elif name == "H":
+            here = go_home(g, made)
+        elif name == "W":
+            saved = [step(made, *one["saved"]) for one in state]
+            grad_in, grad_out = weight_call(kept, saved)
+            here = [grad_in]
+        events[name + str(g)] = here
+
+    away, stay, gate_grad = token_call(gates, places, cotangent, [home[k] for k in range(experts)])
+    got = lax.ppermute(away, "rep", [(0, 1), (1, 0)])
+    output, grad_tokens, grad_gates = end_call(stay, got, gate_grad)
+    return output.T, grad_tokens.T, grad_gates.T, grad_in[None], grad_out[None]
+
+
 def solution(mesh):
     placed = (
         P("dp", None),
@@ -137,6 +659,7 @@
         P("dp", "rep", None),
         P("dp", None),
     )
+    body = plane_body if mesh.shape["rep"] == 2 and mesh.shape["dp"] == 4 * HBLK else general_body
     return jax.shard_map(
         body,
         mesh=mesh,

time: 535 us -> 124 us (0.23); the launches traced: 528 us -> 123 us
  waiting for transfers between devices: 220 us -> 40.9 us
  blocking collectives: 103 us -> 0 us
  local copies, waits for them, and re-layouts: 70.7 us -> 6.81 us
  other arithmetic: 44.6 us -> 4.28 us
  matrix products: 32.8 us -> 0 us
  Pallas kernels: 0 us -> 26.2 us
  between operations: 14.6 us -> 1.08 us
    all_to_all x3 -> x0, waiting for transfers between devices: 190 us -> none  [the longest x1 67.1 us: body(): lax.all_to_all(partial_dx, 'dp', split_axis=0, concat_axis=0, tiled=True)]
    all_to_all x1 -> x0, blocking collectives: 89.4 us -> none  [body(): lax.all_to_all(widen(send_rows), 'dp', split_axis=0, concat_axis=0, tiled...]
    ppermute x0 -> x35, starting transfers between devices: none -> 44.1 us  [the longest x34 43.6 us: send(): return lax.ppermute(array, ('dp', 'rep'), permutation(move))]
    all_to_all x3 -> x0, starting transfers between devices: 41.4 us -> none  [the longest x1 18.4 us: body(): lax.all_to_all(partial_out, 'dp', split_axis=0, concat_axis=0, tiled=True)]
    ppermute x0 -> x35, waiting for transfers between devices: none -> 40.9 us  [the longest x34 35.5 us: send(): return lax.ppermute(array, ('dp', 'rep'), permutation(move))]
    gather x4 -> x0, local copies, waits for them, and re-layouts: 36.4 us -> none  [the longest x2 20.3 us: pick_rows(): picked = jnp.take(returned, pick_index, axis=0)]
    dot_general x9 -> x0, matrix products: 32.8 us -> none  [the longest x1 6.51 us: body(): hidden_pre = jnp.dot(rows, matrix_in, preferred_element_type=jnp.float32)]
    unnamed x5 -> x0, waiting for transfers between devices: 30.2 us -> none
  transfers between devices with their start and end apart: 6 -> 35, of which waited for: 5 -> 12; matrix products, arithmetic and copies ran while one was open for 12% -> 4% of each run, Pallas kernels for 0% -> 18%
where the time goes in v3:
time: 124 us; the launch traced here: 123 us
  starting transfers between devices  44.1 us (36%)
  waiting for transfers between devices  40.9 us (33%)
  Pallas kernels  26.2 us (21%)
  local copies, waits for them, and re-layouts  6.81 us (5%)
  other arithmetic  4.28 us (3%)
    ppermute x34, starting transfers between devices, send(): return lax.ppermute(array, ('dp', 'rep'), permutation(move))  43.6 us
    ppermute x34, waiting for transfers between devices, send(): return lax.ppermute(array, ('dp', 'rep'), permutation(move))  35.5 us
    pallas_call x1, Pallas kernels, weight_call(): pl.pallas_call(weight_kernel, grid=(pl.cdiv(width, tile),), out_shape=(ja...  11.3 us
    pallas_call x4, Pallas kernels, expert_call(): pl.pallas_call(expert_kernel, out_shape=(jax.ShapeDtypeStruct((rows, widt...  10.2 us
    unnamed x44, local copies, waits for them, and re-layouts  6.67 us
    ppermute x1, waiting for transfers between devices, plane_body(): got = lax.ppermute(away, 'rep', [(0, 1), (1, 0)])  5.42 us
  transfers between devices with their start and end apart: 35, of which 12 were waited for; matrix products, arithmetic and copies ran while one was open for 4% of the time, Pallas kernels for 18%

profile of v3, /device:TPU:0, one launch (start us, length us, event | category | flops | bytes accessed | tf_op | source)
XLA Modules:
  0.0 123.4 jit_solution(13257235888526911627)
XLA Ops:
  0.6 2.4 %shard_map.110 = (bf16[2,4,72,128]{3,2,1,0:T(8,128)(2,1)}, bf16[80,1664]{1,0:T(8,128)(2,1)}, bf16[80,1664]{1,0:T(8,128)(2,1)}, bf16[80,1664]{1,0:T(8,128)(2,1)}, bf16[80,1664]{1,0:T(8,128)(2,1)}) custom-call(s32[2,128]{1,0:T(2,128)} %bitcast.20, s32[1,128]{1,0:T(1,128)} %bitcast.21, f32[2,128]{1,0:T(2,128)} %bitcast.18, bf16[128,1664]{1,0:T(8,128)(2,1)} %tokens_at.1, ...), custom_call_target="tpu_custom_call" | custom-call | tf_op jit(solution)/shard_map/pallas_call | solution.py:274
  3.0 3.0 %collective-permute-start = (bf16[80,1664]{1,0:T(8,128)(2,1)}, bf16[80,1664]{1,0:T(8,128)(2,1)S(1)}, u32[]{:S(2)}, u32[]{:S(2)}) collective-permute-start(bf16[80,1664]{1,0:T(8,128)(2,1)} %get-tuple-element.87), channel_id=1, source_target_pairs={{0,1},{1,0},{2,6},{3,7},{4,5},{5,4},{6,2},{7,3},{8,9},{9,8},{10,14... | collective-permute-start | bytes 798728 | tf_op jit(solution)/shard_map/ppermute | solution.py:505
  9.1 2.6 %collective-permute-start.18 = (bf16[80,1664]{1,0:T(8,128)(2,1)}, bf16[80,1664]{1,0:T(8,128)(2,1)S(1)}, u32[]{:S(2)}, u32[]{:S(2)}) collective-permute-start(bf16[80,1664]{1,0:T(8,128)(2,1)} %get-tuple-element.105), channel_id=1, source_target_pairs={{0,16},{1,17},{2,18},{3,19},{4,20},{5,21},{6,22},{7,23},{8,24},{9,... | collective-permute-start | bytes 798728 | tf_op jit(solution)/shard_map/ppermute | solution.py:505
  13.1 2.2 %collective-permute-start.2 = (bf16[80,1664]{1,0:T(8,128)(2,1)S(1)}, bf16[80,1664]{1,0:T(8,128)(2,1)S(1)}, u32[]{:S(2)}, u32[]{:S(2)}) collective-permute-start(bf16[80,1664]{1,0:T(8,128)(2,1)S(1)} %collective-permute-done), channel_id=1, source_target_pairs={{0,4},{1,5},{2,3},{3,2},{4,0},{5,1},{6,7},{7,6},{8,12},{9,13},{10,... | collective-permute-start | bytes 798728 | tf_op jit(solution)/shard_map/ppermute | solution.py:505
  15.2 2.2 %collective-permute-done.4 = bf16[80,1664]{1,0:T(8,128)(2,1)S(1)} collective-permute-done((bf16[80,1664]{1,0:T(8,128)(2,1)}, bf16[80,1664]{1,0:T(8,128)(2,1)S(1)}, u32[]{:S(2)}, u32[]{:S(2)}) %collective-permute-start.4) | collective-permute-done | bytes 266272 | tf_op jit(solution)/shard_map/ppermute | solution.py:505
  17.8 1.8 %collective-permute-start.6 = (bf16[80,1664]{1,0:T(8,128)(2,1)S(1)}, bf16[80,1664]{1,0:T(8,128)(2,1)S(1)}, u32[]{:S(2)}, u32[]{:S(2)}) collective-permute-start(bf16[80,1664]{1,0:T(8,128)(2,1)S(1)} %collective-permute-done.4), channel_id=1, source_target_pairs={{0,4},{1,5},{2,3},{3,2},{4,0},{5,1},{6,7},{7,6},{8,12},{9,13},{10,... | collective-permute-start | bytes 798728 | tf_op jit(solution)/shard_map/ppermute | solution.py:505
  19.6 7.9 %collective-permute-done.18 = bf16[80,1664]{1,0:T(8,128)(2,1)S(1)} collective-permute-done((bf16[80,1664]{1,0:T(8,128)(2,1)}, bf16[80,1664]{1,0:T(8,128)(2,1)S(1)}, u32[]{:S(2)}, u32[]{:S(2)}) %collective-permute-start.18) | collective-permute-done | bytes 266272 | tf_op jit(solution)/shard_map/ppermute | solution.py:505
  33.2 3.5 %collective-permute-done.19 = bf16[80,1664]{1,0:T(8,128)(2,1)S(1)} collective-permute-done((bf16[80,1664]{1,0:T(8,128)(2,1)S(1)}, bf16[80,1664]{1,0:T(8,128)(2,1)S(1)}, u32[]{:S(2)}, u32[]{:S(2)}) %collective-permute-start.19) | collective-permute-done | bytes 266272 | tf_op jit(solution)/shard_map/ppermute | solution.py:505
  37.1 5.4 %collective-permute-done.12 = bf16[80,1664]{1,0:T(8,128)(2,1)S(1)} collective-permute-done((bf16[80,1664]{1,0:T(8,128)(2,1)S(1)}, bf16[80,1664]{1,0:T(8,128)(2,1)S(1)}, u32[]{:S(2)}, u32[]{:S(2)}) %collective-permute-start.12) | collective-permute-done | bytes 266272 | tf_op jit(solution)/shard_map/ppermute | solution.py:505
  44.3 2.9 %collective-permute-done.21 = bf16[80,1664]{1,0:T(8,128)(2,1)S(1)} collective-permute-done((bf16[80,1664]{1,0:T(8,128)(2,1)S(1)}, bf16[80,1664]{1,0:T(8,128)(2,1)S(1)}, u32[]{:S(2)}, u32[]{:S(2)}) %collective-permute-start.21) | collective-permute-done | bytes 266272 | tf_op jit(solution)/shard_map/ppermute | solution.py:505
  47.1 2.9 %collective-permute-done.14 = bf16[80,1664]{1,0:T(8,128)(2,1)S(1)} collective-permute-done((bf16[80,1664]{1,0:T(8,128)(2,1)S(1)}, bf16[80,1664]{1,0:T(8,128)(2,1)S(1)}, u32[]{:S(2)}, u32[]{:S(2)}) %collective-permute-start.14) | collective-permute-done | bytes 266272 | tf_op jit(solution)/shard_map/ppermute | solution.py:505
  52.8 2.5 %shard_map.111 = (bf16[320,1664]{1,0:T(8,128)(2,1)S(1)}, bf16[320,1664]{1,0:T(8,128)(2,1)S(1)}, bf16[320,512]{1,0:T(8,128)(2,1)S(1)}, bf16[320,512]{1,0:T(8,128)(2,1)S(1)}) custom-call(bf16[320,1664]{1,0:T(8,128)(2,1)S(1)} %pad_maximum_fusion.1.near.refs_2_.refs_4_.refs_5_, bf16[320,1664]{1,0:T(8,128)(2,1)S(1)} %collective-permute-done.8.far.refs_3_.refs_6_.refs_7_, ...), custom_call_target="tpu_custom_call" | custom-call | tf_op jit(solution)/shard_map/pallas_call | solution.py:198
  56.3 2.5 %shard_map.112 = (bf16[320,1664]{1,0:T(8,128)(2,1)S(1)}, bf16[320,1664]{1,0:T(8,128)(2,1)S(1)}, bf16[320,512]{1,0:T(8,128)(2,1)S(1)}, bf16[320,512]{1,0:T(8,128)(2,1)S(1)}) custom-call(bf16[320,1664]{1,0:T(8,128)(2,1)S(1)} %pad_maximum_fusion.near.refs_0_.refs_1_, bf16[320,1664]{1,0:T(8,128)(2,1)S(1)} %collective-permute-done.3.far.refs_1_.refs_2_.refs_3_, ...), custom_call_target="tpu_custom_call" | custom-call | tf_op jit(solution)/shard_map/pallas_call | solution.py:198
  60.7 2.5 %shard_map.113 = (bf16[320,1664]{1,0:T(8,128)(2,1)S(1)}, bf16[320,1664]{1,0:T(8,128)(2,1)S(1)}, bf16[320,512]{1,0:T(8,128)(2,1)S(1)}, bf16[320,512]{1,0:T(8,128)(2,1)S(1)}) custom-call(bf16[320,1664]{1,0:T(8,128)(2,1)S(1)} %pad_maximum_fusion.2.near.refs_4_.refs_8_.refs_9_, bf16[320,1664]{1,0:T(8,128)(2,1)S(1)} %collective-permute-done.15.far.refs_5_.refs_10_.refs_11_, ...), custom_call_target="tpu_custom_call" | custom-call | tf_op jit(solution)/shard_map/pallas_call | solution.py:198
  64.2 1.6 %collective-permute-start.16 = (bf16[144,1664]{1,0:T(8,128)(2,1)S(1)}, bf16[144,1664]{1,0:T(8,128)(2,1)S(1)}, u32[]{:S(2)}, u32[]{:S(2)}) collective-permute-start(bf16[144,1664]{1,0:T(8,128)(2,1)S(1)} %pad_maximum_fusion.4), channel_id=1, source_target_pairs={{0,1},{1,0},{2,6},{3,7},{4,5},{5,4},{6,2},{7,3},{8,9},{9,8},{10,14... | collective-permute-start | bytes 1437704 | tf_op jit(solution)/shard_map/ppermute | solution.py:505
  65.8 2.5 %shard_map.114 = (bf16[320,1664]{1,0:T(8,128)(2,1)S(1)}, bf16[320,1664]{1,0:T(8,128)(2,1)S(1)}, bf16[320,512]{1,0:T(8,128)(2,1)S(1)}, bf16[320,512]{1,0:T(8,128)(2,1)S(1)}) custom-call(bf16[320,1664]{1,0:T(8,128)(2,1)S(1)} %pad_maximum_fusion.3.near.refs_6_.refs_12_.refs_13_, bf16[320,1664]{1,0:T(8,128)(2,1)S(1)} %collective-permute-done.22.far.refs_7_.refs_14_.refs_15_, ...), custom_call_target="tpu_custom_call" | custom-call | tf_op jit(solution)/shard_map/pallas_call | solution.py:198
  76.0 4.6 %collective-permute-done.24 = bf16[144,1664]{1,0:T(8,128)(2,1)S(1)} collective-permute-done((bf16[144,1664]{1,0:T(8,128)(2,1)S(1)}, bf16[144,1664]{1,0:T(8,128)(2,1)S(1)}, u32[]{:S(2)}, u32[]{:S(2)}) %collective-permute-start.24) | collective-permute-done | bytes 479264 | tf_op jit(solution)/shard_map/ppermute | solution.py:505
  82.2 7.1 %collective-permute-start.31 = (bf16[72,1664]{1,0:T(8,128)(2,1)S(1)}, bf16[72,1664]{1,0:T(8,128)(2,1)S(1)}, u32[]{:S(2)}, u32[]{:S(2)}) collective-permute-start(bf16[72,1664]{1,0:T(8,128)(2,1)S(1)} %multiply_convert_fusion.3), channel_id=1, source_target_pairs={{0,24},{1,25},{2,26},{3,27},{4,28},{5,29},{6,30},{7,31},{8,0},{9,1... | collective-permute-start | bytes 718856 | tf_op jit(solution)/shard_map/ppermute | solution.py:505
  89.7 1.6 %collective-permute-start.26 = (bf16[144,1664]{1,0:T(8,128)(2,1)S(1)}, bf16[144,1664]{1,0:T(8,128)(2,1)S(1)}, u32[]{:S(2)}, u32[]{:S(2)}) collective-permute-start(bf16[144,1664]{1,0:T(8,128)(2,1)S(1)} %pad_maximum_fusion.7), channel_id=1, source_target_pairs={{0,1},{1,0},{2,6},{3,7},{4,5},{5,4},{6,2},{7,3},{8,9},{9,8},{10,14... | collective-permute-start | bytes 1437704 | tf_op jit(solution)/shard_map/ppermute | solution.py:505
  92.6 2.6 %collective-permute-start.33 = (bf16[72,1664]{1,0:T(8,128)(2,1)S(1)}, bf16[72,1664]{1,0:T(8,128)(2,1)S(1)}, u32[]{:S(2)}, u32[]{:S(2)}) collective-permute-start(bf16[72,1664]{1,0:T(8,128)(2,1)S(1)} %multiply_convert_fusion.2), channel_id=1, source_target_pairs={{0,8},{1,9},{2,10},{3,11},{4,12},{5,13},{6,14},{7,15},{8,16},{9,17... | collective-permute-start | bytes 718856 | tf_op jit(solution)/shard_map/ppermute | solution.py:505
  95.2 4.1 %collective-permute-done.26 = bf16[144,1664]{1,0:T(8,128)(2,1)S(1)} collective-permute-done((bf16[144,1664]{1,0:T(8,128)(2,1)S(1)}, bf16[144,1664]{1,0:T(8,128)(2,1)S(1)}, u32[]{:S(2)}, u32[]{:S(2)}) %collective-permute-start.26) | collective-permute-done | bytes 479264 | tf_op jit(solution)/shard_map/ppermute | solution.py:505
  100.1 3.3 %collective-permute-start.32 = (bf16[72,1664]{1,0:T(8,128)(2,1)S(1)}, bf16[72,1664]{1,0:T(8,128)(2,1)S(1)}, u32[]{:S(2)}, u32[]{:S(2)}) collective-permute-start(bf16[72,1664]{1,0:T(8,128)(2,1)S(1)} %multiply_convert_fusion.1), channel_id=1, source_target_pairs={{0,16},{1,17},{2,18},{3,19},{4,20},{5,21},{6,22},{7,23},{8,24},{9,... | collective-permute-start | bytes 718856 | tf_op jit(solution)/shard_map/ppermute | solution.py:505
  103.4 11.3 %shard_map.116 = (bf16[1664,512]{1,0:T(8,128)(2,1)}, bf16[512,1664]{1,0:T(8,128)(2,1)}) custom-call(bf16[1280,128]{1,0:T(8,128)(2,1)} %copy-done.19, bf16[320,1664]{1,0:T(8,128)(2,1)} %copy-done.3, bf16[320,1664]{1,0:T(8,128)(2,1)} %copy-done.3, bf16[320,1664]{1,0:T(8,128)(2,1)} %copy-done.7, bf16[320,1664]{1,0:T(8,128)(2,1)} %copy-done.7, ...), custom_call_target="tpu_custom_call" | custom-call | tf_op jit(solution)/shard_map/pallas_call | solution.py:385
  117.1 5.4 %collective-permute-done.34.got = bf16[848,128]{1,0:T(8,128)(2,1)S(1)} collective-permute-done((bf16[848,128]{1,0:T(8,128)(2,1)S(1)}, bf16[848,128]{1,0:T(8,128)(2,1)S(1)}, u32[]{:S(2)}, u32[]{:S(2)}) %collective-permute-start.34) | collective-permute-done | bytes 217120 | tf_op jit(solution)/shard_map/ppermute | solution.py:647
  (127 shorter events, 33.9 us)
Async XLA Ops:
  3.0 10.0 %collective-permute-start = (bf16[80,1664]{1,0:T(8,128)(2,1)}, bf16[80,1664]{1,0:T(8,128)(2,1)S(1)}, u32[]{:S(2)}, u32[]{:S(2)}) collective-permute-start(bf16[80,1664]{1,0:T(8,128)(2,1)} %get-tuple-element.87), channel_id=1, source_target_pairs={{0,1},{1,0},{2,6},{3,7},{4,5},{5,4},{6,2},{7,3},{8,9},{9,8},{10,14... | collective-permute-start | bytes 798728 | tf_op jit(solution)/shard_map/ppermute | solution.py:505
  6.0 11.4 %collective-permute-start.4 = (bf16[80,1664]{1,0:T(8,128)(2,1)}, bf16[80,1664]{1,0:T(8,128)(2,1)S(1)}, u32[]{:S(2)}, u32[]{:S(2)}) collective-permute-start(bf16[80,1664]{1,0:T(8,128)(2,1)} %get-tuple-element.88), channel_id=1, source_target_pairs={{0,8},{1,9},{2,10},{3,11},{4,12},{5,13},{6,14},{7,15},{8,16},{9,17... | collective-permute-start | bytes 798728 | tf_op jit(solution)/shard_map/ppermute | solution.py:505
  7.6 10.2 %collective-permute-start.1 = (bf16[80,1664]{1,0:T(8,128)(2,1)}, bf16[80,1664]{1,0:T(8,128)(2,1)S(1)}, u32[]{:S(2)}, u32[]{:S(2)}) collective-permute-start(bf16[80,1664]{1,0:T(8,128)(2,1)} %get-tuple-element.87), channel_id=1, source_target_pairs={{0,4},{1,5},{2,3},{3,2},{4,0},{5,1},{6,7},{7,6},{8,12},{9,13},{10,... | collective-permute-start | bytes 798728 | tf_op jit(solution)/shard_map/ppermute | solution.py:505
  9.1 18.4 %collective-permute-start.18 = (bf16[80,1664]{1,0:T(8,128)(2,1)}, bf16[80,1664]{1,0:T(8,128)(2,1)S(1)}, u32[]{:S(2)}, u32[]{:S(2)}) collective-permute-start(bf16[80,1664]{1,0:T(8,128)(2,1)} %get-tuple-element.105), channel_id=1, source_target_pairs={{0,16},{1,17},{2,18},{3,19},{4,20},{5,21},{6,22},{7,23},{8,24},{9,... | collective-permute-start | bytes 798728 | tf_op jit(solution)/shard_map/ppermute | solution.py:505
  11.7 17.3 %collective-permute-start.11 = (bf16[80,1664]{1,0:T(8,128)(2,1)}, bf16[80,1664]{1,0:T(8,128)(2,1)S(1)}, u32[]{:S(2)}, u32[]{:S(2)}) collective-permute-start(bf16[80,1664]{1,0:T(8,128)(2,1)} %get-tuple-element.96), channel_id=1, source_target_pairs={{0,24},{1,25},{2,26},{3,27},{4,28},{5,29},{6,30},{7,31},{8,0},{9,1... | collective-permute-start | bytes 798728 | tf_op jit(solution)/shard_map/ppermute | solution.py:505
  13.1 16.5 %collective-permute-start.2 = (bf16[80,1664]{1,0:T(8,128)(2,1)S(1)}, bf16[80,1664]{1,0:T(8,128)(2,1)S(1)}, u32[]{:S(2)}, u32[]{:S(2)}) collective-permute-start(bf16[80,1664]{1,0:T(8,128)(2,1)S(1)} %collective-permute-done), channel_id=1, source_target_pairs={{0,4},{1,5},{2,3},{3,2},{4,0},{5,1},{6,7},{7,6},{8,12},{9,13},{10,... | collective-permute-start | bytes 798728 | tf_op jit(solution)/shard_map/ppermute | solution.py:505
  17.5 12.6 %collective-permute-start.5 = (bf16[80,1664]{1,0:T(8,128)(2,1)S(1)}, bf16[80,1664]{1,0:T(8,128)(2,1)S(1)}, u32[]{:S(2)}, u32[]{:S(2)}) collective-permute-start(bf16[80,1664]{1,0:T(8,128)(2,1)S(1)} %collective-permute-done.4), channel_id=1, source_target_pairs={{0,1},{1,0},{2,6},{3,7},{4,5},{5,4},{6,2},{7,3},{8,9},{9,8},{10,14... | collective-permute-start | bytes 798728 | tf_op jit(solution)/shard_map/ppermute | solution.py:505
  17.8 14.9 %collective-permute-start.6 = (bf16[80,1664]{1,0:T(8,128)(2,1)S(1)}, bf16[80,1664]{1,0:T(8,128)(2,1)S(1)}, u32[]{:S(2)}, u32[]{:S(2)}) collective-permute-start(bf16[80,1664]{1,0:T(8,128)(2,1)S(1)} %collective-permute-done.4), channel_id=1, source_target_pairs={{0,4},{1,5},{2,3},{3,2},{4,0},{5,1},{6,7},{7,6},{8,12},{9,13},{10,... | collective-permute-start | bytes 798728 | tf_op jit(solution)/shard_map/ppermute | solution.py:505
  29.0 14.2 %collective-permute-start.20 = (bf16[80,1664]{1,0:T(8,128)(2,1)S(1)}, bf16[80,1664]{1,0:T(8,128)(2,1)S(1)}, u32[]{:S(2)}, u32[]{:S(2)}) collective-permute-start(bf16[80,1664]{1,0:T(8,128)(2,1)S(1)} %collective-permute-done.18), channel_id=1, source_target_pairs={{0,4},{1,5},{2,3},{3,2},{4,0},{5,1},{6,7},{7,6},{8,12},{9,13},{10,... | collective-permute-start | bytes 798728 | tf_op jit(solution)/shard_map/ppermute | solution.py:505
  29.5 12.9 %collective-permute-start.12 = (bf16[80,1664]{1,0:T(8,128)(2,1)S(1)}, bf16[80,1664]{1,0:T(8,128)(2,1)S(1)}, u32[]{:S(2)}, u32[]{:S(2)}) collective-permute-start(bf16[80,1664]{1,0:T(8,128)(2,1)S(1)} %collective-permute-done.11), channel_id=1, source_target_pairs={{0,1},{1,0},{2,6},{3,7},{4,5},{5,4},{6,2},{7,3},{8,9},{9,8},{10,14... | collective-permute-start | bytes 798728 | tf_op jit(solution)/shard_map/ppermute | solution.py:505
  30.0 12.7 %collective-permute-start.7 = (bf16[80,1664]{1,0:T(8,128)(2,1)S(1)}, bf16[80,1664]{1,0:T(8,128)(2,1)S(1)}, u32[]{:S(2)}, u32[]{:S(2)}) collective-permute-start(bf16[80,1664]{1,0:T(8,128)(2,1)S(1)} %collective-permute-done.5), channel_id=1, source_target_pairs={{0,4},{1,5},{2,3},{3,2},{4,0},{5,1},{6,7},{7,6},{8,12},{9,13},{10,... | collective-permute-start | bytes 798728 | tf_op jit(solution)/shard_map/ppermute | solution.py:505
  32.7 11.6 %collective-permute-start.13 = (bf16[80,1664]{1,0:T(8,128)(2,1)S(1)}, bf16[80,1664]{1,0:T(8,128)(2,1)S(1)}, u32[]{:S(2)}, u32[]{:S(2)}) collective-permute-start(bf16[80,1664]{1,0:T(8,128)(2,1)S(1)} %collective-permute-done.11), channel_id=1, source_target_pairs={{0,4},{1,5},{2,3},{3,2},{4,0},{5,1},{6,7},{7,6},{8,12},{9,13},{10,... | collective-permute-start | bytes 798728 | tf_op jit(solution)/shard_map/ppermute | solution.py:505
  36.7 10.4 %collective-permute-start.21 = (bf16[80,1664]{1,0:T(8,128)(2,1)S(1)}, bf16[80,1664]{1,0:T(8,128)(2,1)S(1)}, u32[]{:S(2)}, u32[]{:S(2)}) collective-permute-start(bf16[80,1664]{1,0:T(8,128)(2,1)S(1)} %collective-permute-done.19), channel_id=1, source_target_pairs={{0,4},{1,5},{2,3},{3,2},{4,0},{5,1},{6,7},{7,6},{8,12},{9,13},{10,... | collective-permute-start | bytes 798728 | tf_op jit(solution)/shard_map/ppermute | solution.py:505
  43.2 13.1 %collective-permute-start.3 = (bf16[320,1664]{1,0:T(8,128)(2,1)S(1)}, bf16[320,1664]{1,0:T(8,128)(2,1)S(1)}, u32[]{:S(2)}, u32[]{:S(2)}) collective-permute-start(bf16[320,1664]{1,0:T(8,128)(2,1)S(1)} %pad_maximum_fusion.near.refs_0_.refs_1_), channel_id=1, source_target_pairs={{0,2},{1,3},{2,0},{3,1},{4,6},{5,7},{6,4},{7,5},{8,10},{9,11},{10,... | collective-permute-start | bytes 3194888 | tf_op jit(solution)/shard_map/ppermute | solution.py:505
  50.4 10.3 %collective-permute-start.15 = (bf16[320,1664]{1,0:T(8,128)(2,1)S(1)}, bf16[320,1664]{1,0:T(8,128)(2,1)S(1)}, u32[]{:S(2)}, u32[]{:S(2)}) collective-permute-start(bf16[320,1664]{1,0:T(8,128)(2,1)S(1)} %pad_maximum_fusion.2.near.refs_4_.refs_8_.refs_9_), channel_id=1, source_target_pairs={{0,2},{1,3},{2,0},{3,1},{4,6},{5,7},{6,4},{7,5},{8,10},{9,11},{10,... | collective-permute-start | bytes 3194888 | tf_op jit(solution)/shard_map/ppermute | solution.py:505
  56.2 9.6 %collective-permute-start.22 = (bf16[320,1664]{1,0:T(8,128)(2,1)S(1)}, bf16[320,1664]{1,0:T(8,128)(2,1)S(1)}, u32[]{:S(2)}, u32[]{:S(2)}) collective-permute-start(bf16[320,1664]{1,0:T(8,128)(2,1)S(1)} %pad_maximum_fusion.3.near.refs_6_.refs_12_.refs_13_), channel_id=1, source_target_pairs={{0,2},{1,3},{2,0},{3,1},{4,6},{5,7},{6,4},{7,5},{8,10},{9,11},{10,... | collective-permute-start | bytes 3194888 | tf_op jit(solution)/shard_map/ppermute | solution.py:505
  60.3 29.0 %collective-permute-start.9 = (bf16[320,1664]{1,0:T(8,128)(2,1)S(1)}, bf16[320,1664]{1,0:T(8,128)(2,1)S(1)}, u32[]{:S(2)}, u32[]{:S(2)}) collective-permute-start(bf16[320,1664]{1,0:T(8,128)(2,1)S(1)} %get-tuple-element.93), channel_id=1, source_target_pairs={{0,2},{1,3},{2,0},{3,1},{4,6},{5,7},{6,4},{7,5},{8,10},{9,11},{10,... | collective-permute-start | bytes 3194888 | tf_op jit(solution)/shard_map/ppermute | solution.py:505
  69.3 11.4 %collective-permute-start.24 = (bf16[144,1664]{1,0:T(8,128)(2,1)S(1)}, bf16[144,1664]{1,0:T(8,128)(2,1)S(1)}, u32[]{:S(2)}, u32[]{:S(2)}) collective-permute-start(bf16[144,1664]{1,0:T(8,128)(2,1)S(1)} %pad_maximum_fusion.5), channel_id=1, source_target_pairs={{0,1},{1,0},{2,6},{3,7},{4,5},{5,4},{6,2},{7,3},{8,9},{9,8},{10,14... | collective-permute-start | bytes 1437704 | tf_op jit(solution)/shard_map/ppermute | solution.py:505
  74.4 16.9 %collective-permute-start.28 = (bf16[144,1664]{1,0:T(8,128)(2,1)S(1)}, bf16[144,1664]{1,0:T(8,128)(2,1)S(1)}, u32[]{:S(2)}, u32[]{:S(2)}) collective-permute-start(bf16[144,1664]{1,0:T(8,128)(2,1)S(1)} %pad_maximum_fusion.6), channel_id=1, source_target_pairs={{0,1},{1,0},{2,6},{3,7},{4,5},{5,4},{6,2},{7,3},{8,9},{9,8},{10,14... | collective-permute-start | bytes 1437704 | tf_op jit(solution)/shard_map/ppermute | solution.py:505
  80.7 11.7 %collective-permute-start.27 = (bf16[72,1664]{1,0:T(8,128)(2,1)S(1)}, bf16[72,1664]{1,0:T(8,128)(2,1)S(1)}, u32[]{:S(2)}, u32[]{:S(2)}) collective-permute-start(bf16[72,1664]{1,0:T(8,128)(2,1)S(1)} %add_convert_fusion.6), channel_id=1, source_target_pairs={{0,4},{1,5},{2,3},{3,2},{4,0},{5,1},{6,7},{7,6},{8,12},{9,13},{10,... | collective-permute-start | bytes 718856 | tf_op jit(solution)/shard_map/ppermute | solution.py:505
  82.2 32.7 %collective-permute-start.31 = (bf16[72,1664]{1,0:T(8,128)(2,1)S(1)}, bf16[72,1664]{1,0:T(8,128)(2,1)S(1)}, u32[]{:S(2)}, u32[]{:S(2)}) collective-permute-start(bf16[72,1664]{1,0:T(8,128)(2,1)S(1)} %multiply_convert_fusion.3), channel_id=1, source_target_pairs={{0,24},{1,25},{2,26},{3,27},{4,28},{5,29},{6,30},{7,31},{8,0},{9,1... | collective-permute-start | bytes 718856 | tf_op jit(solution)/shard_map/ppermute | solution.py:505
  92.6 22.2 %collective-permute-start.33 = (bf16[72,1664]{1,0:T(8,128)(2,1)S(1)}, bf16[72,1664]{1,0:T(8,128)(2,1)S(1)}, u32[]{:S(2)}, u32[]{:S(2)}) collective-permute-start(bf16[72,1664]{1,0:T(8,128)(2,1)S(1)} %multiply_convert_fusion.2), channel_id=1, source_target_pairs={{0,8},{1,9},{2,10},{3,11},{4,12},{5,13},{6,14},{7,15},{8,16},{9,17... | collective-permute-start | bytes 718856 | tf_op jit(solution)/shard_map/ppermute | solution.py:505
  99.3 15.4 %collective-permute-start.29 = (bf16[72,1664]{1,0:T(8,128)(2,1)S(1)}, bf16[72,1664]{1,0:T(8,128)(2,1)S(1)}, u32[]{:S(2)}, u32[]{:S(2)}) collective-permute-start(bf16[72,1664]{1,0:T(8,128)(2,1)S(1)} %add_convert_fusion.4), channel_id=1, source_target_pairs={{0,4},{1,5},{2,3},{3,2},{4,0},{5,1},{6,7},{7,6},{8,12},{9,13},{10,... | collective-permute-start | bytes 718856 | tf_op jit(solution)/shard_map/ppermute | solution.py:505
  100.1 14.8 %collective-permute-start.32 = (bf16[72,1664]{1,0:T(8,128)(2,1)S(1)}, bf16[72,1664]{1,0:T(8,128)(2,1)S(1)}, u32[]{:S(2)}, u32[]{:S(2)}) collective-permute-start(bf16[72,1664]{1,0:T(8,128)(2,1)S(1)} %multiply_convert_fusion.1), channel_id=1, source_target_pairs={{0,16},{1,17},{2,18},{3,19},{4,20},{5,21},{6,22},{7,23},{8,24},{9,... | collective-permute-start | bytes 718856 | tf_op jit(solution)/shard_map/ppermute | solution.py:505
  (33 other events, 244.1 us)

commit v4 on v3

--- a/solution.py
+++ b/solution.py
@@ -145,13 +145,13 @@
     "D1 2",
     "SEL 1",
     "D2 2",
-    "D1 3",
+    "D1 3 SEL0",
     "D2 3",
     "SEL 2",
-    "SEL 3",
-    "E 1",
-    "E 0 E1",
-    "E 2 E0",
+    "E 0",
+    "E 1 E0",
+    "SEL 3 E0",
+    "E 2 E1",
     "R1 1 E2",
     "E 3 R11",
     "CUT 0",

time: 124 us -> 117 us (0.944)
  waiting for transfers between devices: 40.9 us -> 26.4 us
  starting transfers between devices: 44.1 us -> 54.2 us
  local copies, waits for them, and re-layouts: 6.81 us -> 4.19 us
    ppermute x34, waiting for transfers between devices: 35.5 us -> 21.9 us  [send(): return lax.ppermute(array, ('dp', 'rep'), permutation(move))]
    ppermute x34, starting transfers between devices: 43.6 us -> 52.8 us  [send(): return lax.ppermute(array, ('dp', 'rep'), permutation(move))]
    unnamed x44, local copies, waits for them, and re-layouts: 6.67 us -> 4.05 us
  transfers between devices with their start and end apart: 35 -> 35, of which waited for: 12 -> 12; matrix products, arithmetic and copies ran while one was open for 4% -> 4% of each run, Pallas kernels for 18% -> 19%
where the time goes in v4:
time: 117 us
  starting transfers between devices  54.2 us (46%)
  waiting for transfers between devices  26.4 us (23%)
  Pallas kernels  26.2 us (22%)
  other arithmetic  4.3 us (4%)
  local copies, waits for them, and re-layouts  4.19 us (4%)
  between operations  1.18 us (1%)
    ppermute x34, starting transfers between devices, send(): return lax.ppermute(array, ('dp', 'rep'), permutation(move))  52.8 us
    ppermute x34, waiting for transfers between devices, send(): return lax.ppermute(array, ('dp', 'rep'), permutation(move))  21.9 us
    pallas_call x1, Pallas kernels, weight_call(): pl.pallas_call(weight_kernel, grid=(pl.cdiv(width, tile),), out_shape=(ja...  11.3 us
    pallas_call x4, Pallas kernels, expert_call(): pl.pallas_call(expert_kernel, out_shape=(jax.ShapeDtypeStruct((rows, widt...  10.2 us
    ppermute x1, waiting for transfers between devices, plane_body(): got = lax.ppermute(away, 'rep', [(0, 1), (1, 0)])  4.55 us
    unnamed x44, local copies, waits for them, and re-layouts  4.05 us
    pallas_call x1, Pallas kernels, start_call(): pl.pallas_call(functools.partial(start_kernel, experts), out_shape=(jax.S...  2.4 us
  transfers between devices with their start and end apart: 35, of which 12 were waited for; matrix products, arithmetic and copies ran while one was open for 4% of the time, Pallas kernels for 19%

profile of v4, /device:TPU:0, one launch (start us, length us, event | category | flops | bytes accessed | tf_op | source)
XLA Modules:
  0.0 116.5 jit_solution(3544445602973783973)
XLA Ops:
  0.6 2.4 %shard_map.110 = (bf16[2,4,72,128]{3,2,1,0:T(8,128)(2,1)}, bf16[80,1664]{1,0:T(8,128)(2,1)}, bf16[80,1664]{1,0:T(8,128)(2,1)}, bf16[80,1664]{1,0:T(8,128)(2,1)}, bf16[80,1664]{1,0:T(8,128)(2,1)}) custom-call(s32[2,128]{1,0:T(2,128)} %bitcast.20, s32[1,128]{1,0:T(1,128)} %bitcast.21, f32[2,128]{1,0:T(2,128)} %bitcast.18, bf16[128,1664]{1,0:T(8,128)(2,1)} %tokens_at.1, ...), custom_call_target="tpu_custom_call" | custom-call | tf_op jit(solution)/shard_map/pallas_call | solution.py:274
  3.0 3.0 %collective-permute-start = (bf16[80,1664]{1,0:T(8,128)(2,1)}, bf16[80,1664]{1,0:T(8,128)(2,1)S(1)}, u32[]{:S(2)}, u32[]{:S(2)}) collective-permute-start(bf16[80,1664]{1,0:T(8,128)(2,1)} %get-tuple-element.92), channel_id=1, source_target_pairs={{0,1},{1,0},{2,6},{3,7},{4,5},{5,4},{6,2},{7,3},{8,9},{9,8},{10,14... | collective-permute-start | bytes 798728 | tf_op jit(solution)/shard_map/ppermute | solution.py:505
  9.1 2.5 %collective-permute-done = bf16[80,1664]{1,0:T(8,128)(2,1)S(1)} collective-permute-done((bf16[80,1664]{1,0:T(8,128)(2,1)}, bf16[80,1664]{1,0:T(8,128)(2,1)S(1)}, u32[]{:S(2)}, u32[]{:S(2)}) %collective-permute-start) | collective-permute-done | bytes 266272 | tf_op jit(solution)/shard_map/ppermute | solution.py:505
  11.7 3.6 %collective-permute-start.2 = (bf16[80,1664]{1,0:T(8,128)(2,1)S(1)}, bf16[80,1664]{1,0:T(8,128)(2,1)S(1)}, u32[]{:S(2)}, u32[]{:S(2)}) collective-permute-start(bf16[80,1664]{1,0:T(8,128)(2,1)S(1)} %collective-permute-done), channel_id=1, source_target_pairs={{0,4},{1,5},{2,3},{3,2},{4,0},{5,1},{6,7},{7,6},{8,12},{9,13},{10,... | collective-permute-start | bytes 798728 | tf_op jit(solution)/shard_map/ppermute | solution.py:505
  15.2 2.6 %collective-permute-start.18 = (bf16[80,1664]{1,0:T(8,128)(2,1)}, bf16[80,1664]{1,0:T(8,128)(2,1)S(1)}, u32[]{:S(2)}, u32[]{:S(2)}) collective-permute-start(bf16[80,1664]{1,0:T(8,128)(2,1)} %get-tuple-element.110), channel_id=1, source_target_pairs={{0,16},{1,17},{2,18},{3,19},{4,20},{5,21},{6,22},{7,23},{8,24},{9,... | collective-permute-start | bytes 798728 | tf_op jit(solution)/shard_map/ppermute | solution.py:505
  22.4 2.5 %collective-permute-start.7 = (bf16[80,1664]{1,0:T(8,128)(2,1)S(1)}, bf16[80,1664]{1,0:T(8,128)(2,1)S(1)}, u32[]{:S(2)}, u32[]{:S(2)}) collective-permute-start(bf16[80,1664]{1,0:T(8,128)(2,1)S(1)} %collective-permute-done.5), channel_id=1, source_target_pairs={{0,4},{1,5},{2,3},{3,2},{4,0},{5,1},{6,7},{7,6},{8,12},{9,13},{10,... | collective-permute-start | bytes 798728 | tf_op jit(solution)/shard_map/ppermute | solution.py:505
  30.4 2.3 %collective-permute-start.13 = (bf16[80,1664]{1,0:T(8,128)(2,1)S(1)}, bf16[80,1664]{1,0:T(8,128)(2,1)S(1)}, u32[]{:S(2)}, u32[]{:S(2)}) collective-permute-start(bf16[80,1664]{1,0:T(8,128)(2,1)S(1)} %collective-permute-done.11), channel_id=1, source_target_pairs={{0,4},{1,5},{2,3},{3,2},{4,0},{5,1},{6,7},{7,6},{8,12},{9,13},{10,... | collective-permute-start | bytes 798728 | tf_op jit(solution)/shard_map/ppermute | solution.py:505
  32.7 3.2 %collective-permute-done.12 = bf16[80,1664]{1,0:T(8,128)(2,1)S(1)} collective-permute-done((bf16[80,1664]{1,0:T(8,128)(2,1)S(1)}, bf16[80,1664]{1,0:T(8,128)(2,1)S(1)}, u32[]{:S(2)}, u32[]{:S(2)}) %collective-permute-start.12) | collective-permute-done | bytes 266272 | tf_op jit(solution)/shard_map/ppermute | solution.py:505
  39.3 2.3 %collective-permute-done.19 = bf16[80,1664]{1,0:T(8,128)(2,1)S(1)} collective-permute-done((bf16[80,1664]{1,0:T(8,128)(2,1)S(1)}, bf16[80,1664]{1,0:T(8,128)(2,1)S(1)}, u32[]{:S(2)}, u32[]{:S(2)}) %collective-permute-start.19) | collective-permute-done | bytes 266272 | tf_op jit(solution)/shard_map/ppermute | solution.py:505
  45.2 2.5 %shard_map.111 = (bf16[320,1664]{1,0:T(8,128)(2,1)S(1)}, bf16[320,1664]{1,0:T(8,128)(2,1)S(1)}, bf16[320,512]{1,0:T(8,128)(2,1)S(1)}, bf16[320,512]{1,0:T(8,128)(2,1)S(1)}) custom-call(bf16[320,1664]{1,0:T(8,128)(2,1)S(1)} %pad_maximum_fusion.near.refs_0_.refs_1_, bf16[320,1664]{1,0:T(8,128)(2,1)S(1)} %collective-permute-done.3.far.refs_1_.refs_2_.refs_3_, ...), custom_call_target="tpu_custom_call" | custom-call | tf_op jit(solution)/shard_map/pallas_call | solution.py:198
  50.0 2.5 %shard_map.112 = (bf16[320,1664]{1,0:T(8,128)(2,1)S(1)}, bf16[320,1664]{1,0:T(8,128)(2,1)S(1)}, bf16[320,512]{1,0:T(8,128)(2,1)S(1)}, bf16[320,512]{1,0:T(8,128)(2,1)S(1)}) custom-call(bf16[320,1664]{1,0:T(8,128)(2,1)S(1)} %pad_maximum_fusion.1.near.refs_2_.refs_4_.refs_5_, bf16[320,1664]{1,0:T(8,128)(2,1)S(1)} %collective-permute-done.9.far.refs_3_.refs_6_.refs_7_, ...), custom_call_target="tpu_custom_call" | custom-call | tf_op jit(solution)/shard_map/pallas_call | solution.py:198
  53.7 2.5 %shard_map.113 = (bf16[320,1664]{1,0:T(8,128)(2,1)S(1)}, bf16[320,1664]{1,0:T(8,128)(2,1)S(1)}, bf16[320,512]{1,0:T(8,128)(2,1)S(1)}, bf16[320,512]{1,0:T(8,128)(2,1)S(1)}) custom-call(bf16[320,1664]{1,0:T(8,128)(2,1)S(1)} %pad_maximum_fusion.2.near.refs_4_.refs_8_.refs_9_, bf16[320,1664]{1,0:T(8,128)(2,1)S(1)} %collective-permute-done.15.far.refs_5_.refs_10_.refs_11_, ...), custom_call_target="tpu_custom_call" | custom-call | tf_op jit(solution)/shard_map/pallas_call | solution.py:198
  57.2 2.1 %collective-permute-start.16 = (bf16[144,1664]{1,0:T(8,128)(2,1)S(1)}, bf16[144,1664]{1,0:T(8,128)(2,1)S(1)}, u32[]{:S(2)}, u32[]{:S(2)}) collective-permute-start(bf16[144,1664]{1,0:T(8,128)(2,1)S(1)} %pad_maximum_fusion.4), channel_id=1, source_target_pairs={{0,1},{1,0},{2,6},{3,7},{4,5},{5,4},{6,2},{7,3},{8,9},{9,8},{10,14... | collective-permute-start | bytes 1437704 | tf_op jit(solution)/shard_map/ppermute | solution.py:505
  59.4 2.5 %shard_map.114 = (bf16[320,1664]{1,0:T(8,128)(2,1)S(1)}, bf16[320,1664]{1,0:T(8,128)(2,1)S(1)}, bf16[320,512]{1,0:T(8,128)(2,1)S(1)}, bf16[320,512]{1,0:T(8,128)(2,1)S(1)}) custom-call(bf16[320,1664]{1,0:T(8,128)(2,1)S(1)} %pad_maximum_fusion.3.near.refs_6_.refs_12_.refs_13_, bf16[320,1664]{1,0:T(8,128)(2,1)S(1)} %collective-permute-done.22.far.refs_7_.refs_14_.refs_15_, ...), custom_call_target="tpu_custom_call" | custom-call | tf_op jit(solution)/shard_map/pallas_call | solution.py:198
  66.1 2.0 %collective-permute-start.23 = (bf16[72,1664]{1,0:T(8,128)(2,1)S(1)}, bf16[72,1664]{1,0:T(8,128)(2,1)S(1)}, u32[]{:S(2)}, u32[]{:S(2)}) collective-permute-start(bf16[72,1664]{1,0:T(8,128)(2,1)S(1)} %add_convert_fusion.7), channel_id=1, source_target_pairs={{0,4},{1,5},{2,3},{3,2},{4,0},{5,1},{6,7},{7,6},{8,12},{9,13},{10,... | collective-permute-start | bytes 718856 | tf_op jit(solution)/shard_map/ppermute | solution.py:505
  68.6 1.8 %collective-permute-start.28 = (bf16[144,1664]{1,0:T(8,128)(2,1)S(1)}, bf16[144,1664]{1,0:T(8,128)(2,1)S(1)}, u32[]{:S(2)}, u32[]{:S(2)}) collective-permute-start(bf16[144,1664]{1,0:T(8,128)(2,1)S(1)} %pad_maximum_fusion.6), channel_id=1, source_target_pairs={{0,1},{1,0},{2,6},{3,7},{4,5},{5,4},{6,2},{7,3},{8,9},{9,8},{10,14... | collective-permute-start | bytes 1437704 | tf_op jit(solution)/shard_map/ppermute | solution.py:505
  70.4 4.5 %collective-permute-done.24 = bf16[144,1664]{1,0:T(8,128)(2,1)S(1)} collective-permute-done((bf16[144,1664]{1,0:T(8,128)(2,1)S(1)}, bf16[144,1664]{1,0:T(8,128)(2,1)S(1)}, u32[]{:S(2)}, u32[]{:S(2)}) %collective-permute-start.24) | collective-permute-done | bytes 479264 | tf_op jit(solution)/shard_map/ppermute | solution.py:505
  75.0 1.8 %collective-permute-start.27 = (bf16[72,1664]{1,0:T(8,128)(2,1)S(1)}, bf16[72,1664]{1,0:T(8,128)(2,1)S(1)}, u32[]{:S(2)}, u32[]{:S(2)}) collective-permute-start(bf16[72,1664]{1,0:T(8,128)(2,1)S(1)} %add_convert_fusion.6), channel_id=1, source_target_pairs={{0,4},{1,5},{2,3},{3,2},{4,0},{5,1},{6,7},{7,6},{8,12},{9,13},{10,... | collective-permute-start | bytes 718856 | tf_op jit(solution)/shard_map/ppermute | solution.py:505
  77.1 5.4 %collective-permute-start.31 = (bf16[72,1664]{1,0:T(8,128)(2,1)S(1)}, bf16[72,1664]{1,0:T(8,128)(2,1)S(1)}, u32[]{:S(2)}, u32[]{:S(2)}) collective-permute-start(bf16[72,1664]{1,0:T(8,128)(2,1)S(1)} %multiply_convert_fusion.3), channel_id=1, source_target_pairs={{0,24},{1,25},{2,26},{3,27},{4,28},{5,29},{6,30},{7,31},{8,0},{9,1... | collective-permute-start | bytes 718856 | tf_op jit(solution)/shard_map/ppermute | solution.py:505
  85.1 4.6 %collective-permute-start.33 = (bf16[72,1664]{1,0:T(8,128)(2,1)S(1)}, bf16[72,1664]{1,0:T(8,128)(2,1)S(1)}, u32[]{:S(2)}, u32[]{:S(2)}) collective-permute-start(bf16[72,1664]{1,0:T(8,128)(2,1)S(1)} %multiply_convert_fusion.2), channel_id=1, source_target_pairs={{0,8},{1,9},{2,10},{3,11},{4,12},{5,13},{6,14},{7,15},{8,16},{9,17... | collective-permute-start | bytes 718856 | tf_op jit(solution)/shard_map/ppermute | solution.py:505
  89.7 3.1 %collective-permute-done.26 = bf16[144,1664]{1,0:T(8,128)(2,1)S(1)} collective-permute-done((bf16[144,1664]{1,0:T(8,128)(2,1)S(1)}, bf16[144,1664]{1,0:T(8,128)(2,1)S(1)}, u32[]{:S(2)}, u32[]{:S(2)}) %collective-permute-start.26) | collective-permute-done | bytes 479264 | tf_op jit(solution)/shard_map/ppermute | solution.py:505
  93.1 3.4 %collective-permute-start.32 = (bf16[72,1664]{1,0:T(8,128)(2,1)S(1)}, bf16[72,1664]{1,0:T(8,128)(2,1)S(1)}, u32[]{:S(2)}, u32[]{:S(2)}) collective-permute-start(bf16[72,1664]{1,0:T(8,128)(2,1)S(1)} %multiply_convert_fusion.1), channel_id=1, source_target_pairs={{0,16},{1,17},{2,18},{3,19},{4,20},{5,21},{6,22},{7,23},{8,24},{9,... | collective-permute-start | bytes 718856 | tf_op jit(solution)/shard_map/ppermute | solution.py:505
  96.5 11.3 %shard_map.116 = (bf16[1664,512]{1,0:T(8,128)(2,1)}, bf16[512,1664]{1,0:T(8,128)(2,1)}) custom-call(bf16[1280,128]{1,0:T(8,128)(2,1)} %copy-done.19, bf16[320,1664]{1,0:T(8,128)(2,1)} %copy-done.2, bf16[320,1664]{1,0:T(8,128)(2,1)} %copy-done.2, bf16[320,1664]{1,0:T(8,128)(2,1)} %copy-done.6, bf16[320,1664]{1,0:T(8,128)(2,1)} %copy-done.6, ...), custom_call_target="tpu_custom_call" | custom-call | tf_op jit(solution)/shard_map/pallas_call | solution.py:385
  111.1 4.5 %collective-permute-done.34.got = bf16[848,128]{1,0:T(8,128)(2,1)S(1)} collective-permute-done((bf16[848,128]{1,0:T(8,128)(2,1)S(1)}, bf16[848,128]{1,0:T(8,128)(2,1)S(1)}, u32[]{:S(2)}, u32[]{:S(2)}) %collective-permute-start.34) | collective-permute-done | bytes 217120 | tf_op jit(solution)/shard_map/ppermute | solution.py:647
  (127 shorter events, 36.0 us)
Async XLA Ops:
  6.0 13.1 %collective-permute-start.5 = (bf16[80,1664]{1,0:T(8,128)(2,1)}, bf16[80,1664]{1,0:T(8,128)(2,1)S(1)}, u32[]{:S(2)}, u32[]{:S(2)}) collective-permute-start(bf16[80,1664]{1,0:T(8,128)(2,1)} %get-tuple-element.95), channel_id=1, source_target_pairs={{0,8},{1,9},{2,10},{3,11},{4,12},{5,13},{6,14},{7,15},{8,16},{9,17... | collective-permute-start | bytes 798728 | tf_op jit(solution)/shard_map/ppermute | solution.py:505
  7.6 13.1 %collective-permute-start.1 = (bf16[80,1664]{1,0:T(8,128)(2,1)}, bf16[80,1664]{1,0:T(8,128)(2,1)S(1)}, u32[]{:S(2)}, u32[]{:S(2)}) collective-permute-start(bf16[80,1664]{1,0:T(8,128)(2,1)} %get-tuple-element.92), channel_id=1, source_target_pairs={{0,4},{1,5},{2,3},{3,2},{4,0},{5,1},{6,7},{7,6},{8,12},{9,13},{10,... | collective-permute-start | bytes 798728 | tf_op jit(solution)/shard_map/ppermute | solution.py:505
  11.7 9.5 %collective-permute-start.2 = (bf16[80,1664]{1,0:T(8,128)(2,1)S(1)}, bf16[80,1664]{1,0:T(8,128)(2,1)S(1)}, u32[]{:S(2)}, u32[]{:S(2)}) collective-permute-start(bf16[80,1664]{1,0:T(8,128)(2,1)S(1)} %collective-permute-done), channel_id=1, source_target_pairs={{0,4},{1,5},{2,3},{3,2},{4,0},{5,1},{6,7},{7,6},{8,12},{9,13},{10,... | collective-permute-start | bytes 798728 | tf_op jit(solution)/shard_map/ppermute | solution.py:505
  15.2 13.5 %collective-permute-start.18 = (bf16[80,1664]{1,0:T(8,128)(2,1)}, bf16[80,1664]{1,0:T(8,128)(2,1)S(1)}, u32[]{:S(2)}, u32[]{:S(2)}) collective-permute-start(bf16[80,1664]{1,0:T(8,128)(2,1)} %get-tuple-element.110), channel_id=1, source_target_pairs={{0,16},{1,17},{2,18},{3,19},{4,20},{5,21},{6,22},{7,23},{8,24},{9,... | collective-permute-start | bytes 798728 | tf_op jit(solution)/shard_map/ppermute | solution.py:505
  17.8 8.9 %collective-permute-start.11 = (bf16[80,1664]{1,0:T(8,128)(2,1)}, bf16[80,1664]{1,0:T(8,128)(2,1)S(1)}, u32[]{:S(2)}, u32[]{:S(2)}) collective-permute-start(bf16[80,1664]{1,0:T(8,128)(2,1)} %get-tuple-element.101), channel_id=1, source_target_pairs={{0,24},{1,25},{2,26},{3,27},{4,28},{5,29},{6,30},{7,31},{8,0},{9,1... | collective-permute-start | bytes 798728 | tf_op jit(solution)/shard_map/ppermute | solution.py:505
  19.2 9.5 %collective-permute-start.6 = (bf16[80,1664]{1,0:T(8,128)(2,1)S(1)}, bf16[80,1664]{1,0:T(8,128)(2,1)S(1)}, u32[]{:S(2)}, u32[]{:S(2)}) collective-permute-start(bf16[80,1664]{1,0:T(8,128)(2,1)S(1)} %collective-permute-done.5), channel_id=1, source_target_pairs={{0,1},{1,0},{2,6},{3,7},{4,5},{5,4},{6,2},{7,3},{8,9},{9,8},{10,14... | collective-permute-start | bytes 798728 | tf_op jit(solution)/shard_map/ppermute | solution.py:505
  22.3 20.3 %collective-permute-start.3 = (bf16[320,1664]{1,0:T(8,128)(2,1)S(1)}, bf16[320,1664]{1,0:T(8,128)(2,1)S(1)}, u32[]{:S(2)}, u32[]{:S(2)}) collective-permute-start(bf16[320,1664]{1,0:T(8,128)(2,1)S(1)} %pad_maximum_fusion.near.refs_0_.refs_1_), channel_id=1, source_target_pairs={{0,2},{1,3},{2,0},{3,1},{4,6},{5,7},{6,4},{7,5},{8,10},{9,11},{10,... | collective-permute-start | bytes 3194888 | tf_op jit(solution)/shard_map/ppermute | solution.py:505
  26.7 9.2 %collective-permute-start.12 = (bf16[80,1664]{1,0:T(8,128)(2,1)S(1)}, bf16[80,1664]{1,0:T(8,128)(2,1)S(1)}, u32[]{:S(2)}, u32[]{:S(2)}) collective-permute-start(bf16[80,1664]{1,0:T(8,128)(2,1)S(1)} %collective-permute-done.11), channel_id=1, source_target_pairs={{0,1},{1,0},{2,6},{3,7},{4,5},{5,4},{6,2},{7,3},{8,9},{9,8},{10,14... | collective-permute-start | bytes 798728 | tf_op jit(solution)/shard_map/ppermute | solution.py:505
  28.7 9.2 %collective-permute-start.8 = (bf16[80,1664]{1,0:T(8,128)(2,1)S(1)}, bf16[80,1664]{1,0:T(8,128)(2,1)S(1)}, u32[]{:S(2)}, u32[]{:S(2)}) collective-permute-start(bf16[80,1664]{1,0:T(8,128)(2,1)S(1)} %collective-permute-done.6), channel_id=1, source_target_pairs={{0,4},{1,5},{2,3},{3,2},{4,0},{5,1},{6,7},{7,6},{8,12},{9,13},{10,... | collective-permute-start | bytes 798728 | tf_op jit(solution)/shard_map/ppermute | solution.py:505
  30.0 11.6 %collective-permute-start.19 = (bf16[80,1664]{1,0:T(8,128)(2,1)S(1)}, bf16[80,1664]{1,0:T(8,128)(2,1)S(1)}, u32[]{:S(2)}, u32[]{:S(2)}) collective-permute-start(bf16[80,1664]{1,0:T(8,128)(2,1)S(1)} %collective-permute-done.18), channel_id=1, source_target_pairs={{0,1},{1,0},{2,6},{3,7},{4,5},{5,4},{6,2},{7,3},{8,9},{9,8},{10,14... | collective-permute-start | bytes 798728 | tf_op jit(solution)/shard_map/ppermute | solution.py:505
  30.4 19.0 %collective-permute-start.13 = (bf16[80,1664]{1,0:T(8,128)(2,1)S(1)}, bf16[80,1664]{1,0:T(8,128)(2,1)S(1)}, u32[]{:S(2)}, u32[]{:S(2)}) collective-permute-start(bf16[80,1664]{1,0:T(8,128)(2,1)S(1)} %collective-permute-done.11), channel_id=1, source_target_pairs={{0,4},{1,5},{2,3},{3,2},{4,0},{5,1},{6,7},{7,6},{8,12},{9,13},{10,... | collective-permute-start | bytes 798728 | tf_op jit(solution)/shard_map/ppermute | solution.py:505
  35.9 11.8 %collective-permute-start.20 = (bf16[80,1664]{1,0:T(8,128)(2,1)S(1)}, bf16[80,1664]{1,0:T(8,128)(2,1)S(1)}, u32[]{:S(2)}, u32[]{:S(2)}) collective-permute-start(bf16[80,1664]{1,0:T(8,128)(2,1)S(1)} %collective-permute-done.18), channel_id=1, source_target_pairs={{0,4},{1,5},{2,3},{3,2},{4,0},{5,1},{6,7},{7,6},{8,12},{9,13},{10,... | collective-permute-start | bytes 798728 | tf_op jit(solution)/shard_map/ppermute | solution.py:505
  37.9 11.4 %collective-permute-start.14 = (bf16[80,1664]{1,0:T(8,128)(2,1)S(1)}, bf16[80,1664]{1,0:T(8,128)(2,1)S(1)}, u32[]{:S(2)}, u32[]{:S(2)}) collective-permute-start(bf16[80,1664]{1,0:T(8,128)(2,1)S(1)} %collective-permute-done.12), channel_id=1, source_target_pairs={{0,4},{1,5},{2,3},{3,2},{4,0},{5,1},{6,7},{7,6},{8,12},{9,13},{10,... | collective-permute-start | bytes 798728 | tf_op jit(solution)/shard_map/ppermute | solution.py:505
  53.0 29.6 %collective-permute-start.4 = (bf16[320,1664]{1,0:T(8,128)(2,1)S(1)}, bf16[320,1664]{1,0:T(8,128)(2,1)S(1)}, u32[]{:S(2)}, u32[]{:S(2)}) collective-permute-start(bf16[320,1664]{1,0:T(8,128)(2,1)S(1)} %get-tuple-element.94), channel_id=1, source_target_pairs={{0,2},{1,3},{2,0},{3,1},{4,6},{5,7},{6,4},{7,5},{8,10},{9,11},{10,... | collective-permute-start | bytes 3194888 | tf_op jit(solution)/shard_map/ppermute | solution.py:505
  57.2 8.8 %collective-permute-start.16 = (bf16[144,1664]{1,0:T(8,128)(2,1)S(1)}, bf16[144,1664]{1,0:T(8,128)(2,1)S(1)}, u32[]{:S(2)}, u32[]{:S(2)}) collective-permute-start(bf16[144,1664]{1,0:T(8,128)(2,1)S(1)} %pad_maximum_fusion.4), channel_id=1, source_target_pairs={{0,1},{1,0},{2,6},{3,7},{4,5},{5,4},{6,2},{7,3},{8,9},{9,8},{10,14... | collective-permute-start | bytes 1437704 | tf_op jit(solution)/shard_map/ppermute | solution.py:505
  63.6 11.3 %collective-permute-start.24 = (bf16[144,1664]{1,0:T(8,128)(2,1)S(1)}, bf16[144,1664]{1,0:T(8,128)(2,1)S(1)}, u32[]{:S(2)}, u32[]{:S(2)}) collective-permute-start(bf16[144,1664]{1,0:T(8,128)(2,1)S(1)} %pad_maximum_fusion.5), channel_id=1, source_target_pairs={{0,1},{1,0},{2,6},{3,7},{4,5},{5,4},{6,2},{7,3},{8,9},{9,8},{10,14... | collective-permute-start | bytes 1437704 | tf_op jit(solution)/shard_map/ppermute | solution.py:505
  66.1 10.7 %collective-permute-start.23 = (bf16[72,1664]{1,0:T(8,128)(2,1)S(1)}, bf16[72,1664]{1,0:T(8,128)(2,1)S(1)}, u32[]{:S(2)}, u32[]{:S(2)}) collective-permute-start(bf16[72,1664]{1,0:T(8,128)(2,1)S(1)} %add_convert_fusion.7), channel_id=1, source_target_pairs={{0,4},{1,5},{2,3},{3,2},{4,0},{5,1},{6,7},{7,6},{8,12},{9,13},{10,... | collective-permute-start | bytes 718856 | tf_op jit(solution)/shard_map/ppermute | solution.py:505
  68.6 15.7 %collective-permute-start.28 = (bf16[144,1664]{1,0:T(8,128)(2,1)S(1)}, bf16[144,1664]{1,0:T(8,128)(2,1)S(1)}, u32[]{:S(2)}, u32[]{:S(2)}) collective-permute-start(bf16[144,1664]{1,0:T(8,128)(2,1)S(1)} %pad_maximum_fusion.6), channel_id=1, source_target_pairs={{0,1},{1,0},{2,6},{3,7},{4,5},{5,4},{6,2},{7,3},{8,9},{9,8},{10,14... | collective-permute-start | bytes 1437704 | tf_op jit(solution)/shard_map/ppermute | solution.py:505
  75.0 10.0 %collective-permute-start.27 = (bf16[72,1664]{1,0:T(8,128)(2,1)S(1)}, bf16[72,1664]{1,0:T(8,128)(2,1)S(1)}, u32[]{:S(2)}, u32[]{:S(2)}) collective-permute-start(bf16[72,1664]{1,0:T(8,128)(2,1)S(1)} %add_convert_fusion.6), channel_id=1, source_target_pairs={{0,4},{1,5},{2,3},{3,2},{4,0},{5,1},{6,7},{7,6},{8,12},{9,13},{10,... | collective-permute-start | bytes 718856 | tf_op jit(solution)/shard_map/ppermute | solution.py:505
  77.1 30.8 %collective-permute-start.31 = (bf16[72,1664]{1,0:T(8,128)(2,1)S(1)}, bf16[72,1664]{1,0:T(8,128)(2,1)S(1)}, u32[]{:S(2)}, u32[]{:S(2)}) collective-permute-start(bf16[72,1664]{1,0:T(8,128)(2,1)S(1)} %multiply_convert_fusion.3), channel_id=1, source_target_pairs={{0,24},{1,25},{2,26},{3,27},{4,28},{5,29},{6,30},{7,31},{8,0},{9,1... | collective-permute-start | bytes 718856 | tf_op jit(solution)/shard_map/ppermute | solution.py:505
  83.0 9.8 %collective-permute-start.26 = (bf16[144,1664]{1,0:T(8,128)(2,1)S(1)}, bf16[144,1664]{1,0:T(8,128)(2,1)S(1)}, u32[]{:S(2)}, u32[]{:S(2)}) collective-permute-start(bf16[144,1664]{1,0:T(8,128)(2,1)S(1)} %pad_maximum_fusion.7), channel_id=1, source_target_pairs={{0,1},{1,0},{2,6},{3,7},{4,5},{5,4},{6,2},{7,3},{8,9},{9,8},{10,14... | collective-permute-start | bytes 1437704 | tf_op jit(solution)/shard_map/ppermute | solution.py:505
  85.1 22.9 %collective-permute-start.33 = (bf16[72,1664]{1,0:T(8,128)(2,1)S(1)}, bf16[72,1664]{1,0:T(8,128)(2,1)S(1)}, u32[]{:S(2)}, u32[]{:S(2)}) collective-permute-start(bf16[72,1664]{1,0:T(8,128)(2,1)S(1)} %multiply_convert_fusion.2), channel_id=1, source_target_pairs={{0,8},{1,9},{2,10},{3,11},{4,12},{5,13},{6,14},{7,15},{8,16},{9,17... | collective-permute-start | bytes 718856 | tf_op jit(solution)/shard_map/ppermute | solution.py:505
  92.9 14.9 %collective-permute-start.29 = (bf16[72,1664]{1,0:T(8,128)(2,1)S(1)}, bf16[72,1664]{1,0:T(8,128)(2,1)S(1)}, u32[]{:S(2)}, u32[]{:S(2)}) collective-permute-start(bf16[72,1664]{1,0:T(8,128)(2,1)S(1)} %add_convert_fusion.4), channel_id=1, source_target_pairs={{0,4},{1,5},{2,3},{3,2},{4,0},{5,1},{6,7},{7,6},{8,12},{9,13},{10,... | collective-permute-start | bytes 718856 | tf_op jit(solution)/shard_map/ppermute | solution.py:505
  93.1 14.9 %collective-permute-start.32 = (bf16[72,1664]{1,0:T(8,128)(2,1)S(1)}, bf16[72,1664]{1,0:T(8,128)(2,1)S(1)}, u32[]{:S(2)}, u32[]{:S(2)}) collective-permute-start(bf16[72,1664]{1,0:T(8,128)(2,1)S(1)} %multiply_convert_fusion.1), channel_id=1, source_target_pairs={{0,16},{1,17},{2,18},{3,19},{4,20},{5,21},{6,22},{7,23},{8,24},{9,... | collective-permute-start | bytes 718856 | tf_op jit(solution)/shard_map/ppermute | solution.py:505
  (33 other events, 223.1 us)

commit v5 on v4

--- a/solution.py
+++ b/solution.py
@@ -139,8 +139,9 @@
     "Z 3",
     "Z 2",
     "D2 0",
+    "L 0",
     "D1 1",
-    "SEL 0",
+    "SEL 0 L0",
     "D2 1",
     "D1 2",
     "SEL 1",
@@ -156,9 +157,9 @@
     "E 3 R11",
     "CUT 0",
     "R1 2 E3",
-    "R2 1 R12",
-    "R1 3 R21",
-    "R2 2 R13",
+    "R1 3 R12",
+    "R2 1 R13",
+    "R2 2 R21",
     "H 1 R22",
     "R1 0 H1",
     "R2 3 R10",
@@ -345,59 +346,110 @@
 
 
 def weight_kernel(kept, *refs):
-    group_count = (len(refs) - 4) // 6
-    parts, hiddens = refs[: 4 * group_count], refs[4 * group_count : 6 * group_count]
-    grad_in, grad_out, act, pre = refs[6 * group_count :]
-
-    @pl.when(pl.program_id(0) == 0)
-    def _():
-        keep = kept[:, 0:1]
-        act[...] = jnp.concatenate([one[...] for one in hiddens[::2]], axis=0) * keep
-        pre[...] = jnp.concatenate([one[...] for one in hiddens[1::2]], axis=0) * keep
-
+    group_count = (len(refs) - 10) // 4
+    pieces, out_at = refs[: 4 * group_count], refs[4 * group_count : 4 * group_count + 2]
+    rows, grads, act, pre, grad_in, grad_out, sems, out_sems = refs[4 * group_count + 2 :]
+    steps, base = ([], [], [], []), 0
+    for g in range(group_count):
+        near, far, act_at, pre_at = pieces[4 * g : 4 * g + 4]
+        count = near.shape[0]
+        half = count // 2
+        for slot, (whole, to) in enumerate(((pre_at, pre), (act_at, act))):
+            steps[2 * slot].append(
+                pltpu.make_async_copy(whole, to.at[pl.ds(base, count)], sems.at[g, 3 * slot])
+            )
+        for part, whole in enumerate((near, far)):
+            for kind, to in enumerate((rows, grads)):
+                steps[2 * kind + 1].append(
+                    pltpu.make_async_copy(
+                        whole.at[pl.ds(kind * half, half)],
+                        to.at[pl.ds(base + part * half, half)],
+                        sems.at[g, 3 * kind + 1 + part],
+                    )
+                )
+        base += count
+    for copies in steps:
+        for copy in copies:
+            copy.start()
     contract_first = (((0,), (0,)), ((), ()))
-    rows = jnp.concatenate([one[...] for one in parts[::2]], axis=0)
-    grads = jnp.concatenate([one[...] for one in parts[1::2]], axis=0)
-    grad_in[...] = lax.dot_general(
-        rows, pre[...], contract_first, preferred_element_type=jnp.float32
-    ).astype(jnp.bfloat16)
-    grad_out[...] = lax.dot_general(
-        act[...], grads, contract_first, preferred_element_type=jnp.float32
-    ).astype(jnp.bfloat16)
+    keep = kept[:, 0:1]
+    width = rows.shape[1]
+    sent = []
+
+    for copy in steps[0]:
+        copy.wait()
+    pre[...] = pre[...] * keep
+    for copy in steps[1]:
+        copy.wait()
+    for first in range(0, width, 256):
+        span = slice(first, min(width, first + 256))
+        grad_in[span] = lax.dot_general(
+            rows[:, span], pre[...], contract_first, preferred_element_type=jnp.float32
+        ).astype(jnp.bfloat16)
+    sent.append(pltpu.make_async_copy(grad_in, out_at[0], out_sems.at[0]))
+    sent[-1].start()
+    for copy in steps[2]:
+        copy.wait()
+    act[...] = act[...] * keep
+    for copy in steps[3]:
+        copy.wait()
+    for first in range(0, width, 256):
+        span = slice(first, min(width, first + 256))
+        grad_out[:, span] = lax.dot_general(
+            act[...], grads[:, span], contract_first, preferred_element_type=jnp.float32
+        ).astype(jnp.bfloat16)
+    sent.append(pltpu.make_async_copy(grad_out, out_at[1], out_sems.at[1]))
+    sent[-1].start()
+    for copy in sent:
+        copy.wait()
 
 
 def weight_call(kept, saved):
-    width, hidden = saved[0][0].shape[1], saved[0][2].shape[1]
+    pieces = [piece for one in saved for piece in one]
+    width, hidden = pieces[0].shape[1], pieces[2].shape[1]
     all_rows = sum(one[2].shape[0] for one in saved)
-    tile = 256
-    operands, specs = [], []
-    for near, far, _, _ in saved:
-        for whole in (near, far):
-            for kind in range(2):
-                operands.append(whole)
-                specs.append(
-                    pl.BlockSpec((whole.shape[0] // 2, tile), functools.partial(lambda kind, j: (kind, j), kind))
-                )
-    for _, _, act, pre in saved:
-        for whole in (act, pre):
-            operands.append(whole)
-            specs.append(pl.BlockSpec(whole.shape, lambda j: (0, 0)))
+    vmem, anywhere = pl.BlockSpec(memory_space=pltpu.VMEM), pl.BlockSpec(memory_space=pl.ANY)
     return pl.pallas_call(
         weight_kernel,
-        grid=(pl.cdiv(width, tile),),
         out_shape=(
             jax.ShapeDtypeStruct((width, hidden), jnp.bfloat16),
             jax.ShapeDtypeStruct((hidden, width), jnp.bfloat16),
         ),
-        in_specs=[pl.BlockSpec(kept.shape, lambda j: (0, 0))] + specs,
-        out_specs=(
-            pl.BlockSpec((tile, hidden), lambda j: (j, 0)),
-            pl.BlockSpec((hidden, tile), lambda j: (0, j)),
-        ),
-        scratch_shapes=[pltpu.VMEM((all_rows, hidden), jnp.bfloat16)] * 2,
+        in_specs=[vmem] + [anywhere] * len(pieces),
+        out_specs=(anywhere,) * 2,
+        scratch_shapes=[pltpu.VMEM((all_rows, width), jnp.bfloat16)] * 2
+        + [pltpu.VMEM((all_rows, hidden), jnp.bfloat16)] * 2
+        + [pltpu.VMEM((width, hidden), jnp.bfloat16), pltpu.VMEM((hidden, width), jnp.bfloat16)]
+        + [pltpu.SemaphoreType.DMA((len(saved), 6)), pltpu.SemaphoreType.DMA((2,))],
         compiler_params=pltpu.CompilerParams(vmem_limit_bytes=WLIM * MIB),
         cost_estimate=pl.CostEstimate(flops=0, bytes_accessed=0, transcendentals=0),
-    )(kept, *operands)
+    )(kept, *pieces)
+
+
+def load_kernel(in_at, out_at, matrix_in, matrix_out, sems):
+    copies = [
+        pltpu.make_async_copy(in_at, matrix_in, sems.at[0]),
+        pltpu.make_async_copy(out_at, matrix_out, sems.at[1]),
+    ]
+    for copy in copies:
+        copy.start()
+    for copy in copies:
+        copy.wait()
+
+
+def load_call(matrix_in, matrix_out):
+    vmem, anywhere = pl.BlockSpec(memory_space=pltpu.VMEM), pl.BlockSpec(memory_space=pl.ANY)
+    return pl.pallas_call(
+        load_kernel,
+        out_shape=tuple(
+            jax.ShapeDtypeStruct(one.shape, one.dtype) for one in (matrix_in, matrix_out)
+        ),
+        in_specs=[anywhere] * 2,
+        out_specs=(vmem,) * 2,
+        scratch_shapes=[pltpu.SemaphoreType.DMA((2,))],
+        compiler_params=pltpu.CompilerParams(vmem_limit_bytes=8 * MIB),
+        cost_estimate=pl.CostEstimate(flops=0, bytes_accessed=0, transcendentals=0),
+    )(matrix_in, matrix_out)
 
 
 def token_kernel(gates, places, cotangent, *refs):
@@ -571,7 +623,7 @@
         one["far"] = send(one["near"], other_core)
         return [one["near"]]
 
-    def expert_work(g, made):
+    def expert_work(g, made, matrix_in, matrix_out):
         one = state[g]
         near_rows, far_rows = step(made, one["near"], one["far"])
         near_parts, far_parts, act, pre = expert_call(near_rows, far_rows, matrix_in, matrix_out)
@@ -625,8 +677,11 @@
             here = spread_second(g, made)
         elif name == "SEL":
             here = gather_near(g, made)
+        elif name == "L":
+            matrix_in, matrix_out = load_call(matrix_in, matrix_out)
+            here = [matrix_out]
         elif name == "E":
-            here = expert_work(g, made)
+            here = expert_work(g, made, matrix_in, matrix_out)
         elif name == "CUT":
             pieces = [piece for one in state for piece in one["saved"][:2]]
             kept, mine = cut_call(step(made, *pieces), slot_count, block_rows, capacity)

time: 117 us -> 115 us (0.983)
  starting transfers between devices: 54.2 us -> 43 us
  waiting for transfers between devices: 26.4 us -> 37.2 us
    ppermute x34, starting transfers between devices: 52.8 us -> 42.1 us  [send(): return lax.ppermute(array, ('dp', 'rep'), permutation(move))]
    ppermute x34, waiting for transfers between devices: 21.9 us -> 32.1 us  [send(): return lax.ppermute(array, ('dp', 'rep'), permutation(move))]
    pallas_call x1 -> x2, Pallas kernels: 11.3 us -> 10.7 us  [the longest x1 10.2 us: weight_call(): pl.pallas_call(weight_kernel, out_shape=(jax.ShapeDtypeStruct((width, hid...]
    unnamed x44 -> x46, local copies, waits for them, and re-layouts: 4.05 us -> 4.35 us
  transfers between devices with their start and end apart: 35 -> 35, of which waited for: 12 -> 10; matrix products, arithmetic and copies ran while one was open for 4% -> 3% of each run, Pallas kernels for 19% -> 19%
where the time goes in v5:
time: 115 us
  starting transfers between devices  43 us (37%)
  waiting for transfers between devices  37.2 us (32%)
  Pallas kernels  25.7 us (22%)
  local copies, waits for them, and re-layouts  4.49 us (4%)
  other arithmetic  3.18 us (3%)
  between operations  1.22 us (1%)
    ppermute x34, starting transfers between devices, send(): return lax.ppermute(array, ('dp', 'rep'), permutation(move))  42.1 us
    ppermute x34, waiting for transfers between devices, send(): return lax.ppermute(array, ('dp', 'rep'), permutation(move))  32.1 us
    pallas_call x1, Pallas kernels, weight_call(): pl.pallas_call(weight_kernel, out_shape=(jax.ShapeDtypeStruct((width, hid...  10.2 us
    pallas_call x4, Pallas kernels, expert_call(): pl.pallas_call(expert_kernel, out_shape=(jax.ShapeDtypeStruct((rows, widt...  10.2 us
    ppermute x1, waiting for transfers between devices, plane_body(): got = lax.ppermute(away, 'rep', [(0, 1), (1, 0)])  5.09 us
    unnamed x46, local copies, waits for them, and re-layouts  4.35 us
    pallas_call x1, Pallas kernels, start_call(): pl.pallas_call(functools.partial(start_kernel, experts), out_shape=(jax.S...  2.39 us
  transfers between devices with their start and end apart: 35, of which 10 were waited for; matrix products, arithmetic and copies ran while one was open for 3% of the time, Pallas kernels for 19%

profile of v5, /device:TPU:0, one launch (start us, length us, event | category | flops | bytes accessed | tf_op | source)
XLA Modules:
  0.0 114.8 jit_solution(6213222319528114345)
XLA Ops:
  0.6 2.4 %shard_map.110 = (bf16[2,4,72,128]{3,2,1,0:T(8,128)(2,1)}, bf16[80,1664]{1,0:T(8,128)(2,1)}, bf16[80,1664]{1,0:T(8,128)(2,1)}, bf16[80,1664]{1,0:T(8,128)(2,1)}, bf16[80,1664]{1,0:T(8,128)(2,1)}) custom-call(s32[2,128]{1,0:T(2,128)} %bitcast.14, s32[1,128]{1,0:T(1,128)} %bitcast.15, f32[2,128]{1,0:T(2,128)} %bitcast.12, bf16[128,1664]{1,0:T(8,128)(2,1)} %tokens_at.1, ...), custom_call_target="tpu_custom_call" | custom-call | tf_op jit(solution)/shard_map/pallas_call | solution.py:275
  3.0 3.0 %collective-permute-start = (bf16[80,1664]{1,0:T(8,128)(2,1)}, bf16[80,1664]{1,0:T(8,128)(2,1)S(1)}, u32[]{:S(2)}, u32[]{:S(2)}) collective-permute-start(bf16[80,1664]{1,0:T(8,128)(2,1)} %get-tuple-element.100), channel_id=1, source_target_pairs={{0,1},{1,0},{2,6},{3,7},{4,5},{5,4},{6,2},{7,3},{8,9},{9,8},{10,14... | collective-permute-start | bytes 798728 | tf_op jit(solution)/shard_map/ppermute | solution.py:557
  6.0 1.6 %collective-permute-start.5 = (bf16[80,1664]{1,0:T(8,128)(2,1)}, bf16[80,1664]{1,0:T(8,128)(2,1)S(1)}, u32[]{:S(2)}, u32[]{:S(2)}) collective-permute-start(bf16[80,1664]{1,0:T(8,128)(2,1)} %get-tuple-element.107), channel_id=1, source_target_pairs={{0,8},{1,9},{2,10},{3,11},{4,12},{5,13},{6,14},{7,15},{8,16},{9,17... | collective-permute-start | bytes 798728 | tf_op jit(solution)/shard_map/ppermute | solution.py:557
  7.6 1.5 %collective-permute-start.1 = (bf16[80,1664]{1,0:T(8,128)(2,1)}, bf16[80,1664]{1,0:T(8,128)(2,1)S(1)}, u32[]{:S(2)}, u32[]{:S(2)}) collective-permute-start(bf16[80,1664]{1,0:T(8,128)(2,1)} %get-tuple-element.100), channel_id=1, source_target_pairs={{0,4},{1,5},{2,3},{3,2},{4,0},{5,1},{6,7},{7,6},{8,12},{9,13},{10,... | collective-permute-start | bytes 798728 | tf_op jit(solution)/shard_map/ppermute | solution.py:557
  9.1 2.5 %collective-permute-done = bf16[80,1664]{1,0:T(8,128)(2,1)S(1)} collective-permute-done((bf16[80,1664]{1,0:T(8,128)(2,1)}, bf16[80,1664]{1,0:T(8,128)(2,1)S(1)}, u32[]{:S(2)}, u32[]{:S(2)}) %collective-permute-start) | collective-permute-done | bytes 266272 | tf_op jit(solution)/shard_map/ppermute | solution.py:557
  11.7 3.6 %collective-permute-start.2 = (bf16[80,1664]{1,0:T(8,128)(2,1)S(1)}, bf16[80,1664]{1,0:T(8,128)(2,1)S(1)}, u32[]{:S(2)}, u32[]{:S(2)}) collective-permute-start(bf16[80,1664]{1,0:T(8,128)(2,1)S(1)} %collective-permute-done), channel_id=1, source_target_pairs={{0,4},{1,5},{2,3},{3,2},{4,0},{5,1},{6,7},{7,6},{8,12},{9,13},{10,... | collective-permute-start | bytes 798728 | tf_op jit(solution)/shard_map/ppermute | solution.py:557
  15.2 3.0 %collective-permute-start.11 = (bf16[80,1664]{1,0:T(8,128)(2,1)}, bf16[80,1664]{1,0:T(8,128)(2,1)S(1)}, u32[]{:S(2)}, u32[]{:S(2)}) collective-permute-start(bf16[80,1664]{1,0:T(8,128)(2,1)} %get-tuple-element.113), channel_id=1, source_target_pairs={{0,24},{1,25},{2,26},{3,27},{4,28},{5,29},{6,30},{7,31},{8,0},{9,1... | collective-permute-start | bytes 798728 | tf_op jit(solution)/shard_map/ppermute | solution.py:557
  21.8 1.6 %collective-permute-start.6 = (bf16[80,1664]{1,0:T(8,128)(2,1)S(1)}, bf16[80,1664]{1,0:T(8,128)(2,1)S(1)}, u32[]{:S(2)}, u32[]{:S(2)}) collective-permute-start(bf16[80,1664]{1,0:T(8,128)(2,1)S(1)} %collective-permute-done.5), channel_id=1, source_target_pairs={{0,1},{1,0},{2,6},{3,7},{4,5},{5,4},{6,2},{7,3},{8,9},{9,8},{10,14... | collective-permute-start | bytes 798728 | tf_op jit(solution)/shard_map/ppermute | solution.py:557
  25.5 8.2 %collective-permute-done.17 = bf16[80,1664]{1,0:T(8,128)(2,1)S(1)} collective-permute-done((bf16[80,1664]{1,0:T(8,128)(2,1)}, bf16[80,1664]{1,0:T(8,128)(2,1)S(1)}, u32[]{:S(2)}, u32[]{:S(2)}) %collective-permute-start.17) | collective-permute-done | bytes 266272 | tf_op jit(solution)/shard_map/ppermute | solution.py:557
  37.4 2.8 %collective-permute-done.8 = bf16[80,1664]{1,0:T(8,128)(2,1)S(1)} collective-permute-done((bf16[80,1664]{1,0:T(8,128)(2,1)S(1)}, bf16[80,1664]{1,0:T(8,128)(2,1)S(1)}, u32[]{:S(2)}, u32[]{:S(2)}) %collective-permute-start.8) | collective-permute-done | bytes 266272 | tf_op jit(solution)/shard_map/ppermute | solution.py:557
  40.7 2.9 %collective-permute-done.18 = bf16[80,1664]{1,0:T(8,128)(2,1)S(1)} collective-permute-done((bf16[80,1664]{1,0:T(8,128)(2,1)S(1)}, bf16[80,1664]{1,0:T(8,128)(2,1)S(1)}, u32[]{:S(2)}, u32[]{:S(2)}) %collective-permute-start.18) | collective-permute-done | bytes 266272 | tf_op jit(solution)/shard_map/ppermute | solution.py:557
  43.6 1.5 %collective-permute-start.20 = (bf16[80,1664]{1,0:T(8,128)(2,1)S(1)}, bf16[80,1664]{1,0:T(8,128)(2,1)S(1)}, u32[]{:S(2)}, u32[]{:S(2)}) collective-permute-start(bf16[80,1664]{1,0:T(8,128)(2,1)S(1)} %collective-permute-done.18), channel_id=1, source_target_pairs={{0,4},{1,5},{2,3},{3,2},{4,0},{5,1},{6,7},{7,6},{8,12},{9,13},{10,... | collective-permute-start | bytes 798728 | tf_op jit(solution)/shard_map/ppermute | solution.py:557
  45.5 2.5 %shard_map.112 = (bf16[320,1664]{1,0:T(8,128)(2,1)S(1)}, bf16[320,1664]{1,0:T(8,128)(2,1)S(1)}, bf16[320,512]{1,0:T(8,128)(2,1)S(1)}, bf16[320,512]{1,0:T(8,128)(2,1)S(1)}) custom-call(bf16[320,1664]{1,0:T(8,128)(2,1)S(1)} %pad_maximum_fusion.near.refs_0_, bf16[320,1664]{1,0:T(8,128)(2,1)S(1)} %collective-permute-done.3.far.refs_1_, ...), custom_call_target="tpu_custom_call" | custom-call | tf_op jit(solution)/shard_map/pallas_call | solution.py:199
  48.0 3.6 %collective-permute-done.20 = bf16[80,1664]{1,0:T(8,128)(2,1)S(1)} collective-permute-done((bf16[80,1664]{1,0:T(8,128)(2,1)S(1)}, bf16[80,1664]{1,0:T(8,128)(2,1)S(1)}, u32[]{:S(2)}, u32[]{:S(2)}) %collective-permute-start.20) | collective-permute-done | bytes 266272 | tf_op jit(solution)/shard_map/ppermute | solution.py:557
  52.1 2.5 %shard_map.113 = (bf16[320,1664]{1,0:T(8,128)(2,1)S(1)}, bf16[320,1664]{1,0:T(8,128)(2,1)S(1)}, bf16[320,512]{1,0:T(8,128)(2,1)S(1)}, bf16[320,512]{1,0:T(8,128)(2,1)S(1)}) custom-call(bf16[320,1664]{1,0:T(8,128)(2,1)S(1)} %pad_maximum_fusion.1.near.refs_2_.refs_4_, bf16[320,1664]{1,0:T(8,128)(2,1)S(1)} %collective-permute-done.9.far.refs_3_.refs_5_, ...), custom_call_target="tpu_custom_call" | custom-call | tf_op jit(solution)/shard_map/pallas_call | solution.py:199
  56.0 2.5 %shard_map.114 = (bf16[320,1664]{1,0:T(8,128)(2,1)S(1)}, bf16[320,1664]{1,0:T(8,128)(2,1)S(1)}, bf16[320,512]{1,0:T(8,128)(2,1)S(1)}, bf16[320,512]{1,0:T(8,128)(2,1)S(1)}) custom-call(bf16[320,1664]{1,0:T(8,128)(2,1)S(1)} %pad_maximum_fusion.2.near.refs_4_.refs_8_, bf16[320,1664]{1,0:T(8,128)(2,1)S(1)} %collective-permute-done.15.far.refs_5_.refs_9_, ...), custom_call_target="tpu_custom_call" | custom-call | tf_op jit(solution)/shard_map/pallas_call | solution.py:199
  60.5 2.5 %shard_map.115 = (bf16[320,1664]{1,0:T(8,128)(2,1)S(1)}, bf16[320,1664]{1,0:T(8,128)(2,1)S(1)}, bf16[320,512]{1,0:T(8,128)(2,1)S(1)}, bf16[320,512]{1,0:T(8,128)(2,1)S(1)}) custom-call(bf16[320,1664]{1,0:T(8,128)(2,1)S(1)} %pad_maximum_fusion.3.near.refs_6_.refs_12_, bf16[320,1664]{1,0:T(8,128)(2,1)S(1)} %collective-permute-done.21.far.refs_7_.refs_13_, ...), custom_call_target="tpu_custom_call" | custom-call | tf_op jit(solution)/shard_map/pallas_call | solution.py:199
  69.0 7.1 %collective-permute-done.25 = bf16[144,1664]{1,0:T(8,128)(2,1)S(1)} collective-permute-done((bf16[144,1664]{1,0:T(8,128)(2,1)S(1)}, bf16[144,1664]{1,0:T(8,128)(2,1)S(1)}, u32[]{:S(2)}, u32[]{:S(2)}) %collective-permute-start.25) | collective-permute-done | bytes 479264 | tf_op jit(solution)/shard_map/ppermute | solution.py:557
  77.7 5.2 %collective-permute-start.31 = (bf16[72,1664]{1,0:T(8,128)(2,1)S(1)}, bf16[72,1664]{1,0:T(8,128)(2,1)S(1)}, u32[]{:S(2)}, u32[]{:S(2)}) collective-permute-start(bf16[72,1664]{1,0:T(8,128)(2,1)S(1)} %multiply_convert_fusion.3), channel_id=1, source_target_pairs={{0,24},{1,25},{2,26},{3,27},{4,28},{5,29},{6,30},{7,31},{8,0},{9,1... | collective-permute-start | bytes 718856 | tf_op jit(solution)/shard_map/ppermute | solution.py:557
  85.7 2.6 %collective-permute-start.33 = (bf16[72,1664]{1,0:T(8,128)(2,1)S(1)}, bf16[72,1664]{1,0:T(8,128)(2,1)S(1)}, u32[]{:S(2)}, u32[]{:S(2)}) collective-permute-start(bf16[72,1664]{1,0:T(8,128)(2,1)S(1)} %multiply_convert_fusion.2), channel_id=1, source_target_pairs={{0,8},{1,9},{2,10},{3,11},{4,12},{5,13},{6,14},{7,15},{8,16},{9,17... | collective-permute-start | bytes 718856 | tf_op jit(solution)/shard_map/ppermute | solution.py:557
  88.3 4.0 %collective-permute-done.26 = bf16[144,1664]{1,0:T(8,128)(2,1)S(1)} collective-permute-done((bf16[144,1664]{1,0:T(8,128)(2,1)S(1)}, bf16[144,1664]{1,0:T(8,128)(2,1)S(1)}, u32[]{:S(2)}, u32[]{:S(2)}) %collective-permute-start.26) | collective-permute-done | bytes 479264 | tf_op jit(solution)/shard_map/ppermute | solution.py:557
  93.7 2.1 %collective-permute-start.32 = (bf16[72,1664]{1,0:T(8,128)(2,1)S(1)}, bf16[72,1664]{1,0:T(8,128)(2,1)S(1)}, u32[]{:S(2)}, u32[]{:S(2)}) collective-permute-start(bf16[72,1664]{1,0:T(8,128)(2,1)S(1)} %multiply_convert_fusion.1), channel_id=1, source_target_pairs={{0,16},{1,17},{2,18},{3,19},{4,20},{5,21},{6,22},{7,23},{8,24},{9,... | collective-permute-start | bytes 718856 | tf_op jit(solution)/shard_map/ppermute | solution.py:557
  95.8 10.2 %shard_map.117 = (bf16[1664,512]{1,0:T(8,128)(2,1)}, bf16[512,1664]{1,0:T(8,128)(2,1)}) custom-call(bf16[1280,128]{1,0:T(8,128)(2,1)} %copy-done.19, bf16[320,1664]{1,0:T(8,128)(2,1)} %copy-done, bf16[320,1664]{1,0:T(8,128)(2,1)} %copy-done.4, bf16[320,512]{1,0:T(8,128)(2,1)} %copy-done.11, bf16[320,512]{1,0:T(8,128)(2,1)} %copy-done.12, ...), custom_call_target="tpu_custom_call" | custom-call | tf_op jit(solution)/shard_map/pallas_call | solution.py:412
  108.8 5.1 %collective-permute-done.34.got = bf16[848,128]{1,0:T(8,128)(2,1)S(1)} collective-permute-done((bf16[848,128]{1,0:T(8,128)(2,1)S(1)}, bf16[848,128]{1,0:T(8,128)(2,1)S(1)}, u32[]{:S(2)}, u32[]{:S(2)}) %collective-permute-start.34) | collective-permute-done | bytes 217120 | tf_op jit(solution)/shard_map/ppermute | solution.py:702
  (130 shorter events, 29.1 us)
Async XLA Ops:
  6.0 15.7 %collective-permute-start.5 = (bf16[80,1664]{1,0:T(8,128)(2,1)}, bf16[80,1664]{1,0:T(8,128)(2,1)S(1)}, u32[]{:S(2)}, u32[]{:S(2)}) collective-permute-start(bf16[80,1664]{1,0:T(8,128)(2,1)} %get-tuple-element.107), channel_id=1, source_target_pairs={{0,8},{1,9},{2,10},{3,11},{4,12},{5,13},{6,14},{7,15},{8,16},{9,17... | collective-permute-start | bytes 798728 | tf_op jit(solution)/shard_map/ppermute | solution.py:557
  7.6 15.7 %collective-permute-start.1 = (bf16[80,1664]{1,0:T(8,128)(2,1)}, bf16[80,1664]{1,0:T(8,128)(2,1)S(1)}, u32[]{:S(2)}, u32[]{:S(2)}) collective-permute-start(bf16[80,1664]{1,0:T(8,128)(2,1)} %get-tuple-element.100), channel_id=1, source_target_pairs={{0,4},{1,5},{2,3},{3,2},{4,0},{5,1},{6,7},{7,6},{8,12},{9,13},{10,... | collective-permute-start | bytes 798728 | tf_op jit(solution)/shard_map/ppermute | solution.py:557
  11.7 11.7 %collective-permute-start.2 = (bf16[80,1664]{1,0:T(8,128)(2,1)S(1)}, bf16[80,1664]{1,0:T(8,128)(2,1)S(1)}, u32[]{:S(2)}, u32[]{:S(2)}) collective-permute-start(bf16[80,1664]{1,0:T(8,128)(2,1)S(1)} %collective-permute-done), channel_id=1, source_target_pairs={{0,4},{1,5},{2,3},{3,2},{4,0},{5,1},{6,7},{7,6},{8,12},{9,13},{10,... | collective-permute-start | bytes 798728 | tf_op jit(solution)/shard_map/ppermute | solution.py:557
  15.2 9.9 %collective-permute-start.11 = (bf16[80,1664]{1,0:T(8,128)(2,1)}, bf16[80,1664]{1,0:T(8,128)(2,1)S(1)}, u32[]{:S(2)}, u32[]{:S(2)}) collective-permute-start(bf16[80,1664]{1,0:T(8,128)(2,1)} %get-tuple-element.113), channel_id=1, source_target_pairs={{0,24},{1,25},{2,26},{3,27},{4,28},{5,29},{6,30},{7,31},{8,0},{9,1... | collective-permute-start | bytes 798728 | tf_op jit(solution)/shard_map/ppermute | solution.py:557
  18.2 15.5 %collective-permute-start.17 = (bf16[80,1664]{1,0:T(8,128)(2,1)}, bf16[80,1664]{1,0:T(8,128)(2,1)S(1)}, u32[]{:S(2)}, u32[]{:S(2)}) collective-permute-start(bf16[80,1664]{1,0:T(8,128)(2,1)} %get-tuple-element.120), channel_id=1, source_target_pairs={{0,16},{1,17},{2,18},{3,19},{4,20},{5,21},{6,22},{7,23},{8,24},{9,... | collective-permute-start | bytes 798728 | tf_op jit(solution)/shard_map/ppermute | solution.py:557
  21.8 12.0 %collective-permute-start.6 = (bf16[80,1664]{1,0:T(8,128)(2,1)S(1)}, bf16[80,1664]{1,0:T(8,128)(2,1)S(1)}, u32[]{:S(2)}, u32[]{:S(2)}) collective-permute-start(bf16[80,1664]{1,0:T(8,128)(2,1)S(1)} %collective-permute-done.5), channel_id=1, source_target_pairs={{0,1},{1,0},{2,6},{3,7},{4,5},{5,4},{6,2},{7,3},{8,9},{9,8},{10,14... | collective-permute-start | bytes 798728 | tf_op jit(solution)/shard_map/ppermute | solution.py:557
  23.6 21.8 %collective-permute-start.3 = (bf16[320,1664]{1,0:T(8,128)(2,1)S(1)}, bf16[320,1664]{1,0:T(8,128)(2,1)S(1)}, u32[]{:S(2)}, u32[]{:S(2)}) collective-permute-start(bf16[320,1664]{1,0:T(8,128)(2,1)S(1)} %pad_maximum_fusion.near.refs_0_), channel_id=1, source_target_pairs={{0,2},{1,3},{2,0},{3,1},{4,6},{5,7},{6,4},{7,5},{8,10},{9,11},{10,... | collective-permute-start | bytes 3194888 | tf_op jit(solution)/shard_map/ppermute | solution.py:557
  23.7 11.7 %collective-permute-start.7 = (bf16[80,1664]{1,0:T(8,128)(2,1)S(1)}, bf16[80,1664]{1,0:T(8,128)(2,1)S(1)}, u32[]{:S(2)}, u32[]{:S(2)}) collective-permute-start(bf16[80,1664]{1,0:T(8,128)(2,1)S(1)} %collective-permute-done.5), channel_id=1, source_target_pairs={{0,4},{1,5},{2,3},{3,2},{4,0},{5,1},{6,7},{7,6},{8,12},{9,13},{10,... | collective-permute-start | bytes 798728 | tf_op jit(solution)/shard_map/ppermute | solution.py:557
  25.1 11.5 %collective-permute-start.12 = (bf16[80,1664]{1,0:T(8,128)(2,1)S(1)}, bf16[80,1664]{1,0:T(8,128)(2,1)S(1)}, u32[]{:S(2)}, u32[]{:S(2)}) collective-permute-start(bf16[80,1664]{1,0:T(8,128)(2,1)S(1)} %collective-permute-done.11), channel_id=1, source_target_pairs={{0,1},{1,0},{2,6},{3,7},{4,5},{5,4},{6,2},{7,3},{8,9},{9,8},{10,14... | collective-permute-start | bytes 798728 | tf_op jit(solution)/shard_map/ppermute | solution.py:557
  34.3 9.3 %collective-permute-start.18 = (bf16[80,1664]{1,0:T(8,128)(2,1)S(1)}, bf16[80,1664]{1,0:T(8,128)(2,1)S(1)}, u32[]{:S(2)}, u32[]{:S(2)}) collective-permute-start(bf16[80,1664]{1,0:T(8,128)(2,1)S(1)} %collective-permute-done.17), channel_id=1, source_target_pairs={{0,1},{1,0},{2,6},{3,7},{4,5},{5,4},{6,2},{7,3},{8,9},{9,8},{10,14... | collective-permute-start | bytes 798728 | tf_op jit(solution)/shard_map/ppermute | solution.py:557
  35.3 16.2 %collective-permute-start.13 = (bf16[80,1664]{1,0:T(8,128)(2,1)S(1)}, bf16[80,1664]{1,0:T(8,128)(2,1)S(1)}, u32[]{:S(2)}, u32[]{:S(2)}) collective-permute-start(bf16[80,1664]{1,0:T(8,128)(2,1)S(1)} %collective-permute-done.11), channel_id=1, source_target_pairs={{0,4},{1,5},{2,3},{3,2},{4,0},{5,1},{6,7},{7,6},{8,12},{9,13},{10,... | collective-permute-start | bytes 798728 | tf_op jit(solution)/shard_map/ppermute | solution.py:557
  36.6 11.4 %collective-permute-start.19 = (bf16[80,1664]{1,0:T(8,128)(2,1)S(1)}, bf16[80,1664]{1,0:T(8,128)(2,1)S(1)}, u32[]{:S(2)}, u32[]{:S(2)}) collective-permute-start(bf16[80,1664]{1,0:T(8,128)(2,1)S(1)} %collective-permute-done.17), channel_id=1, source_target_pairs={{0,4},{1,5},{2,3},{3,2},{4,0},{5,1},{6,7},{7,6},{8,12},{9,13},{10,... | collective-permute-start | bytes 798728 | tf_op jit(solution)/shard_map/ppermute | solution.py:557
  40.2 11.4 %collective-permute-start.14 = (bf16[80,1664]{1,0:T(8,128)(2,1)S(1)}, bf16[80,1664]{1,0:T(8,128)(2,1)S(1)}, u32[]{:S(2)}, u32[]{:S(2)}) collective-permute-start(bf16[80,1664]{1,0:T(8,128)(2,1)S(1)} %collective-permute-done.12), channel_id=1, source_target_pairs={{0,4},{1,5},{2,3},{3,2},{4,0},{5,1},{6,7},{7,6},{8,12},{9,13},{10,... | collective-permute-start | bytes 798728 | tf_op jit(solution)/shard_map/ppermute | solution.py:557
  56.0 26.9 %collective-permute-start.4 = (bf16[320,1664]{1,0:T(8,128)(2,1)S(1)}, bf16[320,1664]{1,0:T(8,128)(2,1)S(1)}, u32[]{:S(2)}, u32[]{:S(2)}) collective-permute-start(bf16[320,1664]{1,0:T(8,128)(2,1)S(1)} %get-tuple-element.106), channel_id=1, source_target_pairs={{0,2},{1,3},{2,0},{3,1},{4,6},{5,7},{6,4},{7,5},{8,10},{9,11},{10,... | collective-permute-start | bytes 3194888 | tf_op jit(solution)/shard_map/ppermute | solution.py:557
  64.8 11.3 %collective-permute-start.25 = (bf16[144,1664]{1,0:T(8,128)(2,1)S(1)}, bf16[144,1664]{1,0:T(8,128)(2,1)S(1)}, u32[]{:S(2)}, u32[]{:S(2)}) collective-permute-start(bf16[144,1664]{1,0:T(8,128)(2,1)S(1)} %pad_maximum_fusion.5), channel_id=1, source_target_pairs={{0,1},{1,0},{2,6},{3,7},{4,5},{5,4},{6,2},{7,3},{8,9},{9,8},{10,14... | collective-permute-start | bytes 1437704 | tf_op jit(solution)/shard_map/ppermute | solution.py:557
  66.6 17.5 %collective-permute-start.28 = (bf16[144,1664]{1,0:T(8,128)(2,1)S(1)}, bf16[144,1664]{1,0:T(8,128)(2,1)S(1)}, u32[]{:S(2)}, u32[]{:S(2)}) collective-permute-start(bf16[144,1664]{1,0:T(8,128)(2,1)S(1)} %pad_maximum_fusion.6), channel_id=1, source_target_pairs={{0,1},{1,0},{2,6},{3,7},{4,5},{5,4},{6,2},{7,3},{8,9},{9,8},{10,14... | collective-permute-start | bytes 1437704 | tf_op jit(solution)/shard_map/ppermute | solution.py:557
  68.4 9.1 %collective-permute-start.24 = (bf16[72,1664]{1,0:T(8,128)(2,1)S(1)}, bf16[72,1664]{1,0:T(8,128)(2,1)S(1)}, u32[]{:S(2)}, u32[]{:S(2)}) collective-permute-start(bf16[72,1664]{1,0:T(8,128)(2,1)S(1)} %add_convert_fusion.7), channel_id=1, source_target_pairs={{0,4},{1,5},{2,3},{3,2},{4,0},{5,1},{6,7},{7,6},{8,12},{9,13},{10,... | collective-permute-start | bytes 718856 | tf_op jit(solution)/shard_map/ppermute | solution.py:557
  76.2 9.4 %collective-permute-start.27 = (bf16[72,1664]{1,0:T(8,128)(2,1)S(1)}, bf16[72,1664]{1,0:T(8,128)(2,1)S(1)}, u32[]{:S(2)}, u32[]{:S(2)}) collective-permute-start(bf16[72,1664]{1,0:T(8,128)(2,1)S(1)} %add_convert_fusion.6), channel_id=1, source_target_pairs={{0,4},{1,5},{2,3},{3,2},{4,0},{5,1},{6,7},{7,6},{8,12},{9,13},{10,... | collective-permute-start | bytes 718856 | tf_op jit(solution)/shard_map/ppermute | solution.py:557
  77.7 28.5 %collective-permute-start.31 = (bf16[72,1664]{1,0:T(8,128)(2,1)S(1)}, bf16[72,1664]{1,0:T(8,128)(2,1)S(1)}, u32[]{:S(2)}, u32[]{:S(2)}) collective-permute-start(bf16[72,1664]{1,0:T(8,128)(2,1)S(1)} %multiply_convert_fusion.3), channel_id=1, source_target_pairs={{0,24},{1,25},{2,26},{3,27},{4,28},{5,29},{6,30},{7,31},{8,0},{9,1... | collective-permute-start | bytes 718856 | tf_op jit(solution)/shard_map/ppermute | solution.py:557
  83.3 9.0 %collective-permute-start.26 = (bf16[144,1664]{1,0:T(8,128)(2,1)S(1)}, bf16[144,1664]{1,0:T(8,128)(2,1)S(1)}, u32[]{:S(2)}, u32[]{:S(2)}) collective-permute-start(bf16[144,1664]{1,0:T(8,128)(2,1)S(1)} %pad_maximum_fusion.7), channel_id=1, source_target_pairs={{0,1},{1,0},{2,6},{3,7},{4,5},{5,4},{6,2},{7,3},{8,9},{9,8},{10,14... | collective-permute-start | bytes 1437704 | tf_op jit(solution)/shard_map/ppermute | solution.py:557
  84.2 9.4 %collective-permute-start.30 = (bf16[72,1664]{1,0:T(8,128)(2,1)S(1)}, bf16[72,1664]{1,0:T(8,128)(2,1)S(1)}, u32[]{:S(2)}, u32[]{:S(2)}) collective-permute-start(bf16[72,1664]{1,0:T(8,128)(2,1)S(1)} %add_convert_fusion.5), channel_id=1, source_target_pairs={{0,4},{1,5},{2,3},{3,2},{4,0},{5,1},{6,7},{7,6},{8,12},{9,13},{10,... | collective-permute-start | bytes 718856 | tf_op jit(solution)/shard_map/ppermute | solution.py:557
  85.7 20.5 %collective-permute-start.33 = (bf16[72,1664]{1,0:T(8,128)(2,1)S(1)}, bf16[72,1664]{1,0:T(8,128)(2,1)S(1)}, u32[]{:S(2)}, u32[]{:S(2)}) collective-permute-start(bf16[72,1664]{1,0:T(8,128)(2,1)S(1)} %multiply_convert_fusion.2), channel_id=1, source_target_pairs={{0,8},{1,9},{2,10},{3,11},{4,12},{5,13},{6,14},{7,15},{8,16},{9,17... | collective-permute-start | bytes 718856 | tf_op jit(solution)/shard_map/ppermute | solution.py:557
  92.3 13.7 %collective-permute-start.29 = (bf16[72,1664]{1,0:T(8,128)(2,1)S(1)}, bf16[72,1664]{1,0:T(8,128)(2,1)S(1)}, u32[]{:S(2)}, u32[]{:S(2)}) collective-permute-start(bf16[72,1664]{1,0:T(8,128)(2,1)S(1)} %add_convert_fusion.4), channel_id=1, source_target_pairs={{0,4},{1,5},{2,3},{3,2},{4,0},{5,1},{6,7},{7,6},{8,12},{9,13},{10,... | collective-permute-start | bytes 718856 | tf_op jit(solution)/shard_map/ppermute | solution.py:557
  93.7 12.5 %collective-permute-start.32 = (bf16[72,1664]{1,0:T(8,128)(2,1)S(1)}, bf16[72,1664]{1,0:T(8,128)(2,1)S(1)}, u32[]{:S(2)}, u32[]{:S(2)}) collective-permute-start(bf16[72,1664]{1,0:T(8,128)(2,1)S(1)} %multiply_convert_fusion.1), channel_id=1, source_target_pairs={{0,16},{1,17},{2,18},{3,19},{4,20},{5,21},{6,22},{7,23},{8,24},{9,... | collective-permute-start | bytes 718856 | tf_op jit(solution)/shard_map/ppermute | solution.py:557
  (34 other events, 212.7 us)

commit v6 on v5

--- a/solution.py
+++ b/solution.py
@@ -132,7 +132,7 @@
 
 GROUPS = ((0,), (1,), (3,), (2,))
 MIB = 1024 * 1024
-WLIM = 56
+WLIM = 32
 PLAN = (
     "Z 1",
     "D1 0",

time: 115 us -> 113 us (0.983)
  Pallas kernels: 25.7 us -> 24 us
  local copies, waits for them, and re-layouts: 4.49 us -> 3.07 us
    pallas_call x1, Pallas kernels: 10.2 us -> 8.49 us  [weight_call(): pl.pallas_call(weight_kernel, out_shape=(jax.ShapeDtypeStruct((width, hid...]
    unnamed x46 -> x12, local copies, waits for them, and re-layouts: 4.35 us -> 2.93 us
  transfers between devices with their start and end apart: 35 -> 35, of which waited for: 10 -> 12; matrix products, arithmetic and copies ran while one was open for 3% -> 3% of each run, Pallas kernels for 19% -> 18%
where the time goes in v6:
time: 113 us; the launch traced here: 112 us
  starting transfers between devices  43.2 us (38%)
  waiting for transfers between devices  38.1 us (34%)
  Pallas kernels  24 us (21%)
  other arithmetic  3.19 us (3%)
  local copies, waits for them, and re-layouts  3.07 us (3%)
    ppermute x34, starting transfers between devices, send(): return lax.ppermute(array, ('dp', 'rep'), permutation(move))  42.1 us
    ppermute x34, waiting for transfers between devices, send(): return lax.ppermute(array, ('dp', 'rep'), permutation(move))  33.1 us
    pallas_call x4, Pallas kernels, expert_call(): pl.pallas_call(expert_kernel, out_shape=(jax.ShapeDtypeStruct((rows, widt...  10.2 us
    pallas_call x1, Pallas kernels, weight_call(): pl.pallas_call(weight_kernel, out_shape=(jax.ShapeDtypeStruct((width, hid...  8.49 us
    ppermute x1, waiting for transfers between devices, plane_body(): got = lax.ppermute(away, 'rep', [(0, 1), (1, 0)])  4.92 us
    unnamed x12, local copies, waits for them, and re-layouts  2.93 us
    pallas_call x1, Pallas kernels, start_call(): pl.pallas_call(functools.partial(start_kernel, experts), out_shape=(jax.S...  2.39 us
  transfers between devices with their start and end apart: 35, of which 12 were waited for; matrix products, arithmetic and copies ran while one was open for 3% of the time, Pallas kernels for 18%

profile of v6, /device:TPU:0, one launch (start us, length us, event | category | flops | bytes accessed | tf_op | source)
XLA Modules:
  0.0 112.4 jit_solution(5241132057321046222)
XLA Ops:
  0.6 2.4 %shard_map.110 = (bf16[2,4,72,128]{3,2,1,0:T(8,128)(2,1)}, bf16[80,1664]{1,0:T(8,128)(2,1)}, bf16[80,1664]{1,0:T(8,128)(2,1)}, bf16[80,1664]{1,0:T(8,128)(2,1)}, bf16[80,1664]{1,0:T(8,128)(2,1)}) custom-call(s32[2,128]{1,0:T(2,128)} %bitcast.14, s32[1,128]{1,0:T(1,128)} %bitcast.15, f32[2,128]{1,0:T(2,128)} %bitcast.12, bf16[128,1664]{1,0:T(8,128)(2,1)} %tokens_at.1, ...), custom_call_target="tpu_custom_call" | custom-call | tf_op jit(solution)/shard_map/pallas_call | solution.py:275
  3.0 3.0 %collective-permute-start = (bf16[80,1664]{1,0:T(8,128)(2,1)}, bf16[80,1664]{1,0:T(8,128)(2,1)S(1)}, u32[]{:S(2)}, u32[]{:S(2)}) collective-permute-start(bf16[80,1664]{1,0:T(8,128)(2,1)} %get-tuple-element.100), channel_id=1, source_target_pairs={{0,1},{1,0},{2,6},{3,7},{4,5},{5,4},{6,2},{7,3},{8,9},{9,8},{10,14... | collective-permute-start | bytes 798728 | tf_op jit(solution)/shard_map/ppermute | solution.py:557
  6.0 1.6 %collective-permute-start.5 = (bf16[80,1664]{1,0:T(8,128)(2,1)}, bf16[80,1664]{1,0:T(8,128)(2,1)S(1)}, u32[]{:S(2)}, u32[]{:S(2)}) collective-permute-start(bf16[80,1664]{1,0:T(8,128)(2,1)} %get-tuple-element.107), channel_id=1, source_target_pairs={{0,8},{1,9},{2,10},{3,11},{4,12},{5,13},{6,14},{7,15},{8,16},{9,17... | collective-permute-start | bytes 798728 | tf_op jit(solution)/shard_map/ppermute | solution.py:557
  7.6 1.5 %collective-permute-start.1 = (bf16[80,1664]{1,0:T(8,128)(2,1)}, bf16[80,1664]{1,0:T(8,128)(2,1)S(1)}, u32[]{:S(2)}, u32[]{:S(2)}) collective-permute-start(bf16[80,1664]{1,0:T(8,128)(2,1)} %get-tuple-element.100), channel_id=1, source_target_pairs={{0,4},{1,5},{2,3},{3,2},{4,0},{5,1},{6,7},{7,6},{8,12},{9,13},{10,... | collective-permute-start | bytes 798728 | tf_op jit(solution)/shard_map/ppermute | solution.py:557
  9.1 2.5 %collective-permute-done = bf16[80,1664]{1,0:T(8,128)(2,1)S(1)} collective-permute-done((bf16[80,1664]{1,0:T(8,128)(2,1)}, bf16[80,1664]{1,0:T(8,128)(2,1)S(1)}, u32[]{:S(2)}, u32[]{:S(2)}) %collective-permute-start) | collective-permute-done | bytes 266272 | tf_op jit(solution)/shard_map/ppermute | solution.py:557
  11.7 3.6 %collective-permute-start.2 = (bf16[80,1664]{1,0:T(8,128)(2,1)S(1)}, bf16[80,1664]{1,0:T(8,128)(2,1)S(1)}, u32[]{:S(2)}, u32[]{:S(2)}) collective-permute-start(bf16[80,1664]{1,0:T(8,128)(2,1)S(1)} %collective-permute-done), channel_id=1, source_target_pairs={{0,4},{1,5},{2,3},{3,2},{4,0},{5,1},{6,7},{7,6},{8,12},{9,13},{10,... | collective-permute-start | bytes 798728 | tf_op jit(solution)/shard_map/ppermute | solution.py:557
  15.2 3.0 %collective-permute-start.11 = (bf16[80,1664]{1,0:T(8,128)(2,1)}, bf16[80,1664]{1,0:T(8,128)(2,1)S(1)}, u32[]{:S(2)}, u32[]{:S(2)}) collective-permute-start(bf16[80,1664]{1,0:T(8,128)(2,1)} %get-tuple-element.113), channel_id=1, source_target_pairs={{0,24},{1,25},{2,26},{3,27},{4,28},{5,29},{6,30},{7,31},{8,0},{9,1... | collective-permute-start | bytes 798728 | tf_op jit(solution)/shard_map/ppermute | solution.py:557
  21.8 1.6 %collective-permute-start.6 = (bf16[80,1664]{1,0:T(8,128)(2,1)S(1)}, bf16[80,1664]{1,0:T(8,128)(2,1)S(1)}, u32[]{:S(2)}, u32[]{:S(2)}) collective-permute-start(bf16[80,1664]{1,0:T(8,128)(2,1)S(1)} %collective-permute-done.5), channel_id=1, source_target_pairs={{0,1},{1,0},{2,6},{3,7},{4,5},{5,4},{6,2},{7,3},{8,9},{9,8},{10,14... | collective-permute-start | bytes 798728 | tf_op jit(solution)/shard_map/ppermute | solution.py:557
  25.5 8.2 %collective-permute-done.17 = bf16[80,1664]{1,0:T(8,128)(2,1)S(1)} collective-permute-done((bf16[80,1664]{1,0:T(8,128)(2,1)}, bf16[80,1664]{1,0:T(8,128)(2,1)S(1)}, u32[]{:S(2)}, u32[]{:S(2)}) %collective-permute-start.17) | collective-permute-done | bytes 266272 | tf_op jit(solution)/shard_map/ppermute | solution.py:557
  37.4 2.8 %collective-permute-done.8 = bf16[80,1664]{1,0:T(8,128)(2,1)S(1)} collective-permute-done((bf16[80,1664]{1,0:T(8,128)(2,1)S(1)}, bf16[80,1664]{1,0:T(8,128)(2,1)S(1)}, u32[]{:S(2)}, u32[]{:S(2)}) %collective-permute-start.8) | collective-permute-done | bytes 266272 | tf_op jit(solution)/shard_map/ppermute | solution.py:557
  40.7 2.9 %collective-permute-done.18 = bf16[80,1664]{1,0:T(8,128)(2,1)S(1)} collective-permute-done((bf16[80,1664]{1,0:T(8,128)(2,1)S(1)}, bf16[80,1664]{1,0:T(8,128)(2,1)S(1)}, u32[]{:S(2)}, u32[]{:S(2)}) %collective-permute-start.18) | collective-permute-done | bytes 266272 | tf_op jit(solution)/shard_map/ppermute | solution.py:557
  45.4 2.5 %shard_map.112 = (bf16[320,1664]{1,0:T(8,128)(2,1)S(1)}, bf16[320,1664]{1,0:T(8,128)(2,1)S(1)}, bf16[320,512]{1,0:T(8,128)(2,1)S(1)}, bf16[320,512]{1,0:T(8,128)(2,1)S(1)}) custom-call(bf16[320,1664]{1,0:T(8,128)(2,1)S(1)} %pad_maximum_fusion.near.refs_0_, bf16[320,1664]{1,0:T(8,128)(2,1)S(1)} %collective-permute-done.3.far.refs_1_, ...), custom_call_target="tpu_custom_call" | custom-call | tf_op jit(solution)/shard_map/pallas_call | solution.py:199
  48.0 3.6 %collective-permute-done.20 = bf16[80,1664]{1,0:T(8,128)(2,1)S(1)} collective-permute-done((bf16[80,1664]{1,0:T(8,128)(2,1)S(1)}, bf16[80,1664]{1,0:T(8,128)(2,1)S(1)}, u32[]{:S(2)}, u32[]{:S(2)}) %collective-permute-start.20) | collective-permute-done | bytes 266272 | tf_op jit(solution)/shard_map/ppermute | solution.py:557
  52.0 2.5 %shard_map.113 = (bf16[320,1664]{1,0:T(8,128)(2,1)S(1)}, bf16[320,1664]{1,0:T(8,128)(2,1)S(1)}, bf16[320,512]{1,0:T(8,128)(2,1)S(1)}, bf16[320,512]{1,0:T(8,128)(2,1)S(1)}) custom-call(bf16[320,1664]{1,0:T(8,128)(2,1)S(1)} %pad_maximum_fusion.1.near.refs_2_.refs_4_, bf16[320,1664]{1,0:T(8,128)(2,1)S(1)} %collective-permute-done.9.far.refs_3_.refs_5_, ...), custom_call_target="tpu_custom_call" | custom-call | tf_op jit(solution)/shard_map/pallas_call | solution.py:199
  55.8 2.5 %shard_map.114 = (bf16[320,1664]{1,0:T(8,128)(2,1)S(1)}, bf16[320,1664]{1,0:T(8,128)(2,1)S(1)}, bf16[320,512]{1,0:T(8,128)(2,1)S(1)}, bf16[320,512]{1,0:T(8,128)(2,1)S(1)}) custom-call(bf16[320,1664]{1,0:T(8,128)(2,1)S(1)} %pad_maximum_fusion.2.near.refs_4_.refs_8_, bf16[320,1664]{1,0:T(8,128)(2,1)S(1)} %collective-permute-done.15.far.refs_5_.refs_9_, ...), custom_call_target="tpu_custom_call" | custom-call | tf_op jit(solution)/shard_map/pallas_call | solution.py:199
  59.9 2.5 %shard_map.115 = (bf16[320,1664]{1,0:T(8,128)(2,1)S(1)}, bf16[320,1664]{1,0:T(8,128)(2,1)S(1)}, bf16[320,512]{1,0:T(8,128)(2,1)S(1)}, bf16[320,512]{1,0:T(8,128)(2,1)S(1)}) custom-call(bf16[320,1664]{1,0:T(8,128)(2,1)S(1)} %pad_maximum_fusion.3.near.refs_6_.refs_12_, bf16[320,1664]{1,0:T(8,128)(2,1)S(1)} %collective-permute-done.21.far.refs_7_.refs_13_, ...), custom_call_target="tpu_custom_call" | custom-call | tf_op jit(solution)/shard_map/pallas_call | solution.py:199
  63.7 1.5 %collective-permute-start.25 = (bf16[144,1664]{1,0:T(8,128)(2,1)S(1)}, bf16[144,1664]{1,0:T(8,128)(2,1)S(1)}, u32[]{:S(2)}, u32[]{:S(2)}) collective-permute-start(bf16[144,1664]{1,0:T(8,128)(2,1)S(1)} %pad_maximum_fusion.5), channel_id=1, source_target_pairs={{0,1},{1,0},{2,6},{3,7},{4,5},{5,4},{6,2},{7,3},{8,9},{9,8},{10,14... | collective-permute-start | bytes 1437704 | tf_op jit(solution)/shard_map/ppermute | solution.py:557
  68.4 7.0 %collective-permute-done.25 = bf16[144,1664]{1,0:T(8,128)(2,1)S(1)} collective-permute-done((bf16[144,1664]{1,0:T(8,128)(2,1)S(1)}, bf16[144,1664]{1,0:T(8,128)(2,1)S(1)}, u32[]{:S(2)}, u32[]{:S(2)}) %collective-permute-start.25) | collective-permute-done | bytes 479264 | tf_op jit(solution)/shard_map/ppermute | solution.py:557
  76.7 5.1 %collective-permute-start.31 = (bf16[72,1664]{1,0:T(8,128)(2,1)S(1)}, bf16[72,1664]{1,0:T(8,128)(2,1)S(1)}, u32[]{:S(2)}, u32[]{:S(2)}) collective-permute-start(bf16[72,1664]{1,0:T(8,128)(2,1)S(1)} %multiply_convert_fusion.3), channel_id=1, source_target_pairs={{0,24},{1,25},{2,26},{3,27},{4,28},{5,29},{6,30},{7,31},{8,0},{9,1... | collective-permute-start | bytes 718856 | tf_op jit(solution)/shard_map/ppermute | solution.py:557
  84.8 2.9 %collective-permute-start.33 = (bf16[72,1664]{1,0:T(8,128)(2,1)S(1)}, bf16[72,1664]{1,0:T(8,128)(2,1)S(1)}, u32[]{:S(2)}, u32[]{:S(2)}) collective-permute-start(bf16[72,1664]{1,0:T(8,128)(2,1)S(1)} %multiply_convert_fusion.2), channel_id=1, source_target_pairs={{0,8},{1,9},{2,10},{3,11},{4,12},{5,13},{6,14},{7,15},{8,16},{9,17... | collective-permute-start | bytes 718856 | tf_op jit(solution)/shard_map/ppermute | solution.py:557
  87.7 3.7 %collective-permute-done.26 = bf16[144,1664]{1,0:T(8,128)(2,1)S(1)} collective-permute-done((bf16[144,1664]{1,0:T(8,128)(2,1)S(1)}, bf16[144,1664]{1,0:T(8,128)(2,1)S(1)}, u32[]{:S(2)}, u32[]{:S(2)}) %collective-permute-start.26) | collective-permute-done | bytes 479264 | tf_op jit(solution)/shard_map/ppermute | solution.py:557
  92.8 2.0 %collective-permute-start.32 = (bf16[72,1664]{1,0:T(8,128)(2,1)S(1)}, bf16[72,1664]{1,0:T(8,128)(2,1)S(1)}, u32[]{:S(2)}, u32[]{:S(2)}) collective-permute-start(bf16[72,1664]{1,0:T(8,128)(2,1)S(1)} %multiply_convert_fusion.1), channel_id=1, source_target_pairs={{0,16},{1,17},{2,18},{3,19},{4,20},{5,21},{6,22},{7,23},{8,24},{9,... | collective-permute-start | bytes 718856 | tf_op jit(solution)/shard_map/ppermute | solution.py:557
  94.8 8.5 %shard_map.117 = (bf16[1664,512]{1,0:T(8,128)(2,1)}, bf16[512,1664]{1,0:T(8,128)(2,1)}) custom-call(bf16[1280,128]{1,0:T(8,128)(2,1)S(1)} %get-tuple-element.154.kept, bf16[320,1664]{1,0:T(8,128)(2,1)S(1)} %pad_maximum_fusion.near.refs_0_, bf16[320,1664]{1,0:T(8,128)(2,1)S(1)} %collective-permute-done.3.far.refs_1_, ...), custom_call_target="tpu_custom_call" | custom-call | tf_op jit(solution)/shard_map/pallas_call | solution.py:412
  106.6 4.9 %collective-permute-done.34.got = bf16[848,128]{1,0:T(8,128)(2,1)S(1)} collective-permute-done((bf16[848,128]{1,0:T(8,128)(2,1)S(1)}, bf16[848,128]{1,0:T(8,128)(2,1)S(1)}, u32[]{:S(2)}, u32[]{:S(2)}) %collective-permute-start.34) | collective-permute-done | bytes 217120 | tf_op jit(solution)/shard_map/ppermute | solution.py:702
  (96 shorter events, 29.0 us)
Async XLA Ops:
  6.0 15.7 %collective-permute-start.5 = (bf16[80,1664]{1,0:T(8,128)(2,1)}, bf16[80,1664]{1,0:T(8,128)(2,1)S(1)}, u32[]{:S(2)}, u32[]{:S(2)}) collective-permute-start(bf16[80,1664]{1,0:T(8,128)(2,1)} %get-tuple-element.107), channel_id=1, source_target_pairs={{0,8},{1,9},{2,10},{3,11},{4,12},{5,13},{6,14},{7,15},{8,16},{9,17... | collective-permute-start | bytes 798728 | tf_op jit(solution)/shard_map/ppermute | solution.py:557
  7.6 15.7 %collective-permute-start.1 = (bf16[80,1664]{1,0:T(8,128)(2,1)}, bf16[80,1664]{1,0:T(8,128)(2,1)S(1)}, u32[]{:S(2)}, u32[]{:S(2)}) collective-permute-start(bf16[80,1664]{1,0:T(8,128)(2,1)} %get-tuple-element.100), channel_id=1, source_target_pairs={{0,4},{1,5},{2,3},{3,2},{4,0},{5,1},{6,7},{7,6},{8,12},{9,13},{10,... | collective-permute-start | bytes 798728 | tf_op jit(solution)/shard_map/ppermute | solution.py:557
  11.7 11.7 %collective-permute-start.2 = (bf16[80,1664]{1,0:T(8,128)(2,1)S(1)}, bf16[80,1664]{1,0:T(8,128)(2,1)S(1)}, u32[]{:S(2)}, u32[]{:S(2)}) collective-permute-start(bf16[80,1664]{1,0:T(8,128)(2,1)S(1)} %collective-permute-done), channel_id=1, source_target_pairs={{0,4},{1,5},{2,3},{3,2},{4,0},{5,1},{6,7},{7,6},{8,12},{9,13},{10,... | collective-permute-start | bytes 798728 | tf_op jit(solution)/shard_map/ppermute | solution.py:557
  15.2 9.9 %collective-permute-start.11 = (bf16[80,1664]{1,0:T(8,128)(2,1)}, bf16[80,1664]{1,0:T(8,128)(2,1)S(1)}, u32[]{:S(2)}, u32[]{:S(2)}) collective-permute-start(bf16[80,1664]{1,0:T(8,128)(2,1)} %get-tuple-element.113), channel_id=1, source_target_pairs={{0,24},{1,25},{2,26},{3,27},{4,28},{5,29},{6,30},{7,31},{8,0},{9,1... | collective-permute-start | bytes 798728 | tf_op jit(solution)/shard_map/ppermute | solution.py:557
  18.2 15.5 %collective-permute-start.17 = (bf16[80,1664]{1,0:T(8,128)(2,1)}, bf16[80,1664]{1,0:T(8,128)(2,1)S(1)}, u32[]{:S(2)}, u32[]{:S(2)}) collective-permute-start(bf16[80,1664]{1,0:T(8,128)(2,1)} %get-tuple-element.120), channel_id=1, source_target_pairs={{0,16},{1,17},{2,18},{3,19},{4,20},{5,21},{6,22},{7,23},{8,24},{9,... | collective-permute-start | bytes 798728 | tf_op jit(solution)/shard_map/ppermute | solution.py:557
  21.8 12.0 %collective-permute-start.6 = (bf16[80,1664]{1,0:T(8,128)(2,1)S(1)}, bf16[80,1664]{1,0:T(8,128)(2,1)S(1)}, u32[]{:S(2)}, u32[]{:S(2)}) collective-permute-start(bf16[80,1664]{1,0:T(8,128)(2,1)S(1)} %collective-permute-done.5), channel_id=1, source_target_pairs={{0,1},{1,0},{2,6},{3,7},{4,5},{5,4},{6,2},{7,3},{8,9},{9,8},{10,14... | collective-permute-start | bytes 798728 | tf_op jit(solution)/shard_map/ppermute | solution.py:557
  23.6 21.8 %collective-permute-start.3 = (bf16[320,1664]{1,0:T(8,128)(2,1)S(1)}, bf16[320,1664]{1,0:T(8,128)(2,1)S(1)}, u32[]{:S(2)}, u32[]{:S(2)}) collective-permute-start(bf16[320,1664]{1,0:T(8,128)(2,1)S(1)} %pad_maximum_fusion.near.refs_0_), channel_id=1, source_target_pairs={{0,2},{1,3},{2,0},{3,1},{4,6},{5,7},{6,4},{7,5},{8,10},{9,11},{10,... | collective-permute-start | bytes 3194888 | tf_op jit(solution)/shard_map/ppermute | solution.py:557
  23.7 11.7 %collective-permute-start.7 = (bf16[80,1664]{1,0:T(8,128)(2,1)S(1)}, bf16[80,1664]{1,0:T(8,128)(2,1)S(1)}, u32[]{:S(2)}, u32[]{:S(2)}) collective-permute-start(bf16[80,1664]{1,0:T(8,128)(2,1)S(1)} %collective-permute-done.5), channel_id=1, source_target_pairs={{0,4},{1,5},{2,3},{3,2},{4,0},{5,1},{6,7},{7,6},{8,12},{9,13},{10,... | collective-permute-start | bytes 798728 | tf_op jit(solution)/shard_map/ppermute | solution.py:557
  25.1 11.5 %collective-permute-start.12 = (bf16[80,1664]{1,0:T(8,128)(2,1)S(1)}, bf16[80,1664]{1,0:T(8,128)(2,1)S(1)}, u32[]{:S(2)}, u32[]{:S(2)}) collective-permute-start(bf16[80,1664]{1,0:T(8,128)(2,1)S(1)} %collective-permute-done.11), channel_id=1, source_target_pairs={{0,1},{1,0},{2,6},{3,7},{4,5},{5,4},{6,2},{7,3},{8,9},{9,8},{10,14... | collective-permute-start | bytes 798728 | tf_op jit(solution)/shard_map/ppermute | solution.py:557
  34.3 9.3 %collective-permute-start.18 = (bf16[80,1664]{1,0:T(8,128)(2,1)S(1)}, bf16[80,1664]{1,0:T(8,128)(2,1)S(1)}, u32[]{:S(2)}, u32[]{:S(2)}) collective-permute-start(bf16[80,1664]{1,0:T(8,128)(2,1)S(1)} %collective-permute-done.17), channel_id=1, source_target_pairs={{0,1},{1,0},{2,6},{3,7},{4,5},{5,4},{6,2},{7,3},{8,9},{9,8},{10,14... | collective-permute-start | bytes 798728 | tf_op jit(solution)/shard_map/ppermute | solution.py:557
  35.3 16.2 %collective-permute-start.13 = (bf16[80,1664]{1,0:T(8,128)(2,1)S(1)}, bf16[80,1664]{1,0:T(8,128)(2,1)S(1)}, u32[]{:S(2)}, u32[]{:S(2)}) collective-permute-start(bf16[80,1664]{1,0:T(8,128)(2,1)S(1)} %collective-permute-done.11), channel_id=1, source_target_pairs={{0,4},{1,5},{2,3},{3,2},{4,0},{5,1},{6,7},{7,6},{8,12},{9,13},{10,... | collective-permute-start | bytes 798728 | tf_op jit(solution)/shard_map/ppermute | solution.py:557
  36.6 11.4 %collective-permute-start.19 = (bf16[80,1664]{1,0:T(8,128)(2,1)S(1)}, bf16[80,1664]{1,0:T(8,128)(2,1)S(1)}, u32[]{:S(2)}, u32[]{:S(2)}) collective-permute-start(bf16[80,1664]{1,0:T(8,128)(2,1)S(1)} %collective-permute-done.17), channel_id=1, source_target_pairs={{0,4},{1,5},{2,3},{3,2},{4,0},{5,1},{6,7},{7,6},{8,12},{9,13},{10,... | collective-permute-start | bytes 798728 | tf_op jit(solution)/shard_map/ppermute | solution.py:557
  40.2 11.4 %collective-permute-start.14 = (bf16[80,1664]{1,0:T(8,128)(2,1)S(1)}, bf16[80,1664]{1,0:T(8,128)(2,1)S(1)}, u32[]{:S(2)}, u32[]{:S(2)}) collective-permute-start(bf16[80,1664]{1,0:T(8,128)(2,1)S(1)} %collective-permute-done.12), channel_id=1, source_target_pairs={{0,4},{1,5},{2,3},{3,2},{4,0},{5,1},{6,7},{7,6},{8,12},{9,13},{10,... | collective-permute-start | bytes 798728 | tf_op jit(solution)/shard_map/ppermute | solution.py:557
  55.3 26.5 %collective-permute-start.4 = (bf16[320,1664]{1,0:T(8,128)(2,1)S(1)}, bf16[320,1664]{1,0:T(8,128)(2,1)S(1)}, u32[]{:S(2)}, u32[]{:S(2)}) collective-permute-start(bf16[320,1664]{1,0:T(8,128)(2,1)S(1)} %get-tuple-element.106), channel_id=1, source_target_pairs={{0,2},{1,3},{2,0},{3,1},{4,6},{5,7},{6,4},{7,5},{8,10},{9,11},{10,... | collective-permute-start | bytes 3194888 | tf_op jit(solution)/shard_map/ppermute | solution.py:557
  63.7 11.7 %collective-permute-start.25 = (bf16[144,1664]{1,0:T(8,128)(2,1)S(1)}, bf16[144,1664]{1,0:T(8,128)(2,1)S(1)}, u32[]{:S(2)}, u32[]{:S(2)}) collective-permute-start(bf16[144,1664]{1,0:T(8,128)(2,1)S(1)} %pad_maximum_fusion.5), channel_id=1, source_target_pairs={{0,1},{1,0},{2,6},{3,7},{4,5},{5,4},{6,2},{7,3},{8,9},{9,8},{10,14... | collective-permute-start | bytes 1437704 | tf_op jit(solution)/shard_map/ppermute | solution.py:557
  65.6 17.8 %collective-permute-start.28 = (bf16[144,1664]{1,0:T(8,128)(2,1)S(1)}, bf16[144,1664]{1,0:T(8,128)(2,1)S(1)}, u32[]{:S(2)}, u32[]{:S(2)}) collective-permute-start(bf16[144,1664]{1,0:T(8,128)(2,1)S(1)} %pad_maximum_fusion.6), channel_id=1, source_target_pairs={{0,1},{1,0},{2,6},{3,7},{4,5},{5,4},{6,2},{7,3},{8,9},{9,8},{10,14... | collective-permute-start | bytes 1437704 | tf_op jit(solution)/shard_map/ppermute | solution.py:557
  67.8 8.8 %collective-permute-start.24 = (bf16[72,1664]{1,0:T(8,128)(2,1)S(1)}, bf16[72,1664]{1,0:T(8,128)(2,1)S(1)}, u32[]{:S(2)}, u32[]{:S(2)}) collective-permute-start(bf16[72,1664]{1,0:T(8,128)(2,1)S(1)} %add_convert_fusion.7), channel_id=1, source_target_pairs={{0,4},{1,5},{2,3},{3,2},{4,0},{5,1},{6,7},{7,6},{8,12},{9,13},{10,... | collective-permute-start | bytes 718856 | tf_op jit(solution)/shard_map/ppermute | solution.py:557
  75.5 9.2 %collective-permute-start.27 = (bf16[72,1664]{1,0:T(8,128)(2,1)S(1)}, bf16[72,1664]{1,0:T(8,128)(2,1)S(1)}, u32[]{:S(2)}, u32[]{:S(2)}) collective-permute-start(bf16[72,1664]{1,0:T(8,128)(2,1)S(1)} %add_convert_fusion.6), channel_id=1, source_target_pairs={{0,4},{1,5},{2,3},{3,2},{4,0},{5,1},{6,7},{7,6},{8,12},{9,13},{10,... | collective-permute-start | bytes 718856 | tf_op jit(solution)/shard_map/ppermute | solution.py:557
  76.7 26.8 %collective-permute-start.31 = (bf16[72,1664]{1,0:T(8,128)(2,1)S(1)}, bf16[72,1664]{1,0:T(8,128)(2,1)S(1)}, u32[]{:S(2)}, u32[]{:S(2)}) collective-permute-start(bf16[72,1664]{1,0:T(8,128)(2,1)S(1)} %multiply_convert_fusion.3), channel_id=1, source_target_pairs={{0,24},{1,25},{2,26},{3,27},{4,28},{5,29},{6,30},{7,31},{8,0},{9,1... | collective-permute-start | bytes 718856 | tf_op jit(solution)/shard_map/ppermute | solution.py:557
  82.2 9.2 %collective-permute-start.26 = (bf16[144,1664]{1,0:T(8,128)(2,1)S(1)}, bf16[144,1664]{1,0:T(8,128)(2,1)S(1)}, u32[]{:S(2)}, u32[]{:S(2)}) collective-permute-start(bf16[144,1664]{1,0:T(8,128)(2,1)S(1)} %pad_maximum_fusion.7), channel_id=1, source_target_pairs={{0,1},{1,0},{2,6},{3,7},{4,5},{5,4},{6,2},{7,3},{8,9},{9,8},{10,14... | collective-permute-start | bytes 1437704 | tf_op jit(solution)/shard_map/ppermute | solution.py:557
  83.5 9.1 %collective-permute-start.30 = (bf16[72,1664]{1,0:T(8,128)(2,1)S(1)}, bf16[72,1664]{1,0:T(8,128)(2,1)S(1)}, u32[]{:S(2)}, u32[]{:S(2)}) collective-permute-start(bf16[72,1664]{1,0:T(8,128)(2,1)S(1)} %add_convert_fusion.5), channel_id=1, source_target_pairs={{0,4},{1,5},{2,3},{3,2},{4,0},{5,1},{6,7},{7,6},{8,12},{9,13},{10,... | collective-permute-start | bytes 718856 | tf_op jit(solution)/shard_map/ppermute | solution.py:557
  84.8 18.7 %collective-permute-start.33 = (bf16[72,1664]{1,0:T(8,128)(2,1)S(1)}, bf16[72,1664]{1,0:T(8,128)(2,1)S(1)}, u32[]{:S(2)}, u32[]{:S(2)}) collective-permute-start(bf16[72,1664]{1,0:T(8,128)(2,1)S(1)} %multiply_convert_fusion.2), channel_id=1, source_target_pairs={{0,8},{1,9},{2,10},{3,11},{4,12},{5,13},{6,14},{7,15},{8,16},{9,17... | collective-permute-start | bytes 718856 | tf_op jit(solution)/shard_map/ppermute | solution.py:557
  91.4 11.9 %collective-permute-start.29 = (bf16[72,1664]{1,0:T(8,128)(2,1)S(1)}, bf16[72,1664]{1,0:T(8,128)(2,1)S(1)}, u32[]{:S(2)}, u32[]{:S(2)}) collective-permute-start(bf16[72,1664]{1,0:T(8,128)(2,1)S(1)} %add_convert_fusion.4), channel_id=1, source_target_pairs={{0,4},{1,5},{2,3},{3,2},{4,0},{5,1},{6,7},{7,6},{8,12},{9,13},{10,... | collective-permute-start | bytes 718856 | tf_op jit(solution)/shard_map/ppermute | solution.py:557
  92.8 11.9 %collective-permute-start.32 = (bf16[72,1664]{1,0:T(8,128)(2,1)S(1)}, bf16[72,1664]{1,0:T(8,128)(2,1)S(1)}, u32[]{:S(2)}, u32[]{:S(2)}) collective-permute-start(bf16[72,1664]{1,0:T(8,128)(2,1)S(1)} %multiply_convert_fusion.1), channel_id=1, source_target_pairs={{0,16},{1,17},{2,18},{3,19},{4,20},{5,21},{6,22},{7,23},{8,24},{9,... | collective-permute-start | bytes 718856 | tf_op jit(solution)/shard_map/ppermute | solution.py:557
  (17 other events, 82.3 us)

commit v7 on v6

--- a/solution.py
+++ b/solution.py
@@ -132,7 +132,7 @@
 
 GROUPS = ((0,), (1,), (3,), (2,))
 MIB = 1024 * 1024
-WLIM = 32
+WLIM = 24
 PLAN = (
     "Z 1",
     "D1 0",

time: 113 us -> 113 us (level)
  no operation moved by 1% of the time
where the time goes in v7:
time: 113 us; the launch traced here: 112 us
  starting transfers between devices  43 us (38%)
  waiting for transfers between devices  38.3 us (34%)
  Pallas kernels  24 us (21%)
  other arithmetic  3.16 us (3%)
  local copies, waits for them, and re-layouts  3.07 us (3%)
    ppermute x34, starting transfers between devices, send(): return lax.ppermute(array, ('dp', 'rep'), permutation(move))  42 us
    ppermute x34, waiting for transfers between devices, send(): return lax.ppermute(array, ('dp', 'rep'), permutation(move))  33.3 us
    pallas_call x4, Pallas kernels, expert_call(): pl.pallas_call(expert_kernel, out_shape=(jax.ShapeDtypeStruct((rows, widt...  10.2 us
    pallas_call x1, Pallas kernels, weight_call(): pl.pallas_call(weight_kernel, out_shape=(jax.ShapeDtypeStruct((width, hid...  8.49 us
    ppermute x1, waiting for transfers between devices, plane_body(): got = lax.ppermute(away, 'rep', [(0, 1), (1, 0)])  5 us
    unnamed x12, local copies, waits for them, and re-layouts  2.93 us
    pallas_call x1, Pallas kernels, start_call(): pl.pallas_call(functools.partial(start_kernel, experts), out_shape=(jax.S...  2.39 us
  transfers between devices with their start and end apart: 35, of which 12 were waited for; matrix products, arithmetic and copies ran while one was open for 3% of the time, Pallas kernels for 18%

profile of v7, /device:TPU:0, one launch (start us, length us, event | category | flops | bytes accessed | tf_op | source)
XLA Modules:
  0.0 112.5 jit_solution(5061166962959314793)
XLA Ops:
  0.6 2.4 %shard_map.110 = (bf16[2,4,72,128]{3,2,1,0:T(8,128)(2,1)}, bf16[80,1664]{1,0:T(8,128)(2,1)}, bf16[80,1664]{1,0:T(8,128)(2,1)}, bf16[80,1664]{1,0:T(8,128)(2,1)}, bf16[80,1664]{1,0:T(8,128)(2,1)}) custom-call(s32[2,128]{1,0:T(2,128)} %bitcast.14, s32[1,128]{1,0:T(1,128)} %bitcast.15, f32[2,128]{1,0:T(2,128)} %bitcast.12, bf16[128,1664]{1,0:T(8,128)(2,1)} %tokens_at.1, ...), custom_call_target="tpu_custom_call" | custom-call | tf_op jit(solution)/shard_map/pallas_call | solution.py:275
  3.0 3.0 %collective-permute-start = (bf16[80,1664]{1,0:T(8,128)(2,1)}, bf16[80,1664]{1,0:T(8,128)(2,1)S(1)}, u32[]{:S(2)}, u32[]{:S(2)}) collective-permute-start(bf16[80,1664]{1,0:T(8,128)(2,1)} %get-tuple-element.100), channel_id=1, source_target_pairs={{0,1},{1,0},{2,6},{3,7},{4,5},{5,4},{6,2},{7,3},{8,9},{9,8},{10,14... | collective-permute-start | bytes 798728 | tf_op jit(solution)/shard_map/ppermute | solution.py:557
  6.0 1.6 %collective-permute-start.5 = (bf16[80,1664]{1,0:T(8,128)(2,1)}, bf16[80,1664]{1,0:T(8,128)(2,1)S(1)}, u32[]{:S(2)}, u32[]{:S(2)}) collective-permute-start(bf16[80,1664]{1,0:T(8,128)(2,1)} %get-tuple-element.107), channel_id=1, source_target_pairs={{0,8},{1,9},{2,10},{3,11},{4,12},{5,13},{6,14},{7,15},{8,16},{9,17... | collective-permute-start | bytes 798728 | tf_op jit(solution)/shard_map/ppermute | solution.py:557
  7.6 1.5 %collective-permute-start.1 = (bf16[80,1664]{1,0:T(8,128)(2,1)}, bf16[80,1664]{1,0:T(8,128)(2,1)S(1)}, u32[]{:S(2)}, u32[]{:S(2)}) collective-permute-start(bf16[80,1664]{1,0:T(8,128)(2,1)} %get-tuple-element.100), channel_id=1, source_target_pairs={{0,4},{1,5},{2,3},{3,2},{4,0},{5,1},{6,7},{7,6},{8,12},{9,13},{10,... | collective-permute-start | bytes 798728 | tf_op jit(solution)/shard_map/ppermute | solution.py:557
  9.1 2.5 %collective-permute-done = bf16[80,1664]{1,0:T(8,128)(2,1)S(1)} collective-permute-done((bf16[80,1664]{1,0:T(8,128)(2,1)}, bf16[80,1664]{1,0:T(8,128)(2,1)S(1)}, u32[]{:S(2)}, u32[]{:S(2)}) %collective-permute-start) | collective-permute-done | bytes 266272 | tf_op jit(solution)/shard_map/ppermute | solution.py:557
  11.7 3.6 %collective-permute-start.2 = (bf16[80,1664]{1,0:T(8,128)(2,1)S(1)}, bf16[80,1664]{1,0:T(8,128)(2,1)S(1)}, u32[]{:S(2)}, u32[]{:S(2)}) collective-permute-start(bf16[80,1664]{1,0:T(8,128)(2,1)S(1)} %collective-permute-done), channel_id=1, source_target_pairs={{0,4},{1,5},{2,3},{3,2},{4,0},{5,1},{6,7},{7,6},{8,12},{9,13},{10,... | collective-permute-start | bytes 798728 | tf_op jit(solution)/shard_map/ppermute | solution.py:557
  15.2 3.0 %collective-permute-start.11 = (bf16[80,1664]{1,0:T(8,128)(2,1)}, bf16[80,1664]{1,0:T(8,128)(2,1)S(1)}, u32[]{:S(2)}, u32[]{:S(2)}) collective-permute-start(bf16[80,1664]{1,0:T(8,128)(2,1)} %get-tuple-element.113), channel_id=1, source_target_pairs={{0,24},{1,25},{2,26},{3,27},{4,28},{5,29},{6,30},{7,31},{8,0},{9,1... | collective-permute-start | bytes 798728 | tf_op jit(solution)/shard_map/ppermute | solution.py:557
  21.8 1.6 %collective-permute-start.6 = (bf16[80,1664]{1,0:T(8,128)(2,1)S(1)}, bf16[80,1664]{1,0:T(8,128)(2,1)S(1)}, u32[]{:S(2)}, u32[]{:S(2)}) collective-permute-start(bf16[80,1664]{1,0:T(8,128)(2,1)S(1)} %collective-permute-done.5), channel_id=1, source_target_pairs={{0,1},{1,0},{2,6},{3,7},{4,5},{5,4},{6,2},{7,3},{8,9},{9,8},{10,14... | collective-permute-start | bytes 798728 | tf_op jit(solution)/shard_map/ppermute | solution.py:557
  25.5 8.2 %collective-permute-done.17 = bf16[80,1664]{1,0:T(8,128)(2,1)S(1)} collective-permute-done((bf16[80,1664]{1,0:T(8,128)(2,1)}, bf16[80,1664]{1,0:T(8,128)(2,1)S(1)}, u32[]{:S(2)}, u32[]{:S(2)}) %collective-permute-start.17) | collective-permute-done | bytes 266272 | tf_op jit(solution)/shard_map/ppermute | solution.py:557
  37.4 2.8 %collective-permute-done.8 = bf16[80,1664]{1,0:T(8,128)(2,1)S(1)} collective-permute-done((bf16[80,1664]{1,0:T(8,128)(2,1)S(1)}, bf16[80,1664]{1,0:T(8,128)(2,1)S(1)}, u32[]{:S(2)}, u32[]{:S(2)}) %collective-permute-start.8) | collective-permute-done | bytes 266272 | tf_op jit(solution)/shard_map/ppermute | solution.py:557
  40.7 2.9 %collective-permute-done.18 = bf16[80,1664]{1,0:T(8,128)(2,1)S(1)} collective-permute-done((bf16[80,1664]{1,0:T(8,128)(2,1)S(1)}, bf16[80,1664]{1,0:T(8,128)(2,1)S(1)}, u32[]{:S(2)}, u32[]{:S(2)}) %collective-permute-start.18) | collective-permute-done | bytes 266272 | tf_op jit(solution)/shard_map/ppermute | solution.py:557
  43.6 1.5 %collective-permute-start.20 = (bf16[80,1664]{1,0:T(8,128)(2,1)S(1)}, bf16[80,1664]{1,0:T(8,128)(2,1)S(1)}, u32[]{:S(2)}, u32[]{:S(2)}) collective-permute-start(bf16[80,1664]{1,0:T(8,128)(2,1)S(1)} %collective-permute-done.18), channel_id=1, source_target_pairs={{0,4},{1,5},{2,3},{3,2},{4,0},{5,1},{6,7},{7,6},{8,12},{9,13},{10,... | collective-permute-start | bytes 798728 | tf_op jit(solution)/shard_map/ppermute | solution.py:557
  45.4 2.5 %shard_map.112 = (bf16[320,1664]{1,0:T(8,128)(2,1)S(1)}, bf16[320,1664]{1,0:T(8,128)(2,1)S(1)}, bf16[320,512]{1,0:T(8,128)(2,1)S(1)}, bf16[320,512]{1,0:T(8,128)(2,1)S(1)}) custom-call(bf16[320,1664]{1,0:T(8,128)(2,1)S(1)} %pad_maximum_fusion.near.refs_0_, bf16[320,1664]{1,0:T(8,128)(2,1)S(1)} %collective-permute-done.3.far.refs_1_, ...), custom_call_target="tpu_custom_call" | custom-call | tf_op jit(solution)/shard_map/pallas_call | solution.py:199
  48.0 3.6 %collective-permute-done.20 = bf16[80,1664]{1,0:T(8,128)(2,1)S(1)} collective-permute-done((bf16[80,1664]{1,0:T(8,128)(2,1)S(1)}, bf16[80,1664]{1,0:T(8,128)(2,1)S(1)}, u32[]{:S(2)}, u32[]{:S(2)}) %collective-permute-start.20) | collective-permute-done | bytes 266272 | tf_op jit(solution)/shard_map/ppermute | solution.py:557
  52.0 2.5 %shard_map.113 = (bf16[320,1664]{1,0:T(8,128)(2,1)S(1)}, bf16[320,1664]{1,0:T(8,128)(2,1)S(1)}, bf16[320,512]{1,0:T(8,128)(2,1)S(1)}, bf16[320,512]{1,0:T(8,128)(2,1)S(1)}) custom-call(bf16[320,1664]{1,0:T(8,128)(2,1)S(1)} %pad_maximum_fusion.1.near.refs_2_.refs_4_, bf16[320,1664]{1,0:T(8,128)(2,1)S(1)} %collective-permute-done.9.far.refs_3_.refs_5_, ...), custom_call_target="tpu_custom_call" | custom-call | tf_op jit(solution)/shard_map/pallas_call | solution.py:199
  55.8 2.5 %shard_map.114 = (bf16[320,1664]{1,0:T(8,128)(2,1)S(1)}, bf16[320,1664]{1,0:T(8,128)(2,1)S(1)}, bf16[320,512]{1,0:T(8,128)(2,1)S(1)}, bf16[320,512]{1,0:T(8,128)(2,1)S(1)}) custom-call(bf16[320,1664]{1,0:T(8,128)(2,1)S(1)} %pad_maximum_fusion.2.near.refs_4_.refs_8_, bf16[320,1664]{1,0:T(8,128)(2,1)S(1)} %collective-permute-done.15.far.refs_5_.refs_9_, ...), custom_call_target="tpu_custom_call" | custom-call | tf_op jit(solution)/shard_map/pallas_call | solution.py:199
  59.8 2.5 %shard_map.115 = (bf16[320,1664]{1,0:T(8,128)(2,1)S(1)}, bf16[320,1664]{1,0:T(8,128)(2,1)S(1)}, bf16[320,512]{1,0:T(8,128)(2,1)S(1)}, bf16[320,512]{1,0:T(8,128)(2,1)S(1)}) custom-call(bf16[320,1664]{1,0:T(8,128)(2,1)S(1)} %pad_maximum_fusion.3.near.refs_6_.refs_12_, bf16[320,1664]{1,0:T(8,128)(2,1)S(1)} %collective-permute-done.21.far.refs_7_.refs_13_, ...), custom_call_target="tpu_custom_call" | custom-call | tf_op jit(solution)/shard_map/pallas_call | solution.py:199
  68.4 7.0 %collective-permute-done.25 = bf16[144,1664]{1,0:T(8,128)(2,1)S(1)} collective-permute-done((bf16[144,1664]{1,0:T(8,128)(2,1)S(1)}, bf16[144,1664]{1,0:T(8,128)(2,1)S(1)}, u32[]{:S(2)}, u32[]{:S(2)}) %collective-permute-start.25) | collective-permute-done | bytes 479264 | tf_op jit(solution)/shard_map/ppermute | solution.py:557
  76.7 5.1 %collective-permute-start.31 = (bf16[72,1664]{1,0:T(8,128)(2,1)S(1)}, bf16[72,1664]{1,0:T(8,128)(2,1)S(1)}, u32[]{:S(2)}, u32[]{:S(2)}) collective-permute-start(bf16[72,1664]{1,0:T(8,128)(2,1)S(1)} %multiply_convert_fusion.3), channel_id=1, source_target_pairs={{0,24},{1,25},{2,26},{3,27},{4,28},{5,29},{6,30},{7,31},{8,0},{9,1... | collective-permute-start | bytes 718856 | tf_op jit(solution)/shard_map/ppermute | solution.py:557
  84.8 2.8 %collective-permute-start.33 = (bf16[72,1664]{1,0:T(8,128)(2,1)S(1)}, bf16[72,1664]{1,0:T(8,128)(2,1)S(1)}, u32[]{:S(2)}, u32[]{:S(2)}) collective-permute-start(bf16[72,1664]{1,0:T(8,128)(2,1)S(1)} %multiply_convert_fusion.2), channel_id=1, source_target_pairs={{0,8},{1,9},{2,10},{3,11},{4,12},{5,13},{6,14},{7,15},{8,16},{9,17... | collective-permute-start | bytes 718856 | tf_op jit(solution)/shard_map/ppermute | solution.py:557
  87.6 3.8 %collective-permute-done.26 = bf16[144,1664]{1,0:T(8,128)(2,1)S(1)} collective-permute-done((bf16[144,1664]{1,0:T(8,128)(2,1)S(1)}, bf16[144,1664]{1,0:T(8,128)(2,1)S(1)}, u32[]{:S(2)}, u32[]{:S(2)}) %collective-permute-start.26) | collective-permute-done | bytes 479264 | tf_op jit(solution)/shard_map/ppermute | solution.py:557
  92.7 2.0 %collective-permute-start.32 = (bf16[72,1664]{1,0:T(8,128)(2,1)S(1)}, bf16[72,1664]{1,0:T(8,128)(2,1)S(1)}, u32[]{:S(2)}, u32[]{:S(2)}) collective-permute-start(bf16[72,1664]{1,0:T(8,128)(2,1)S(1)} %multiply_convert_fusion.1), channel_id=1, source_target_pairs={{0,16},{1,17},{2,18},{3,19},{4,20},{5,21},{6,22},{7,23},{8,24},{9,... | collective-permute-start | bytes 718856 | tf_op jit(solution)/shard_map/ppermute | solution.py:557
  94.8 8.5 %shard_map.117 = (bf16[1664,512]{1,0:T(8,128)(2,1)}, bf16[512,1664]{1,0:T(8,128)(2,1)}) custom-call(bf16[1280,128]{1,0:T(8,128)(2,1)S(1)} %get-tuple-element.154.kept, bf16[320,1664]{1,0:T(8,128)(2,1)S(1)} %pad_maximum_fusion.near.refs_0_, bf16[320,1664]{1,0:T(8,128)(2,1)S(1)} %collective-permute-done.3.far.refs_1_, ...), custom_call_target="tpu_custom_call" | custom-call | tf_op jit(solution)/shard_map/pallas_call | solution.py:412
  106.6 5.0 %collective-permute-done.34.got = bf16[848,128]{1,0:T(8,128)(2,1)S(1)} collective-permute-done((bf16[848,128]{1,0:T(8,128)(2,1)S(1)}, bf16[848,128]{1,0:T(8,128)(2,1)S(1)}, u32[]{:S(2)}, u32[]{:S(2)}) %collective-permute-start.34) | collective-permute-done | bytes 217120 | tf_op jit(solution)/shard_map/ppermute | solution.py:702
  (96 shorter events, 29.0 us)
Async XLA Ops:
  6.0 15.7 %collective-permute-start.5 = (bf16[80,1664]{1,0:T(8,128)(2,1)}, bf16[80,1664]{1,0:T(8,128)(2,1)S(1)}, u32[]{:S(2)}, u32[]{:S(2)}) collective-permute-start(bf16[80,1664]{1,0:T(8,128)(2,1)} %get-tuple-element.107), channel_id=1, source_target_pairs={{0,8},{1,9},{2,10},{3,11},{4,12},{5,13},{6,14},{7,15},{8,16},{9,17... | collective-permute-start | bytes 798728 | tf_op jit(solution)/shard_map/ppermute | solution.py:557
  7.6 15.7 %collective-permute-start.1 = (bf16[80,1664]{1,0:T(8,128)(2,1)}, bf16[80,1664]{1,0:T(8,128)(2,1)S(1)}, u32[]{:S(2)}, u32[]{:S(2)}) collective-permute-start(bf16[80,1664]{1,0:T(8,128)(2,1)} %get-tuple-element.100), channel_id=1, source_target_pairs={{0,4},{1,5},{2,3},{3,2},{4,0},{5,1},{6,7},{7,6},{8,12},{9,13},{10,... | collective-permute-start | bytes 798728 | tf_op jit(solution)/shard_map/ppermute | solution.py:557
  11.7 11.7 %collective-permute-start.2 = (bf16[80,1664]{1,0:T(8,128)(2,1)S(1)}, bf16[80,1664]{1,0:T(8,128)(2,1)S(1)}, u32[]{:S(2)}, u32[]{:S(2)}) collective-permute-start(bf16[80,1664]{1,0:T(8,128)(2,1)S(1)} %collective-permute-done), channel_id=1, source_target_pairs={{0,4},{1,5},{2,3},{3,2},{4,0},{5,1},{6,7},{7,6},{8,12},{9,13},{10,... | collective-permute-start | bytes 798728 | tf_op jit(solution)/shard_map/ppermute | solution.py:557
  15.2 9.9 %collective-permute-start.11 = (bf16[80,1664]{1,0:T(8,128)(2,1)}, bf16[80,1664]{1,0:T(8,128)(2,1)S(1)}, u32[]{:S(2)}, u32[]{:S(2)}) collective-permute-start(bf16[80,1664]{1,0:T(8,128)(2,1)} %get-tuple-element.113), channel_id=1, source_target_pairs={{0,24},{1,25},{2,26},{3,27},{4,28},{5,29},{6,30},{7,31},{8,0},{9,1... | collective-permute-start | bytes 798728 | tf_op jit(solution)/shard_map/ppermute | solution.py:557
  18.2 15.5 %collective-permute-start.17 = (bf16[80,1664]{1,0:T(8,128)(2,1)}, bf16[80,1664]{1,0:T(8,128)(2,1)S(1)}, u32[]{:S(2)}, u32[]{:S(2)}) collective-permute-start(bf16[80,1664]{1,0:T(8,128)(2,1)} %get-tuple-element.120), channel_id=1, source_target_pairs={{0,16},{1,17},{2,18},{3,19},{4,20},{5,21},{6,22},{7,23},{8,24},{9,... | collective-permute-start | bytes 798728 | tf_op jit(solution)/shard_map/ppermute | solution.py:557
  21.8 12.0 %collective-permute-start.6 = (bf16[80,1664]{1,0:T(8,128)(2,1)S(1)}, bf16[80,1664]{1,0:T(8,128)(2,1)S(1)}, u32[]{:S(2)}, u32[]{:S(2)}) collective-permute-start(bf16[80,1664]{1,0:T(8,128)(2,1)S(1)} %collective-permute-done.5), channel_id=1, source_target_pairs={{0,1},{1,0},{2,6},{3,7},{4,5},{5,4},{6,2},{7,3},{8,9},{9,8},{10,14... | collective-permute-start | bytes 798728 | tf_op jit(solution)/shard_map/ppermute | solution.py:557
  23.6 21.8 %collective-permute-start.3 = (bf16[320,1664]{1,0:T(8,128)(2,1)S(1)}, bf16[320,1664]{1,0:T(8,128)(2,1)S(1)}, u32[]{:S(2)}, u32[]{:S(2)}) collective-permute-start(bf16[320,1664]{1,0:T(8,128)(2,1)S(1)} %pad_maximum_fusion.near.refs_0_), channel_id=1, source_target_pairs={{0,2},{1,3},{2,0},{3,1},{4,6},{5,7},{6,4},{7,5},{8,10},{9,11},{10,... | collective-permute-start | bytes 3194888 | tf_op jit(solution)/shard_map/ppermute | solution.py:557
  23.7 11.7 %collective-permute-start.7 = (bf16[80,1664]{1,0:T(8,128)(2,1)S(1)}, bf16[80,1664]{1,0:T(8,128)(2,1)S(1)}, u32[]{:S(2)}, u32[]{:S(2)}) collective-permute-start(bf16[80,1664]{1,0:T(8,128)(2,1)S(1)} %collective-permute-done.5), channel_id=1, source_target_pairs={{0,4},{1,5},{2,3},{3,2},{4,0},{5,1},{6,7},{7,6},{8,12},{9,13},{10,... | collective-permute-start | bytes 798728 | tf_op jit(solution)/shard_map/ppermute | solution.py:557
  25.1 11.5 %collective-permute-start.12 = (bf16[80,1664]{1,0:T(8,128)(2,1)S(1)}, bf16[80,1664]{1,0:T(8,128)(2,1)S(1)}, u32[]{:S(2)}, u32[]{:S(2)}) collective-permute-start(bf16[80,1664]{1,0:T(8,128)(2,1)S(1)} %collective-permute-done.11), channel_id=1, source_target_pairs={{0,1},{1,0},{2,6},{3,7},{4,5},{5,4},{6,2},{7,3},{8,9},{9,8},{10,14... | collective-permute-start | bytes 798728 | tf_op jit(solution)/shard_map/ppermute | solution.py:557
  34.3 9.3 %collective-permute-start.18 = (bf16[80,1664]{1,0:T(8,128)(2,1)S(1)}, bf16[80,1664]{1,0:T(8,128)(2,1)S(1)}, u32[]{:S(2)}, u32[]{:S(2)}) collective-permute-start(bf16[80,1664]{1,0:T(8,128)(2,1)S(1)} %collective-permute-done.17), channel_id=1, source_target_pairs={{0,1},{1,0},{2,6},{3,7},{4,5},{5,4},{6,2},{7,3},{8,9},{9,8},{10,14... | collective-permute-start | bytes 798728 | tf_op jit(solution)/shard_map/ppermute | solution.py:557
  35.3 16.2 %collective-permute-start.13 = (bf16[80,1664]{1,0:T(8,128)(2,1)S(1)}, bf16[80,1664]{1,0:T(8,128)(2,1)S(1)}, u32[]{:S(2)}, u32[]{:S(2)}) collective-permute-start(bf16[80,1664]{1,0:T(8,128)(2,1)S(1)} %collective-permute-done.11), channel_id=1, source_target_pairs={{0,4},{1,5},{2,3},{3,2},{4,0},{5,1},{6,7},{7,6},{8,12},{9,13},{10,... | collective-permute-start | bytes 798728 | tf_op jit(solution)/shard_map/ppermute | solution.py:557
  36.6 11.4 %collective-permute-start.19 = (bf16[80,1664]{1,0:T(8,128)(2,1)S(1)}, bf16[80,1664]{1,0:T(8,128)(2,1)S(1)}, u32[]{:S(2)}, u32[]{:S(2)}) collective-permute-start(bf16[80,1664]{1,0:T(8,128)(2,1)S(1)} %collective-permute-done.17), channel_id=1, source_target_pairs={{0,4},{1,5},{2,3},{3,2},{4,0},{5,1},{6,7},{7,6},{8,12},{9,13},{10,... | collective-permute-start | bytes 798728 | tf_op jit(solution)/shard_map/ppermute | solution.py:557
  40.2 11.4 %collective-permute-start.14 = (bf16[80,1664]{1,0:T(8,128)(2,1)S(1)}, bf16[80,1664]{1,0:T(8,128)(2,1)S(1)}, u32[]{:S(2)}, u32[]{:S(2)}) collective-permute-start(bf16[80,1664]{1,0:T(8,128)(2,1)S(1)} %collective-permute-done.12), channel_id=1, source_target_pairs={{0,4},{1,5},{2,3},{3,2},{4,0},{5,1},{6,7},{7,6},{8,12},{9,13},{10,... | collective-permute-start | bytes 798728 | tf_op jit(solution)/shard_map/ppermute | solution.py:557
  55.3 26.4 %collective-permute-start.4 = (bf16[320,1664]{1,0:T(8,128)(2,1)S(1)}, bf16[320,1664]{1,0:T(8,128)(2,1)S(1)}, u32[]{:S(2)}, u32[]{:S(2)}) collective-permute-start(bf16[320,1664]{1,0:T(8,128)(2,1)S(1)} %get-tuple-element.106), channel_id=1, source_target_pairs={{0,2},{1,3},{2,0},{3,1},{4,6},{5,7},{6,4},{7,5},{8,10},{9,11},{10,... | collective-permute-start | bytes 3194888 | tf_op jit(solution)/shard_map/ppermute | solution.py:557
  63.7 11.7 %collective-permute-start.25 = (bf16[144,1664]{1,0:T(8,128)(2,1)S(1)}, bf16[144,1664]{1,0:T(8,128)(2,1)S(1)}, u32[]{:S(2)}, u32[]{:S(2)}) collective-permute-start(bf16[144,1664]{1,0:T(8,128)(2,1)S(1)} %pad_maximum_fusion.5), channel_id=1, source_target_pairs={{0,1},{1,0},{2,6},{3,7},{4,5},{5,4},{6,2},{7,3},{8,9},{9,8},{10,14... | collective-permute-start | bytes 1437704 | tf_op jit(solution)/shard_map/ppermute | solution.py:557
  65.6 17.9 %collective-permute-start.28 = (bf16[144,1664]{1,0:T(8,128)(2,1)S(1)}, bf16[144,1664]{1,0:T(8,128)(2,1)S(1)}, u32[]{:S(2)}, u32[]{:S(2)}) collective-permute-start(bf16[144,1664]{1,0:T(8,128)(2,1)S(1)} %pad_maximum_fusion.6), channel_id=1, source_target_pairs={{0,1},{1,0},{2,6},{3,7},{4,5},{5,4},{6,2},{7,3},{8,9},{9,8},{10,14... | collective-permute-start | bytes 1437704 | tf_op jit(solution)/shard_map/ppermute | solution.py:557
  67.7 8.8 %collective-permute-start.24 = (bf16[72,1664]{1,0:T(8,128)(2,1)S(1)}, bf16[72,1664]{1,0:T(8,128)(2,1)S(1)}, u32[]{:S(2)}, u32[]{:S(2)}) collective-permute-start(bf16[72,1664]{1,0:T(8,128)(2,1)S(1)} %add_convert_fusion.7), channel_id=1, source_target_pairs={{0,4},{1,5},{2,3},{3,2},{4,0},{5,1},{6,7},{7,6},{8,12},{9,13},{10,... | collective-permute-start | bytes 718856 | tf_op jit(solution)/shard_map/ppermute | solution.py:557
  75.4 9.2 %collective-permute-start.27 = (bf16[72,1664]{1,0:T(8,128)(2,1)S(1)}, bf16[72,1664]{1,0:T(8,128)(2,1)S(1)}, u32[]{:S(2)}, u32[]{:S(2)}) collective-permute-start(bf16[72,1664]{1,0:T(8,128)(2,1)S(1)} %add_convert_fusion.6), channel_id=1, source_target_pairs={{0,4},{1,5},{2,3},{3,2},{4,0},{5,1},{6,7},{7,6},{8,12},{9,13},{10,... | collective-permute-start | bytes 718856 | tf_op jit(solution)/shard_map/ppermute | solution.py:557
  76.7 26.7 %collective-permute-start.31 = (bf16[72,1664]{1,0:T(8,128)(2,1)S(1)}, bf16[72,1664]{1,0:T(8,128)(2,1)S(1)}, u32[]{:S(2)}, u32[]{:S(2)}) collective-permute-start(bf16[72,1664]{1,0:T(8,128)(2,1)S(1)} %multiply_convert_fusion.3), channel_id=1, source_target_pairs={{0,24},{1,25},{2,26},{3,27},{4,28},{5,29},{6,30},{7,31},{8,0},{9,1... | collective-permute-start | bytes 718856 | tf_op jit(solution)/shard_map/ppermute | solution.py:557
  82.2 9.2 %collective-permute-start.26 = (bf16[144,1664]{1,0:T(8,128)(2,1)S(1)}, bf16[144,1664]{1,0:T(8,128)(2,1)S(1)}, u32[]{:S(2)}, u32[]{:S(2)}) collective-permute-start(bf16[144,1664]{1,0:T(8,128)(2,1)S(1)} %pad_maximum_fusion.7), channel_id=1, source_target_pairs={{0,1},{1,0},{2,6},{3,7},{4,5},{5,4},{6,2},{7,3},{8,9},{9,8},{10,14... | collective-permute-start | bytes 1437704 | tf_op jit(solution)/shard_map/ppermute | solution.py:557
  83.5 9.1 %collective-permute-start.30 = (bf16[72,1664]{1,0:T(8,128)(2,1)S(1)}, bf16[72,1664]{1,0:T(8,128)(2,1)S(1)}, u32[]{:S(2)}, u32[]{:S(2)}) collective-permute-start(bf16[72,1664]{1,0:T(8,128)(2,1)S(1)} %add_convert_fusion.5), channel_id=1, source_target_pairs={{0,4},{1,5},{2,3},{3,2},{4,0},{5,1},{6,7},{7,6},{8,12},{9,13},{10,... | collective-permute-start | bytes 718856 | tf_op jit(solution)/shard_map/ppermute | solution.py:557
  84.8 18.6 %collective-permute-start.33 = (bf16[72,1664]{1,0:T(8,128)(2,1)S(1)}, bf16[72,1664]{1,0:T(8,128)(2,1)S(1)}, u32[]{:S(2)}, u32[]{:S(2)}) collective-permute-start(bf16[72,1664]{1,0:T(8,128)(2,1)S(1)} %multiply_convert_fusion.2), channel_id=1, source_target_pairs={{0,8},{1,9},{2,10},{3,11},{4,12},{5,13},{6,14},{7,15},{8,16},{9,17... | collective-permute-start | bytes 718856 | tf_op jit(solution)/shard_map/ppermute | solution.py:557
  91.5 11.8 %collective-permute-start.29 = (bf16[72,1664]{1,0:T(8,128)(2,1)S(1)}, bf16[72,1664]{1,0:T(8,128)(2,1)S(1)}, u32[]{:S(2)}, u32[]{:S(2)}) collective-permute-start(bf16[72,1664]{1,0:T(8,128)(2,1)S(1)} %add_convert_fusion.4), channel_id=1, source_target_pairs={{0,4},{1,5},{2,3},{3,2},{4,0},{5,1},{6,7},{7,6},{8,12},{9,13},{10,... | collective-permute-start | bytes 718856 | tf_op jit(solution)/shard_map/ppermute | solution.py:557
  92.7 11.9 %collective-permute-start.32 = (bf16[72,1664]{1,0:T(8,128)(2,1)S(1)}, bf16[72,1664]{1,0:T(8,128)(2,1)S(1)}, u32[]{:S(2)}, u32[]{:S(2)}) collective-permute-start(bf16[72,1664]{1,0:T(8,128)(2,1)S(1)} %multiply_convert_fusion.1), channel_id=1, source_target_pairs={{0,16},{1,17},{2,18},{3,19},{4,20},{5,21},{6,22},{7,23},{8,24},{9,... | collective-permute-start | bytes 718856 | tf_op jit(solution)/shard_map/ppermute | solution.py:557
  (17 other events, 82.4 us)
